TPU v7x, 32 devices: a whole 2x2x4 slice. The times are simulated.
32 devices in a mesh: dp: 8 (over y, x, core), fsdp: 4 (over z).
Axes of the slice: x: 2, y: 2, z: 4, core: 2. Of those that a mesh axis runs over, the one named last changes fastest.
Arguments:
- latents: bfloat16 [32, 256, 16], P(('dp', 'fsdp')), may hold values from -6 to 6
- orders: int32 [32, 256], P(('dp', 'fsdp')), may hold values from 0 to 255, each once within a row
- mask_counts: int32 [32], P(('dp', 'fsdp')), may hold values from 1 to 256, 6144 in all
- noise: bfloat16 [6144, 64], P(('dp', 'fsdp')), may hold values from -6 to 6
- timesteps: int32 [6144, 4], P(('dp', 'fsdp')), may hold values from 0 to 999
- loss_weights: float32 [6144, 4], P(('dp', 'fsdp')), may hold values from 0.5 to 7.5
- block_weights: float32 [2, 768, 9216], P(None, ('dp', 'fsdp')), may hold values from -0.21875 to 0.21875
- block_gains: float32 [2, 2, 768], P(None, None, ('dp', 'fsdp')), may hold values from 0.5 to 1.5
- entry_table: float32 [656, 768], P(None, ('dp', 'fsdp')), may hold values from -1.5 to 1.5
- head_weights: float32 [2, 1024, 5120], P(None, ('dp', 'fsdp')), may hold values from -0.1875 to 0.1875
- head_biases: float32 [3, 5120], P(None, ('dp', 'fsdp')), may hold values from -1.5 to 1.5
- head_edges: float32 [4128, 1024], P(None, ('dp', 'fsdp')), may hold values from -1 to 1
- first_blocks: float32 [2, 768, 9216], P(None, ('dp', 'fsdp')), may hold values from -5.722046e-06 to 5.722046e-06
- first_gains: float32 [2, 2, 768], P(None, None, ('dp', 'fsdp')), may hold values from -1.5258789e-05 to 1.5258789e-05
- first_entry: float32 [656, 768], P(None, ('dp', 'fsdp')), may hold values from -5.722046e-06 to 5.722046e-06
- first_head: float32 [2, 1024, 5120], P(None, ('dp', 'fsdp')), may hold values from -5.722046e-06 to 5.722046e-06
- first_biases: float32 [3, 5120], P(None, ('dp', 'fsdp')), may hold values from -1.5258789e-05 to 1.5258789e-05
- first_edges: float32 [4128, 1024], P(None, ('dp', 'fsdp')), may hold values from -5.722046e-06 to 5.722046e-06
- second_blocks: float32 [2, 768, 9216], P(None, ('dp', 'fsdp')), may hold values from 1.3609678e-13 to 5.443871e-13
- second_gains: float32 [2, 2, 768], P(None, None, ('dp', 'fsdp')), may hold values from 1.2248711e-12 to 4.8994845e-12
- second_entry: float32 [656, 768], P(None, ('dp', 'fsdp')), may hold values from 1.3609678e-13 to 5.443871e-13
- second_head: float32 [2, 1024, 5120], P(None, ('dp', 'fsdp')), may hold values from 1.3609678e-13 to 5.443871e-13
- second_biases: float32 [3, 5120], P(None, ('dp', 'fsdp')), may hold values from 1.2248711e-12 to 4.8994845e-12
- second_edges: float32 [4128, 1024], P(None, ('dp', 'fsdp')), may hold values from 1.3609678e-13 to 5.443871e-13
Outputs:
- updated_blocks: float32 [2, 768, 9216], P(None, ('dp', 'fsdp'))
- updated_gains: float32 [2, 2, 768], P(None, None, ('dp', 'fsdp'))
- updated_entry: float32 [656, 768], P(None, ('dp', 'fsdp'))
- updated_head: float32 [2, 1024, 5120], P(None, ('dp', 'fsdp'))
- updated_biases: float32 [3, 5120], P(None, ('dp', 'fsdp'))
- updated_edges: float32 [4128, 1024], P(None, ('dp', 'fsdp'))
- momentum_blocks: float32 [2, 768, 9216], P(None, ('dp', 'fsdp'))
- momentum_gains: float32 [2, 2, 768], P(None, None, ('dp', 'fsdp'))
- momentum_entry: float32 [656, 768], P(None, ('dp', 'fsdp'))
- momentum_head: float32 [2, 1024, 5120], P(None, ('dp', 'fsdp'))
- momentum_biases: float32 [3, 5120], P(None, ('dp', 'fsdp'))
- momentum_edges: float32 [4128, 1024], P(None, ('dp', 'fsdp'))
- variance_blocks: float32 [2, 768, 9216], P(None, ('dp', 'fsdp'))
- variance_gains: float32 [2, 2, 768], P(None, None, ('dp', 'fsdp'))
- variance_entry: float32 [656, 768], P(None, ('dp', 'fsdp'))
- variance_head: float32 [2, 1024, 5120], P(None, ('dp', 'fsdp'))
- variance_biases: float32 [3, 5120], P(None, ('dp', 'fsdp'))
- variance_edges: float32 [4128, 1024], P(None, ('dp', 'fsdp'))
- loss_sum: float32 [], replicated
- weight_sum: float32 [], replicated
- grad_norm: float32 [], replicated
Inputs may be any that keep to these rules, and one draw needn't show every extreme that they name: `orders`: each row is a permutation of 0 to 255. `mask_counts`: the counts of all images sum to 6144; the largest is 256.
All inputs are finite; a program needn't handle non-finite values. No bound on the sum of `mask_counts` on one device may be relied on, other than what follows from the above.
Results may differ from a plain program's by a relative error of at most 0.0088.
Values may be sent and summed in bfloat16 or wider, within the bound.
A program may use at most 512 MiB of HBM per device.

v0:
```python
import math

import jax
import jax.numpy as jnp
from jax import lax
from jax.sharding import PartitionSpec as P

D = 768
HEADS = 12
HD = 64
FF = 3072
HW = 1024
CH = 16
FREQ = 256
LAT = 256
BUF = 64
HB = 2
COPIES = 4
TSTEPS = 1000
ADAM_STEP = 5
SEQ = 320


BETA_ONE = 0.5
BETA_TWO = 0.5
LEARN_RATE = 0.03
GAIN_RATE = 0.3
DECAY_RATE = 0.02
ADAM_EPS = 1e-08
CLIP_NORM = 0.002
NORM_EPS = 1e-06


def entering(array, axis, combine, identity):
    length, position = (lax.axis_size(axis), lax.axis_index(axis))
    everything = lax.all_gather(array, axis)
    start = jnp.broadcast_to(jnp.asarray(identity, array.dtype), array.shape)

    def turn(k, before):
        reached = k < position
        new = combine(before, everything[k])
        return jnp.where(reached, new, before)

    return lax.fori_loop(0, length, turn, start)


def dot_plain(left, right):
    return jnp.dot(left, right, preferred_element_type=jnp.float32)


def dot_left(left, right):
    return lax.dot_general(
        left, right, (((0,), (0,)), ((), ())), preferred_element_type=jnp.float32
    )


def dot_right(left, right):
    return lax.dot_general(
        left, right, (((1,), (1,)), ((), ())), preferred_element_type=jnp.float32
    )


def normalize(values):
    centred = values - jnp.mean(values, -1, keepdims=True)
    inverse = lax.rsqrt(jnp.mean(centred * centred, -1, keepdims=True) + NORM_EPS)
    return (centred * inverse, inverse)


def norm_back(upstream, normed, inverse):
    return inverse * (
        upstream
        - jnp.mean(upstream, -1, keepdims=True)
        - normed * jnp.mean(upstream * normed, -1, keepdims=True)
    )


def local_grad(function, inputs, upstream):
    return jax.vjp(function, inputs)[1](upstream)[0]


def column_sum(values):
    return jnp.sum(values.astype(jnp.float32), 0)


def layer_forward(hidden, weights, gain_rows, key_keep):
    batch_size = key_keep.shape[0]
    gain_values = gain_rows.astype(jnp.float32)
    first_norm, first_inv = normalize(hidden)
    normed = (first_norm * gain_values[0]).astype(jnp.bfloat16)
    packed = dot_plain(normed, weights[:, : 3 * D]).astype(jnp.bfloat16)
    query_rows = packed[:, :D].reshape(batch_size, SEQ, HEADS, HD)
    key_rows = packed[:, D : 2 * D].reshape(batch_size, SEQ, HEADS, HD)
    value_rows = packed[:, 2 * D :].reshape(batch_size, SEQ, HEADS, HD)
    scores = jnp.einsum(
        "bqhd,bkhd->bhqk", query_rows, key_rows, preferred_element_type=jnp.float32
    ) * HD ** (-0.5)
    scores = jnp.where(key_keep[:, None, None, :] > 0, scores, -1e30)
    attention = jax.nn.softmax(scores, -1)
    attention_low = attention.astype(jnp.bfloat16)
    mixed_heads = (
        jnp.einsum("bhqk,bkhd->bqhd", attention_low, value_rows, preferred_element_type=jnp.float32)
        .reshape(-1, D)
        .astype(jnp.bfloat16)
    )
    middle = hidden + dot_plain(mixed_heads, weights[:, 3 * D : 4 * D])
    second_norm, second_inv = normalize(middle)
    second = (second_norm * gain_values[1]).astype(jnp.bfloat16)
    inner_rows = dot_plain(second, weights[:, 4 * D : 4 * D + FF])
    upper_rows = jax.nn.gelu(inner_rows).astype(jnp.bfloat16)
    output = middle + dot_right(upper_rows, weights[:, 4 * D + FF :])
    saved = (
        first_norm,
        first_inv,
        normed,
        query_rows,
        key_rows,
        value_rows,
        attention,
        attention_low,
        mixed_heads,
        second_norm,
        second_inv,
        second,
        inner_rows,
        upper_rows,
    )
    return (output, saved)


def layer_backward(upstream, weights, gain_rows, saved):
    (
        first_norm,
        first_inv,
        normed,
        query_rows,
        key_rows,
        value_rows,
        attention,
        attention_low,
        mixed_heads,
        second_norm,
        second_inv,
        second,
        inner_rows,
        upper_rows,
    ) = saved
    gain_values = gain_rows.astype(jnp.float32)
    batch_size = query_rows.shape[0]
    back_branch = upstream.astype(jnp.bfloat16)
    grad_down = dot_left(back_branch, upper_rows)
    back_upper = dot_plain(back_branch, weights[:, 4 * D + FF :])
    back_inner = local_grad(jax.nn.gelu, inner_rows, back_upper).astype(jnp.bfloat16)
    grad_up = dot_left(second, back_inner)
    back_second = dot_right(back_inner, weights[:, 4 * D : 4 * D + FF])
    grad_gain_two = jnp.sum(back_second * second_norm, 0)
    back_middle = upstream + norm_back(back_second * gain_values[1], second_norm, second_inv)
    back_attn_out = back_middle.astype(jnp.bfloat16)
    grad_out = dot_left(mixed_heads, back_attn_out)
    back_mixed = (
        dot_right(back_attn_out, weights[:, 3 * D : 4 * D])
        .astype(jnp.bfloat16)
        .reshape(batch_size, SEQ, HEADS, HD)
    )
    back_attention = jnp.einsum(
        "bqhd,bkhd->bhqk", back_mixed, value_rows, preferred_element_type=jnp.float32
    )
    back_values = jnp.einsum(
        "bhqk,bqhd->bkhd", attention_low, back_mixed, preferred_element_type=jnp.float32
    )
    back_scores = (
        attention * (back_attention - jnp.sum(back_attention * attention, -1, keepdims=True))
    ).astype(jnp.bfloat16)
    back_queries = jnp.einsum(
        "bhqk,bkhd->bqhd", back_scores, key_rows, preferred_element_type=jnp.float32
    ) * HD ** (-0.5)
    back_keys = jnp.einsum(
        "bhqk,bqhd->bkhd", back_scores, query_rows, preferred_element_type=jnp.float32
    ) * HD ** (-0.5)
    back_packed = jnp.concatenate(
        [back_queries.reshape(-1, D), back_keys.reshape(-1, D), back_values.reshape(-1, D)], 1
    ).astype(jnp.bfloat16)
    grad_packed = dot_left(normed, back_packed)
    back_normed = dot_right(back_packed, weights[:, : 3 * D])
    grad_gain_one = jnp.sum(back_normed * first_norm, 0)
    back_hidden = back_middle + norm_back(back_normed * gain_values[0], first_norm, first_inv)
    grad_weights = jnp.concatenate([grad_packed, grad_out, grad_up, grad_down], 1)
    return (back_hidden, grad_weights, jnp.stack([grad_gain_one, grad_gain_two]))


def head_pass(
    blocks,
    biases,
    edge_rows,
    cond_rows,
    clean_rows,
    noise_rows,
    step_rows,
    weight_rows,
    weight_total,
):
    token_count = cond_rows.shape[0]
    base = D + 2 * CH
    extra = biases[HB].astype(jnp.float32)
    half_freq = FREQ // 2
    frequencies = jnp.exp(-math.log(10000.0) * jnp.arange(half_freq, dtype=jnp.float32) / half_freq)
    step_times = step_rows.astype(jnp.float32)
    angles = step_times.reshape(-1)[:, None] * frequencies
    time_embed = jnp.concatenate([jnp.cos(angles), jnp.sin(angles)], -1).astype(jnp.bfloat16)
    time_inner = dot_plain(time_embed, edge_rows[base : base + FREQ]) + extra[:HW]
    time_hidden = jax.nn.silu(time_inner).astype(jnp.bfloat16)
    time_second = edge_rows[base + FREQ : base + FREQ + HW]
    time_vector = dot_plain(time_hidden, time_second) + extra[HW : 2 * HW]
    projected = dot_plain(cond_rows, edge_rows[:D])
    conditioning = (projected[:, None, :] + time_vector.reshape(token_count, COPIES, HW)).reshape(
        -1, HW
    )
    silu_cond = jax.nn.silu(conditioning).astype(jnp.bfloat16)
    phase_angle = (step_times / TSTEPS + 0.008) / 1.008 * (math.pi / 2)
    keep_part = jnp.cos(phase_angle)[..., None]
    noise_part = jnp.sin(phase_angle)[..., None]
    clean_copies = clean_rows.astype(jnp.float32)[:, None, :]
    fresh_noise = noise_rows.astype(jnp.float32).reshape(token_count, COPIES, CH)
    noisy_rows = (
        (keep_part * clean_copies + noise_part * fresh_noise).reshape(-1, CH).astype(jnp.bfloat16)
    )
    target = (keep_part * fresh_noise - noise_part * clean_copies).reshape(-1, CH)
    stream = dot_plain(noisy_rows, edge_rows[D : D + CH]) + extra[4 * HW :]
    saved = []
    for block_number in range(HB):
        bias_row = biases[block_number].astype(jnp.float32)
        modulation = dot_plain(silu_cond, blocks[block_number, :, : 3 * HW]) + bias_row[: 3 * HW]
        normed, inverse = normalize(stream)
        shaped = (normed * (1.0 + modulation[:, HW : 2 * HW]) + modulation[:, :HW]).astype(
            jnp.bfloat16
        )
        inner_rows = (
            dot_plain(shaped, blocks[block_number, :, 3 * HW : 4 * HW]) + bias_row[3 * HW : 4 * HW]
        )
        hidden = jax.nn.silu(inner_rows).astype(jnp.bfloat16)
        branch = dot_right(hidden, blocks[block_number, :, 4 * HW :]) + bias_row[4 * HW :]
        saved.append((modulation, normed, inverse, shaped, inner_rows, hidden, branch))
        stream = stream + modulation[:, 2 * HW :] * branch
    final_weights = jnp.concatenate(
        [edge_rows[base + FREQ + HW : base + FREQ + 2 * HW], edge_rows[base + FREQ + 2 * HW :]], 1
    )
    final_mod = dot_plain(silu_cond, final_weights) + extra[2 * HW : 4 * HW]
    final_norm, final_inv = normalize(stream)
    final_low = (final_norm * (1.0 + final_mod[:, HW:]) + final_mod[:, :HW]).astype(jnp.bfloat16)
    predicted = dot_right(final_low, edge_rows[D + CH : D + 2 * CH])
    flat_weights = weight_rows.reshape(-1)
    errors = jnp.mean((predicted - target) ** 2, -1)
    loss_local = jnp.sum(flat_weights * errors)
    back_pred = (flat_weights[:, None] * 2.0 * (predicted - target) / (CH * weight_total)).astype(
        jnp.bfloat16
    )
    grad_out_rows = dot_left(back_pred, final_low)
    back_final = dot_plain(back_pred, edge_rows[D + CH : D + 2 * CH])
    back_final_mod = jnp.concatenate([back_final, back_final * final_norm], 1).astype(jnp.bfloat16)
    grad_final = dot_left(silu_cond, back_final_mod)
    back_silu = dot_right(back_final_mod, final_weights)
    back_stream = norm_back(back_final * (1.0 + final_mod[:, HW:]), final_norm, final_inv)
    block_grads = []
    bias_grads = []
    for block_number in reversed(range(HB)):
        modulation, normed, inverse, shaped, inner_rows, hidden, branch = saved[block_number]
        back_branch = (back_stream * modulation[:, 2 * HW :]).astype(jnp.bfloat16)
        back_gate = back_stream * branch
        grad_down = dot_left(back_branch, hidden)
        back_hidden = dot_plain(back_branch, blocks[block_number, :, 4 * HW :])
        back_inner = local_grad(jax.nn.silu, inner_rows, back_hidden).astype(jnp.bfloat16)
        grad_up = dot_left(shaped, back_inner)
        back_shaped = dot_right(back_inner, blocks[block_number, :, 3 * HW : 4 * HW])
        back_stream = back_stream + norm_back(
            back_shaped * (1.0 + modulation[:, HW : 2 * HW]), normed, inverse
        )
        back_modulation = jnp.concatenate([back_shaped, back_shaped * normed, back_gate], 1).astype(
            jnp.bfloat16
        )
        grad_modulation = dot_left(silu_cond, back_modulation)
        back_silu = back_silu + dot_right(back_modulation, blocks[block_number, :, : 3 * HW])
        block_grads.insert(0, jnp.concatenate([grad_modulation, grad_up, grad_down], 1))
        bias_grads.insert(
            0,
            jnp.concatenate(
                [column_sum(back_modulation), column_sum(back_inner), column_sum(back_branch)]
            ),
        )
    back_stream_low = back_stream.astype(jnp.bfloat16)
    grad_in_rows = dot_left(noisy_rows, back_stream_low)
    back_conditioning = local_grad(jax.nn.silu, conditioning, back_silu)
    back_time = back_conditioning.astype(jnp.bfloat16)
    grad_time_two = dot_left(time_hidden, back_time)
    back_time_hidden = dot_right(back_time, time_second)
    back_time_inner = local_grad(jax.nn.silu, time_inner, back_time_hidden).astype(jnp.bfloat16)
    grad_time_one = dot_left(time_embed, back_time_inner)
    back_cond = back_conditioning.reshape(token_count, COPIES, HW).sum(1).astype(jnp.bfloat16)
    grad_cond_rows = dot_left(cond_rows, back_cond)
    back_tokens = dot_right(back_cond, edge_rows[:D])
    bias_grads.append(
        jnp.concatenate(
            [
                column_sum(back_time_inner),
                column_sum(back_time),
                column_sum(back_final_mod),
                column_sum(back_stream_low),
            ]
        )
    )
    grad_edges = jnp.concatenate(
        [
            grad_cond_rows,
            grad_in_rows,
            grad_out_rows,
            grad_time_one,
            grad_time_two,
            grad_final[:, :HW],
            grad_final[:, HW:],
        ],
        0,
    )
    return (loss_local, jnp.stack(block_grads), jnp.stack(bias_grads), grad_edges, back_tokens)


def invert(order_row):
    return (
        jnp.zeros(order_row.shape, jnp.int32)
        .at[order_row]
        .set(jnp.arange(order_row.shape[0], dtype=jnp.int32))
    )


def add_counts(earlier, later):
    return earlier + later


def adamw(master, first, second, gradient, factor, step_rate):
    clipped = gradient * factor
    first_new = BETA_ONE * first + (1.0 - BETA_ONE) * clipped
    second_new = BETA_TWO * second + (1.0 - BETA_TWO) * clipped * clipped
    mean_hat = first_new / (1.0 - BETA_ONE**ADAM_STEP)
    var_hat = second_new / (1.0 - BETA_TWO**ADAM_STEP)
    updated = master - step_rate * (mean_hat / (jnp.sqrt(var_hat) + ADAM_EPS) + DECAY_RATE * master)
    return (updated, first_new, second_new)


def on_device(
    latents,
    orders,
    mask_counts,
    noise,
    timesteps,
    loss_weights,
    block_weights,
    block_gains,
    entry_table,
    head_weights,
    head_biases,
    head_edges,
    first_blocks,
    first_gains,
    first_entry,
    first_head,
    first_biases,
    first_edges,
    second_blocks,
    second_gains,
    second_entry,
    second_head,
    second_biases,
    second_edges,
):
    low_blocks = block_weights.astype(jnp.bfloat16)
    low_gains = block_gains.astype(jnp.bfloat16)
    low_entry = entry_table.astype(jnp.bfloat16)
    low_head = head_weights.astype(jnp.bfloat16)
    low_biases = head_biases.astype(jnp.bfloat16)
    low_edges = head_edges.astype(jnp.bfloat16)
    full_blocks, full_gains, full_entry, full_head, full_biases, full_edges = (
        lax.all_gather(low_blocks, ("dp", "fsdp"), axis=1, tiled=True),
        lax.all_gather(low_gains, ("dp", "fsdp"), axis=2, tiled=True),
        lax.all_gather(low_entry, ("dp", "fsdp"), axis=1, tiled=True),
        lax.all_gather(low_head, ("dp", "fsdp"), axis=1, tiled=True),
        lax.all_gather(low_biases, ("dp", "fsdp"), axis=1, tiled=True),
        lax.all_gather(low_edges, ("dp", "fsdp"), axis=1, tiled=True),
    )
    devices = lax.axis_size(("dp", "fsdp"))
    local_total = jnp.sum(mask_counts)
    offset = entering(local_total, ("dp", "fsdp"), add_counts, jnp.zeros((), jnp.int32))
    weight_total = lax.psum(jnp.sum(loss_weights), ("dp", "fsdp"))
    images = orders.shape[0]
    ranks = jax.vmap(invert)(orders)
    masked = ranks < mask_counts[:, None]
    key_keep = jnp.concatenate(
        [jnp.ones((images, BUF), jnp.float32), 1.0 - masked.astype(jnp.float32)], 1
    )
    clean_flat = latents.reshape(images * LAT, CH)
    positions = full_entry.astype(jnp.float32)
    projected = dot_plain(clean_flat, full_entry[2 * SEQ :]).reshape(images, LAT, D)
    start_rows = (
        jnp.concatenate([jnp.zeros((images, BUF, D), jnp.float32), projected], 1) + positions[:SEQ]
    )
    encoded, encoder_saved = layer_forward(
        start_rows.reshape(-1, D), full_blocks[0], full_gains[0], key_keep
    )
    decoder_input = (
        encoded.reshape(images, SEQ, D) * key_keep[..., None] + positions[SEQ : 2 * SEQ]
    ).reshape(-1, D)
    top_rows, decoder_saved = layer_forward(
        decoder_input, full_blocks[1], full_gains[1], jnp.ones((images, SEQ), jnp.float32)
    )
    local_slots = images * LAT
    count_ends = jnp.cumsum(mask_counts)
    starts = count_ends - mask_counts
    slot_ids = jnp.arange(local_slots, dtype=jnp.int32)
    image_of = jnp.minimum(
        jnp.sum((slot_ids[:, None] >= count_ends[None, :]).astype(jnp.int32), 1), images - 1
    )
    within = jnp.clip(slot_ids - starts[image_of], 0, LAT - 1)
    position = orders[image_of, within]
    top_index = image_of * SEQ + BUF + position
    latent_index = image_of * LAT + position
    capacity = (local_slots + devices - 1) // devices
    local_index = (
        jnp.mod(jnp.arange(devices, dtype=jnp.int32) - offset, devices)[:, None]
        + devices * jnp.arange(capacity, dtype=jnp.int32)[None, :]
    )
    is_valid = local_index < local_total
    safe_index = jnp.minimum(local_index, local_slots - 1)
    cond_send = jnp.where(is_valid[..., None], top_rows[top_index[safe_index]], 0.0).astype(
        jnp.bfloat16
    )
    clean_send = jnp.where(
        is_valid[..., None], clean_flat[latent_index[safe_index]], jnp.zeros((), jnp.bfloat16)
    )
    flag_send = is_valid.astype(jnp.bfloat16)
    cond_recv, clean_recv, flag_recv = (
        lax.all_to_all(cond_send, ("dp", "fsdp"), split_axis=0, concat_axis=0, tiled=True),
        lax.all_to_all(clean_send, ("dp", "fsdp"), split_axis=0, concat_axis=0, tiled=True),
        lax.all_to_all(flag_send, ("dp", "fsdp"), split_axis=0, concat_axis=0, tiled=True),
    )
    head_rows = noise.shape[0]
    is_live = flag_recv.reshape(-1) > 0
    ranked = jnp.cumsum(is_live.astype(jnp.int32)) - 1
    target_row = jnp.where(is_live, ranked, head_rows)
    cond_rows = (
        jnp.zeros((head_rows + 1, D), jnp.bfloat16)
        .at[target_row]
        .set(cond_recv.reshape(-1, D))[:head_rows]
    )
    clean_rows = (
        jnp.zeros((head_rows + 1, CH), jnp.bfloat16)
        .at[target_row]
        .set(clean_recv.reshape(-1, CH))[:head_rows]
    )
    loss_local, grad_head, grad_biases, grad_edges, back_tokens = head_pass(
        full_head,
        full_biases,
        full_edges,
        cond_rows,
        clean_rows,
        noise,
        timesteps,
        loss_weights,
        weight_total,
    )
    token_grads = back_tokens.astype(jnp.bfloat16)
    back_send = jnp.where(
        is_live[:, None],
        token_grads[jnp.minimum(target_row, head_rows - 1)],
        jnp.zeros((), jnp.bfloat16),
    ).reshape(devices, capacity, D)
    returned = lax.all_to_all(back_send, ("dp", "fsdp"), split_axis=0, concat_axis=0, tiled=True)
    arriving = jnp.where(is_valid[..., None], returned.astype(jnp.float32), 0.0)
    back_top = (
        jnp.zeros((images * SEQ, D), jnp.float32)
        .at[top_index[safe_index].reshape(-1)]
        .add(arriving.reshape(-1, D))
    )
    back_decoder, grad_decoder_block, grad_decoder_gain = layer_backward(
        back_top, full_blocks[1], full_gains[1], decoder_saved
    )
    back_encoded = (back_decoder.reshape(images, SEQ, D) * key_keep[..., None]).reshape(-1, D)
    back_start, grad_encoder_block, grad_encoder_gain = layer_backward(
        back_encoded, full_blocks[0], full_gains[0], encoder_saved
    )
    back_start = back_start.reshape(images, SEQ, D)
    grad_input = dot_left(clean_flat, back_start[:, BUF:].reshape(-1, D).astype(jnp.bfloat16))
    grad_entry = jnp.concatenate(
        [jnp.sum(back_start, 0), jnp.sum(back_decoder.reshape(images, SEQ, D), 0), grad_input], 0
    )
    grad_blocks = jnp.stack([grad_encoder_block, grad_decoder_block])
    grad_gains = jnp.stack([grad_encoder_gain, grad_decoder_gain])
    block_grad, gain_grad, entry_grad, head_grad, bias_grad, edge_grad = (
        lax.psum_scatter(grad_blocks, ("dp", "fsdp"), scatter_dimension=1, tiled=True),
        lax.psum_scatter(grad_gains, ("dp", "fsdp"), scatter_dimension=2, tiled=True),
        lax.psum_scatter(grad_entry, ("dp", "fsdp"), scatter_dimension=1, tiled=True),
        lax.psum_scatter(grad_head, ("dp", "fsdp"), scatter_dimension=1, tiled=True),
        lax.psum_scatter(grad_biases, ("dp", "fsdp"), scatter_dimension=1, tiled=True),
        lax.psum_scatter(grad_edges, ("dp", "fsdp"), scatter_dimension=1, tiled=True),
    )
    local_squares = (
        jnp.sum(block_grad * block_grad)
        + jnp.sum(gain_grad * gain_grad)
        + jnp.sum(entry_grad * entry_grad)
        + jnp.sum(head_grad * head_grad)
        + jnp.sum(bias_grad * bias_grad)
        + jnp.sum(edge_grad * edge_grad)
    )
    loss_sum, squares = lax.psum((loss_local, local_squares), ("dp", "fsdp"))
    grad_norm = jnp.sqrt(squares)
    factor = CLIP_NORM / jnp.maximum(grad_norm, CLIP_NORM)
    new_blocks = adamw(block_weights, first_blocks, second_blocks, block_grad, factor, LEARN_RATE)
    new_gains = adamw(block_gains, first_gains, second_gains, gain_grad, factor, GAIN_RATE)
    new_entry = adamw(entry_table, first_entry, second_entry, entry_grad, factor, LEARN_RATE)
    new_head = adamw(head_weights, first_head, second_head, head_grad, factor, LEARN_RATE)
    new_biases = adamw(head_biases, first_biases, second_biases, bias_grad, factor, LEARN_RATE)
    new_edges = adamw(head_edges, first_edges, second_edges, edge_grad, factor, LEARN_RATE)
    return (
        new_blocks[0],
        new_gains[0],
        new_entry[0],
        new_head[0],
        new_biases[0],
        new_edges[0],
        new_blocks[1],
        new_gains[1],
        new_entry[1],
        new_head[1],
        new_biases[1],
        new_edges[1],
        new_blocks[2],
        new_gains[2],
        new_entry[2],
        new_head[2],
        new_biases[2],
        new_edges[2],
        loss_sum,
        weight_total,
        grad_norm,
    )


def solution(mesh):
    in_specs = (
        P(("dp", "fsdp"), None, None),
        P(("dp", "fsdp"), None),
        P(("dp", "fsdp")),
        P(("dp", "fsdp"), None),
        P(("dp", "fsdp"), None),
        P(("dp", "fsdp"), None),
        P(None, ("dp", "fsdp"), None),
        P(None, None, ("dp", "fsdp")),
        P(None, ("dp", "fsdp")),
        P(None, ("dp", "fsdp"), None),
        P(None, ("dp", "fsdp")),
        P(None, ("dp", "fsdp")),
        P(None, ("dp", "fsdp"), None),
        P(None, None, ("dp", "fsdp")),
        P(None, ("dp", "fsdp")),
        P(None, ("dp", "fsdp"), None),
        P(None, ("dp", "fsdp")),
        P(None, ("dp", "fsdp")),
        P(None, ("dp", "fsdp"), None),
        P(None, None, ("dp", "fsdp")),
        P(None, ("dp", "fsdp")),
        P(None, ("dp", "fsdp"), None),
        P(None, ("dp", "fsdp")),
        P(None, ("dp", "fsdp")),
    )
    out_specs = (
        P(None, ("dp", "fsdp"), None),
        P(None, None, ("dp", "fsdp")),
        P(None, ("dp", "fsdp")),
        P(None, ("dp", "fsdp"), None),
        P(None, ("dp", "fsdp")),
        P(None, ("dp", "fsdp")),
        P(None, ("dp", "fsdp"), None),
        P(None, None, ("dp", "fsdp")),
        P(None, ("dp", "fsdp")),
        P(None, ("dp", "fsdp"), None),
        P(None, ("dp", "fsdp")),
        P(None, ("dp", "fsdp")),
        P(None, ("dp", "fsdp"), None),
        P(None, None, ("dp", "fsdp")),
        P(None, ("dp", "fsdp")),
        P(None, ("dp", "fsdp"), None),
        P(None, ("dp", "fsdp")),
        P(None, ("dp", "fsdp")),
        P(),
        P(),
        P(),
    )
    return jax.shard_map(
        on_device, mesh=mesh, in_specs=in_specs, out_specs=out_specs, check_vma=False
    )
```

profile of v0, /device:TPU:0, one launch (start us, length us, event | category | flops | bytes accessed | tf_op | source)
XLA Modules:
  0.0 2602.9 jit_solution(6783415894485542438)
XLA Ops:
  13.5 42.6 %all-reduce.2 = s32[32]{0:T(128)S(1)} all-reduce(s32[32]{0:T(128)S(1)} %dynamic-update-slice), channel_id=1, replica_groups=mesh['dp'=8,'fsdp'=4] {'dp','fsdp'}, use_global_device_ids=true, to_apply=%add.2 | all-reduce | flops 32 | bytes 256
  56.1 40.3 %while.13 = (s32[]{:T(128)}, s32[]{:T(128)}, s32[]{:T(128)}, s32[32]{0:T(128)S(1)}, s32[]{:T(128)}) while((s32[]{:T(128)}, s32[]{:T(128)}, s32[]{:T(128)}, s32[32]{0:T(128)S(1)}, s32[]{:T(128)}) %tuple.130), condition=%wide.region_6.7_spmd, body=%wide.region_5.6_spmd.sunk | while | flops 5 | bytes 107 | solution.py:44
  102.0 97.0 %all_gather.22 = bf16[656,768]{0,1:T(8,128)(2,1)S(1)} all-gather(bf16[656,24]{0,1:T(8,128)(2,1)S(1)} %convert_element_type.273), channel_id=1, replica_groups=mesh['dp'=8,'fsdp'=4] {'dp','fsdp'}, dimensions={1}, use_global_device_ids=true | all-gather | bytes 1039104 | tf_op jit(solution)/shard_map/all_gather | solution.py:381
  208.8 65.9 %all-gather = bf16[32,160,3]{1,2,0:T(4,128)(2,1)S(1)} all-gather(bf16[1,160,3]{1,2,0:T(4,128)(2,1)S(1)} %convert_bitcast_fusion.1), channel_id=1, replica_groups=mesh['dp'=8,'fsdp'=4] {'dp','fsdp'}, dimensions={0}, use_global_device_ids=true | all-gather | bytes 31680 | tf_op jit(solution)/shard_map/all_gather | solution.py:383
  277.9 73.0 %all_gather.23 = bf16[2,2,768]{1,0,2:T(2,128)(2,1)S(1)} all-gather(bf16[2,2,24]{1,0,2:T(2,128)(2,1)S(1)} %copy.247), channel_id=1, replica_groups=mesh['dp'=8,'fsdp'=4] {'dp','fsdp'}, dimensions={2}, use_global_device_ids=true | all-gather | bytes 6336 | tf_op jit(solution)/shard_map/all_gather | solution.py:380
  359.3 9.5 slice_reduce_fusion
  368.9 41.0 %psum.21 = f32[]{:T(128)} all-reduce(f32[]{:T(128)} %get-tuple-element.286), channel_id=1, replica_groups=mesh['dp'=8,'fsdp'=4] {'dp','fsdp'}, use_global_device_ids=true, to_apply=%region_26.27 | all-reduce | flops 1 | bytes 8 | tf_op jit(solution)/shard_map/psum | solution.py:389
  432.4 16.6 slice_bitcast_fusion
  582.4 10.6 fusion.7
  625.7 9.0 fusion.73
  675.5 10.1 fusion.2
  685.6 12.8 convert_reduce_fusion.4
  814.2 17.8 copy.308
  870.2 19.7 maximum_bitcast_fusion
  889.9 18.8 maximum_bitcast_fusion.1
  908.8 37.4 %pad_maximum_fusion = f32[2,768,9216]{2,1,0:T(8,128)} fusion(f32[1,768,9216]{2,1,0:T(8,128)} %maximum_bitcast_fusion.1, f32[1,768,9216]{2,1,0:T(8,128)} %maximum_bitcast_fusion), kind=kLoop, calls=%fused_computation.12 | loop fusion | flops 14155776 | bytes 113246208 | tf_op jit(solution)/shard_map/stack | solution.py:491
  973.7 9.9 maximum_bitcast_fusion.2
  992.1 17.2 maximum_bitcast_fusion.3
  1009.3 23.8 pad_maximum_fusion.1
  1036.4 43.6 %all-reduce.3 = f32[2,2,768]{2,1,0:T(2,128)S(1)} all-reduce(f32[2,2,768]{2,1,0:T(2,128)S(1)} %pad_maximum_fusion.24), channel_id=3, replica_groups=mesh['dp'=8,'fsdp'=4] {'dp','fsdp'}, use_global_device_ids=true, to_apply=%region_47.48.clone | all-reduce | flops 3072 | bytes 24576
  1082.4 88.5 %reduce-scatter.21.cloned.1.call-done = f32[32,4128]{1,0:T(8,128)} async-done(((f32[1024,4128]{1,0:T(8,128)}), f32[32,4128]{1,0:T(8,128)}) %reduce-scatter.21.cloned.1.call-update) | async-done | bytes 528400
  1173.8 475.5 %reduce-scatter.13.cloned.1.call-done = f32[2,24,9216]{2,1,0:T(8,128)} async-done(((f32[2,768,9216]{2,1,0:T(8,128)}), f32[2,24,9216]{2,1,0:T(8,128)}) %reduce-scatter.13.cloned.1.call-update) | async-done | bytes 1769488 | tf_op jit(solution)/shard_map/reduce_scatter | solution.py:494
  1653.8 882.5 %reduce-scatter.15.cloned.1.call-done = f32[2,32,5120]{2,1,0:T(8,128)} async-done(((f32[2,1024,5120]{2,1,0:T(8,128)}), f32[2,32,5120]{2,1,0:T(8,128)}) %reduce-scatter.15.cloned.1.call-update) | async-done | bytes 1310736 | tf_op jit(solution)/shard_map/reduce_scatter | solution.py:497
  2540.7 40.9 %all-reduce.4 = (f32[]{:T(128)}, f32[]{:T(128)}) all-reduce(f32[]{:T(128)S(6)} %add.688, f32[]{:T(128)} %multiply_reduce_fusion.29), channel_id=1, replica_groups=mesh['dp'=8,'fsdp'=4] {'dp','fsdp'}, use_global_device_ids=true, to_apply=%region_71.72 | all-reduce | flops 2 | bytes 16 | tf_op jit(solution)/shard_map/psum | solution.py:509
  (784 shorter events, 493.0 us)
Async XLA Ops:
  7.2 421.1 %all-gather.7.cloned.1.call-start = ((), (), s32[]{:S(2)}) async-start(), calls=%async_computation.10 | async-start | bytes 8921088 | tf_op jit(solution)/shard_map/all_gather | solution.py:384
  9.2 423.2 %all-gather.5.cloned.1.call-start = ((), (), s32[]{:S(2)}) async-start(), calls=%async_computation.9 | async-start | bytes 29196288 | tf_op jit(solution)/shard_map/all_gather | solution.py:379
  11.7 549.8 %all-gather.9.cloned.1.call-start = ((), (), s32[]{:S(2)}) async-start(), calls=%async_computation.11 | async-start | bytes 21626880 | tf_op jit(solution)/shard_map/all_gather | solution.py:382
  97.2 316.9 %all-to-all-start = ((bf16[32,1,8]{2,1,0:T(2,128)(2,1)}), bf16[32,1,8]{2,1,0:T(2,128)(2,1)}, u32[]{:S(2)}, u32[]{:S(2)}) async-start(bf16[32,1,8]{2,1,0:T(2,128)(2,1)} %copy.250), calls=%async_computation | async-start | bytes 32768 | tf_op jit(solution)/shard_map/all_to_all | solution.py:439
  201.9 149.3 %copy-start.47 = (f32[656,768]{1,0:T(8,128)}, f32[656,768]{1,0:T(8,128)S(1)}, u32[]{:S(2)}) copy-start(f32[656,768]{1,0:T(8,128)S(1)} %convert_element_type.274) | copy-start | bytes 6045700
  208.6 145.8 %copy-start.182 = (f32[192,4]{0,1:T(4,128)S(1)}, f32[192,4]{0,1:T(4,128)}, u32[]{:S(2)}) copy-start(f32[192,4]{0,1:T(4,128)} %param.31) | copy-start | bytes 9220
  358.8 170.7 %copy-start.78 = (bf16[768,128]{1,0:T(8,128)(2,1)}, bf16[768,128]{1,0:T(8,128)(2,1)S(1)}, u32[]{:S(2)}) copy-start(bf16[768,128]{1,0:T(8,128)(2,1)S(1)} %get-tuple-element.283) | copy-start | bytes 589828
  358.8 170.7 %copy-start.79 = (bf16[768,128]{1,0:T(8,128)(2,1)}, bf16[768,128]{1,0:T(8,128)(2,1)S(1)}, u32[]{:S(2)}) copy-start(bf16[768,128]{1,0:T(8,128)(2,1)S(1)} %get-tuple-element.284) | copy-start | bytes 589828
  414.1 12.2 all-to-all-start.1
  526.1 15.1 all-to-all-start.2
  711.0 16.7 all-to-all-start.3
  715.2 319.5 %reduce-scatter.19.cloned.1.call-start = ((), (), s32[]{:S(2)}) async-start(), calls=%async_computation.15 | async-start | bytes 2703360
  724.4 356.3 %reduce-scatter.17.cloned.1.call-start = ((), (), s32[]{:S(2)}) async-start(), calls=%async_computation.14 | async-start | bytes 2433024
  793.7 377.2 %reduce-scatter.21.cloned.1.call-start = ((), (), s32[]{:S(2)}) async-start(), calls=%async_computation.16 | async-start | bytes 17842176
  832.0 817.4 %reduce-scatter.13.cloned.1.call-start = ((), (), s32[]{:S(2)}) async-start(), calls=%async_computation.12 | async-start | bytes 58392576 | tf_op jit(solution)/shard_map/reduce_scatter | solution.py:494
  946.2 1590.1 %reduce-scatter.15.cloned.1.call-start = ((), (), s32[]{:S(2)}) async-start(), calls=%async_computation.13 | async-start | bytes 43253760 | tf_op jit(solution)/shard_map/reduce_scatter | solution.py:497
  1172.6 1409.7 %copy-start.185 = (f32[3,160]{1,0:T(4,128)S(1)}, f32[3,160]{1,0:T(4,128)}, u32[]{:S(2)}) copy-start(f32[3,160]{1,0:T(4,128)} %param.36) | copy-start | bytes 5764
  1172.6 1409.7 %copy-start.191 = (f32[3,160]{1,0:T(4,128)S(1)}, f32[3,160]{1,0:T(4,128)}, u32[]{:S(2)}) copy-start(f32[3,160]{1,0:T(4,128)} %param.42) | copy-start | bytes 5764
  1172.6 1409.7 %copy-start.192 = (f32[3,160]{1,0:T(4,128)S(1)}, f32[3,160]{1,0:T(4,128)}, u32[]{:S(2)}) copy-start(f32[3,160]{1,0:T(4,128)} %param.48) | copy-start | bytes 5764
  1172.6 1410.3 %copy-start.189 = (f32[2,2,24]{2,1,0:T(2,128)S(1)}, f32[2,2,24]{2,1,0:T(2,128)}, u32[]{:S(2)}) copy-start(f32[2,2,24]{2,1,0:T(2,128)} %param.33) | copy-start | bytes 1156
  1172.7 1410.3 %copy-start.208 = (f32[2,2,24]{2,1,0:T(2,128)S(1)}, f32[2,2,24]{2,1,0:T(2,128)}, u32[]{:S(2)}) copy-start(f32[2,2,24]{2,1,0:T(2,128)} %param.39) | copy-start | bytes 1156
  1172.7 1410.3 %copy-start.209 = (f32[2,2,24]{2,1,0:T(2,128)S(1)}, f32[2,2,24]{2,1,0:T(2,128)}, u32[]{:S(2)}) copy-start(f32[2,2,24]{2,1,0:T(2,128)} %param.45) | copy-start | bytes 1156
  1172.7 1411.0 %copy-start.71 = (f32[4128,32]{0,1:T(8,128)S(1)}, f32[4128,32]{0,1:T(8,128)}, u32[]{:S(2)}) copy-start(f32[4128,32]{0,1:T(8,128)} %param.37) | copy-start | bytes 1585156
  1173.8 1412.6 %copy-start.46 = (f32[2,32,5120]{2,1,0:T(8,128)S(1)}, f32[2,32,5120]{2,1,0:T(8,128)}, u32[]{:S(2)}) copy-start(f32[2,32,5120]{2,1,0:T(8,128)} %param.35) | copy-start | bytes 3932164
  (217 other events, 2047.6 us)
Sparse Core Ops, SparseCore 0:
  11.4 81.6 all-gather.6
  96.8 188.0 all-gather.4
  288.3 136.6 all-gather.8
  724.5 141.4 reduce-scatter.18
  871.2 97.1 reduce-scatter.16
  975.8 195.0 reduce-scatter.20
  1178.5 470.7 reduce-scatter.12
  1651.7 884.6 reduce-scatter.14
where the time goes:
time: 2610 us; the launch traced here: 2600 us
  waiting for transfers between devices  1450 us (56%)
  blocking collectives  404 us (15%)
  matrix products  317 us (12%)
  other arithmetic  206 us (8%)
  local copies, waits for them, and re-layouts  159 us (6%)
    reduce_scatter x1, waiting for transfers between devices, on_device(): lax.psum_scatter(grad_head, ('dp', 'fsdp'), scatter_dimension=1, tiled=True)  883 us
    reduce_scatter x1, waiting for transfers between devices, on_device(): lax.psum_scatter(grad_blocks, ('dp', 'fsdp'), scatter_dimension=1, tiled=...  476 us
    dot_general x18, matrix products, dot_right(): lax.dot_general(left, right, (((1,), (1,)), ((), ())), preferred_element_...  101 us
    all_gather x1, blocking collectives, on_device(): lax.all_gather(low_entry, ('dp', 'fsdp'), axis=1, tiled=True)  97 us
    dot_general x21, matrix products, dot_plain(): return jnp.dot(left, right, preferred_element_type=jnp.float32)  91.4 us
    dot_general x21, matrix products, dot_left(): lax.dot_general(left, right, (((0,), (0,)), ((), ())), preferred_element_...  90.3 us
    unnamed x11, waiting for transfers between devices  88.6 us
    unnamed x2, blocking collectives  86.3 us
  transfers between devices with their start and end apart: 12, of which 5 were waited for; matrix products, arithmetic and copies ran while one was open for 19% of the time, Pallas kernels for 0%

commit v1 on v0

v1 whole, which is shorter than its diff:
```python
import functools
import math

import jax
import jax.numpy as jnp
from jax import lax
from jax.experimental import pallas as pl
from jax.experimental.pallas import tpu as pltpu
from jax.sharding import PartitionSpec as P

D = 768
HEADS = 12
HD = 64
FF = 3072
HW = 1024
CH = 16
FREQ = 256
LAT = 256
BUF = 64
HB = 2
COPIES = 4
TSTEPS = 1000
ADAM_STEP = 5
SEQ = 320

BETA_ONE = 0.5
BETA_TWO = 0.5
LEARN_RATE = 0.03
GAIN_RATE = 0.3
DECAY_RATE = 0.02
ADAM_EPS = 1e-08
CLIP_NORM = 0.002
NORM_EPS = 1e-06
AXES = ("dp", "fsdp")
HEAD_DIRECT = False
MESH_IDS = pl.DeviceIdType.MESH


def rs_kernel(nz, row_count, width, jobs, extra_count, *refs):
    job_count = len(jobs)
    x_refs, y_refs = refs[:job_count], refs[job_count : 2 * job_count]
    position = 2 * job_count
    extra_ref = None
    if extra_count:
        extra_ref = refs[position]
        position += 1
    out_ref = refs[position]
    (
        x_buf, y_buf, whole, land_core, first, land_first, second, land_second,
        last, last_low, land_last,
        load_sem, core_send, core_recv, first_send, first_recv, second_send, second_recv,
        last_send, last_recv, credit,
    ) = refs[position + 1 :]
    dp, z = lax.axis_index("dp"), lax.axis_index("fsdp")
    core, xb, yb = lax.rem(dp, 2), lax.rem(dp // 2, 2), dp // 4
    group = row_count // 8
    part = group // nz
    starts, total = [], 0
    for _, columns in jobs:
        starts.append(total)
        total += columns // width
    computed = total
    total += extra_count

    core_peer = (dp + 1 - 2 * core, z)
    x_step, y_step = 2 - 4 * xb, 4 - 8 * yb
    z_peers = [(dp, lax.rem(z + s, nz)) for s in range(1, nz)]
    barrier = pltpu.get_barrier_semaphore()
    for peer in [core_peer, (dp + x_step, z), (dp + y_step, z)] + z_peers:
        pl.semaphore_signal(barrier, inc=1, device_id=peer, device_id_type=MESH_IDS)
    pl.semaphore_wait(barrier, 2 + nz)

    def loads(x_ref, y_ref, column, slot):
        return (
            pltpu.make_async_copy(x_ref, x_buf.at[slot], load_sem.at[0, slot]),
            pltpu.make_async_copy(
                y_ref.at[:, pl.ds(pl.multiple_of(column, 128), width)], y_buf.at[slot], load_sem.at[1, slot]
            ),
        )

    def prefetch(g):
        for number, (_, columns) in enumerate(jobs):
            start, stop = starts[number], starts[number] + columns // width

            @pl.when((g >= start) & (g < stop))
            def _():
                for copy in loads(x_refs[number], y_refs[number], (g - start) * width, lax.rem(g, 2)):
                    copy.start()

    def core_copy(g):
        return pltpu.make_async_remote_copy(
            src_ref=whole.at[lax.rem(g, 2), 1 - core],
            dst_ref=land_core.at[lax.rem(g, 4)],
            send_sem=core_send.at[lax.rem(g, 2)],
            recv_sem=core_recv.at[lax.rem(g, 4)],
            device_id=core_peer,
            device_id_type=MESH_IDS,
        )

    def first_copy(g):
        p = lax.rem(g, 2)
        mine = (1 - p) * xb + p * yb
        return pltpu.make_async_remote_copy(
            src_ref=first.at[lax.rem(g, 3), 1 - mine],
            dst_ref=land_first.at[g],
            send_sem=first_send.at[lax.rem(g, 3)],
            recv_sem=first_recv.at[g],
            device_id=(dp + (1 - p) * x_step + p * y_step, z),
            device_id_type=MESH_IDS,
        )

    def second_copy(g):
        p = lax.rem(g, 2)
        mine = (1 - p) * yb + p * xb
        return pltpu.make_async_remote_copy(
            src_ref=second.at[lax.rem(g, 3), 1 - mine],
            dst_ref=land_second.at[g],
            send_sem=second_send.at[lax.rem(g, 3)],
            recv_sem=second_recv.at[g],
            device_id=(dp + (1 - p) * y_step + p * x_step, z),
            device_id_type=MESH_IDS,
        )

    def last_copies(g):
        return [
            pltpu.make_async_remote_copy(
                src_ref=last_low.at[lax.rem(g, 3), lax.rem(z + s, nz)],
                dst_ref=land_last.at[g, s - 1],
                send_sem=last_send.at[lax.rem(g, 3), s - 1],
                recv_sem=last_recv.at[g, s - 1],
                device_id=z_peers[s - 1],
                device_id_type=MESH_IDS,
            )
            for s in range(1, nz)
        ]

    low_rows, low_width = last_low.shape[2:]
    folds = width // low_width

    def fold(block):
        return jnp.concatenate([block[:, k * low_width : (k + 1) * low_width] for k in range(folds)], 0)

    def stage_core(g):
        slot = lax.rem(g, 2)

        @pl.when(g >= 2)
        def _():
            core_copy(g - 2).wait_send()

        def put(number, value):
            yx, c = number // 2, number % 2
            whole[slot, c, yx] = value

        @pl.when(g < computed)
        def _():
            for copy in loads(x_refs[0], y_refs[0], 0, slot):
                copy.wait()
            for number in range(8):
                put(number, lax.dot_general(
                    x_buf[slot, :, pl.ds(number * group, group)], y_buf[slot],
                    (((0,), (0,)), ((), ())), preferred_element_type=jnp.float32,
                ).astype(jnp.bfloat16))

        if extra_count:
            @pl.when(g >= computed)
            def _():
                for number in range(8):
                    put(number, extra_ref[g - computed, pl.ds(number * group, group), :])

        @pl.when(g >= 4)
        def _():
            pl.semaphore_wait(credit, 1)
        core_copy(g).start()

    def stage_first(g):
        p = lax.rem(g, 2)

        @pl.when(g >= 3)
        def _():
            first_copy(g - 3).wait_send()
        core_copy(g).wait_recv()
        for f in range(2):
            for s in range(2):
                yx = (1 - p) * (2 * s + f) + p * (2 * f + s)
                first[lax.rem(g, 3), f, s] = (
                    whole[lax.rem(g, 2), core, yx].astype(jnp.float32)
                    + land_core[lax.rem(g, 4), yx].astype(jnp.float32)
                ).astype(jnp.bfloat16)

        @pl.when(g < total - 4)
        def _():
            pl.semaphore_signal(credit, inc=1, device_id=core_peer, device_id_type=MESH_IDS)
        first_copy(g).start()

    def stage_second(g):
        p = lax.rem(g, 2)
        mine = (1 - p) * xb + p * yb

        @pl.when(g >= 3)
        def _():
            second_copy(g - 3).wait_send()
        first_copy(g).wait_recv()
        for s in range(2):
            second[lax.rem(g, 3), s] = (
                first[lax.rem(g, 3), mine, s].astype(jnp.float32) + land_first[g, s].astype(jnp.float32)
            ).astype(jnp.bfloat16)
        second_copy(g).start()

    def stage_last(g):
        p = lax.rem(g, 2)
        mine = (1 - p) * yb + p * xb

        @pl.when(g >= 3)
        def _():
            for copy in last_copies(g - 3):
                copy.wait_send()
        second_copy(g).wait_recv()
        summed = second[lax.rem(g, 3), mine].astype(jnp.float32) + land_second[g].astype(jnp.float32)
        for k in range(nz):
            block = fold(summed[k * part : (k + 1) * part])
            last[lax.rem(g, 3), k] = block
            last_low[lax.rem(g, 3), k] = block.astype(jnp.bfloat16)
        for copy in last_copies(g):
            copy.start()

    def stage_out(g):
        for copy in last_copies(g):
            copy.wait_recv()
        value = last[lax.rem(g, 3), z]
        for s in range(1, nz):
            value = value + land_last[g, s - 1].astype(jnp.float32)
        for k in range(folds):
            out_ref[g, :, pl.ds(k * low_width, low_width)] = value[k * part : (k + 1) * part]

    lags = (0, 1, 3, 5, 7)
    prefetch(0)

    @pl.loop(0, total + lags[-1])
    def _(i):
        for stage, lag in zip((stage_out, stage_last, stage_second, stage_first), lags[:0:-1]):
            @pl.when((i >= lag) & (i < total + lag))
            def _():
                stage(i - lag)

        @pl.when(i + 1 < computed)
        def _():
            prefetch(i + 1)

        @pl.when(i < total)
        def _():
            stage_core(i)

    for g in range(max(total - 2, 0), total):
        core_copy(g).wait_send()
    for g in range(max(total - 3, 0), total):
        first_copy(g).wait_send()
        second_copy(g).wait_send()
        for copy in last_copies(g):
            copy.wait_send()


def reduce_products(pairs, extras, row_count, width, low_shape, nz, collective_id):
    bf, tokens = jnp.bfloat16, pairs[0][0].shape[0]
    group, part = row_count // 8, row_count // 8 // nz
    jobs = [(x.shape[1], y.shape[1]) for x, y in pairs]
    total = sum(columns // width for _, columns in jobs)
    extra_count = 0 if extras is None else extras.shape[0]
    total += extra_count
    low_rows, low_width = low_shape
    dma, reg = pltpu.SemaphoreType.DMA, pltpu.SemaphoreType.REGULAR
    operands = [x for x, _ in pairs] + [y for _, y in pairs]
    specs = [pl.BlockSpec(memory_space=pl.ANY)] * len(operands)
    if extra_count:
        operands.append(extras)
        specs.append(pl.BlockSpec(memory_space=pltpu.VMEM))
    return pl.pallas_call(
        functools.partial(rs_kernel, nz, row_count, width, jobs, extra_count),
        out_shape=jax.ShapeDtypeStruct((total, part, width), jnp.float32),
        in_specs=specs,
        out_specs=pl.BlockSpec(memory_space=pltpu.VMEM),
        scratch_shapes=[
            pltpu.VMEM((2, tokens, row_count), bf),
            pltpu.VMEM((2, tokens, width), bf),
            pltpu.VMEM((2, 2, 4, group, width), bf),
            pltpu.VMEM((4, 4, group, width), bf),
            pltpu.VMEM((3, 2, 2, group, width), bf),
            pltpu.VMEM((total, 2, group, width), bf),
            pltpu.VMEM((3, 2, group, width), bf),
            pltpu.VMEM((total, group, width), bf),
            pltpu.VMEM((3, nz, low_rows, low_width), jnp.float32),
            pltpu.VMEM((3, nz, low_rows, low_width), bf),
            pltpu.VMEM((total, nz - 1, low_rows, low_width), bf),
            dma((2, 2)), dma((2,)), dma((4,)), dma((3,)), dma((total,)), dma((3,)), dma((total,)),
            dma((3, nz - 1)), dma((total, nz - 1)), reg,
        ],
        compiler_params=pltpu.CompilerParams(
            collective_id=collective_id, has_side_effects=True, vmem_limit_bytes=56 * 2**20
        ),
    )(*operands)


def ag_kernel(nz, chunks, source_count, *refs):
    sources, refs = refs[:source_count], refs[source_count:]
    result_count = 1 + max(chunk[3] for chunk in chunks)
    results, sems = refs[:result_count], refs[result_count:]
    own_sem, last_send, last_recv, first_send, first_recv, second_send, second_recv, core_send, core_recv = sems
    dp, z = lax.axis_index("dp"), lax.axis_index("fsdp")
    core, xb, yb = lax.rem(dp, 2), lax.rem(dp // 2, 2), dp // 4
    core_peer = (dp + 1 - 2 * core, z)
    x_peer, y_peer = (dp + 2 - 4 * xb, z), (dp + 4 - 8 * yb, z)
    z_peers = [(dp, lax.rem(z + s, nz)) for s in range(1, nz)]
    barrier = pltpu.get_barrier_semaphore()
    for peer in [core_peer, x_peer, y_peer] + z_peers:
        pl.semaphore_signal(barrier, inc=1, device_id=peer, device_id_type=MESH_IDS)
    pl.semaphore_wait(barrier, 2 + nz)

    def remote(source, target, send, recv, peer):
        return pltpu.make_async_remote_copy(
            src_ref=source, dst_ref=target, send_sem=send, recv_sem=recv, device_id=peer, device_id_type=MESH_IDS
        )

    def source_of(k):
        source, index, column, _, _, width = chunks[k]
        ref = sources[source] if index is None else sources[source].at[index]
        return ref.at[:, pl.ds(column, width)]

    def result_of(k):
        _, _, _, result, column, width = chunks[k]
        return results[result].at[:, :, :, :, :, pl.ds(column, width)]

    def own(k):
        return pltpu.make_async_copy(source_of(k), result_of(k).at[yb, xb, core, z], own_sem.at[k])

    def z_copies(k):
        return [
            remote(source_of(k), result_of(k).at[yb, xb, core, z], last_send.at[k, s], last_recv.at[k, s], z_peers[s])
            for s in range(nz - 1)
        ]

    def first(k):
        ref = result_of(k).at[yb, xb, core]
        return remote(ref, ref, first_send.at[k], first_recv.at[k], y_peer if k % 2 else x_peer)

    def second(k):
        ref = result_of(k).at[:, xb, core] if k % 2 else result_of(k).at[yb, :, core]
        return remote(ref, ref, second_send.at[k], second_recv.at[k], x_peer if k % 2 else y_peer)

    def across(k):
        ref = result_of(k).at[:, :, core]
        return remote(ref, ref, core_send.at[k], core_recv.at[k], core_peer)

    total = len(chunks)
    for i in range(total + 6):
        k = i - 6
        if k >= 0:
            second(k).wait_recv()
            across(k).start()
        k = i - 4
        if 0 <= k < total:
            first(k).wait_recv()
            second(k).start()
        k = i - 2
        if 0 <= k < total:
            own(k).wait()
            for copy in z_copies(k):
                copy.wait_recv()
            first(k).start()
        if i < total:
            own(i).start()
            for copy in z_copies(i):
                copy.start()
    for k in range(total):
        for copy in z_copies(k) + [first(k), second(k), across(k)]:
            copy.wait_send()
        across(k).wait_recv()


def gather_rows(sources, chunks, widths, rows, nz, collective_id):
    dma = pltpu.SemaphoreType.DMA
    total = len(chunks)
    return pl.pallas_call(
        functools.partial(ag_kernel, nz, chunks, len(sources)),
        out_shape=[jax.ShapeDtypeStruct((2, 2, 2, nz, rows, width), jnp.bfloat16) for width in widths],
        in_specs=[pl.BlockSpec(memory_space=pl.ANY)] * len(sources),
        out_specs=[pl.BlockSpec(memory_space=pl.ANY)] * len(widths),
        scratch_shapes=[
            dma((total,)), dma((total, nz - 1)), dma((total, nz - 1)),
            dma((total,)), dma((total,)), dma((total,)), dma((total,)), dma((total,)), dma((total,)),
        ],
        compiler_params=pltpu.CompilerParams(
            collective_id=collective_id, has_side_effects=True, vmem_limit_bytes=4 * 2**20
        ),
    )(*sources)


def exchange_kernel(dp_count, nz, in_ref, out_ref, send_sem, recv_sem):
    devices = dp_count * nz
    me = lax.axis_index("dp") * nz + lax.axis_index("fsdp")

    def peer(step):
        there = lax.rem(me + step, devices)
        return (there // nz, lax.rem(there, nz))

    barrier = pltpu.get_barrier_semaphore()

    @pl.loop(1, devices)
    def _(step):
        pl.semaphore_signal(barrier, inc=1, device_id=peer(step), device_id_type=MESH_IDS)

    pl.semaphore_wait(barrier, devices - 1)

    def copy(step):
        return pltpu.make_async_remote_copy(
            src_ref=in_ref,
            dst_ref=out_ref.at[me],
            send_sem=send_sem.at[step - 1],
            recv_sem=recv_sem.at[step - 1],
            device_id=peer(step),
            device_id_type=MESH_IDS,
        )

    @pl.loop(1, devices)
    def _(step):
        copy(step).start()

    out_ref[me] = in_ref[...]

    @pl.loop(1, devices)
    def _(step):
        copy(step).wait()


def exchange(values, dp_count, nz, collective_id):
    devices = dp_count * nz
    tile = jnp.broadcast_to(jnp.pad(values, (0, 128 - values.shape[0])), (8, 128))
    out = pl.pallas_call(
        functools.partial(exchange_kernel, dp_count, nz),
        out_shape=jax.ShapeDtypeStruct((devices, 8, 128), jnp.float32),
        in_specs=[pl.BlockSpec(memory_space=pltpu.VMEM)],
        out_specs=pl.BlockSpec(memory_space=pltpu.VMEM),
        scratch_shapes=[pltpu.SemaphoreType.DMA((devices - 1,)), pltpu.SemaphoreType.DMA((devices - 1,))],
        compiler_params=pltpu.CompilerParams(
            collective_id=collective_id, has_side_effects=True, vmem_limit_bytes=4 * 2**20
        ),
    )(tile)
    return out[:, 0, : values.shape[0]]


def dot_plain(left, right):
    return jnp.dot(left, right, preferred_element_type=jnp.float32)


def dot_left(left, right):
    return lax.dot_general(
        left, right, (((0,), (0,)), ((), ())), preferred_element_type=jnp.float32
    )


def dot_right(left, right):
    return lax.dot_general(
        left, right, (((1,), (1,)), ((), ())), preferred_element_type=jnp.float32
    )


def normalize(values):
    centred = values - jnp.mean(values, -1, keepdims=True)
    inverse = lax.rsqrt(jnp.mean(centred * centred, -1, keepdims=True) + NORM_EPS)
    return (centred * inverse, inverse)


def norm_back(upstream, normed, inverse):
    return inverse * (
        upstream
        - jnp.mean(upstream, -1, keepdims=True)
        - normed * jnp.mean(upstream * normed, -1, keepdims=True)
    )


def local_grad(function, inputs, upstream):
    return jax.vjp(function, inputs)[1](upstream)[0]


def column_sum(values):
    return jnp.sum(values.astype(jnp.float32), 0)


def layer_forward(hidden, weights, gains, key_keep):
    w_qkv, w_out, w_up, w_down = weights
    first_norm, first_inv = normalize(hidden)
    normed = (first_norm * gains[0]).astype(jnp.bfloat16)
    packed = dot_plain(normed, w_qkv).astype(jnp.bfloat16)
    query_rows = packed[:, :D].reshape(SEQ, HEADS, HD)
    key_rows = packed[:, D : 2 * D].reshape(SEQ, HEADS, HD)
    value_rows = packed[:, 2 * D :].reshape(SEQ, HEADS, HD)
    scores = jnp.einsum(
        "qhd,khd->hqk", query_rows, key_rows, preferred_element_type=jnp.float32
    ) * HD ** (-0.5)
    if key_keep is not None:
        scores = jnp.where(key_keep[None, None, :] > 0, scores, -1e30)
    attention = jax.nn.softmax(scores, -1)
    attention_low = attention.astype(jnp.bfloat16)
    mixed_heads = (
        jnp.einsum("hqk,khd->qhd", attention_low, value_rows, preferred_element_type=jnp.float32)
        .reshape(-1, D)
        .astype(jnp.bfloat16)
    )
    middle = hidden + dot_plain(mixed_heads, w_out)
    second_norm, second_inv = normalize(middle)
    second = (second_norm * gains[1]).astype(jnp.bfloat16)
    inner_rows = dot_plain(second, w_up)
    upper_rows = jax.nn.gelu(inner_rows).astype(jnp.bfloat16)
    output = middle + dot_right(upper_rows, w_down)
    saved = (
        first_norm, first_inv, normed, query_rows, key_rows, value_rows, attention,
        attention_low, mixed_heads, second_norm, second_inv, second, inner_rows, upper_rows,
    )
    return (output, saved)


def layer_backward(upstream, weights, gains, saved):
    w_qkv, w_out, w_up, w_down = weights
    (
        first_norm, first_inv, normed, query_rows, key_rows, value_rows, attention,
        attention_low, mixed_heads, second_norm, second_inv, second, inner_rows, upper_rows,
    ) = saved
    back_branch = upstream.astype(jnp.bfloat16)
    back_upper = dot_plain(back_branch, w_down)
    back_inner = local_grad(jax.nn.gelu, inner_rows, back_upper).astype(jnp.bfloat16)
    back_second = dot_right(back_inner, w_up)
    grad_gain_two = jnp.sum(back_second * second_norm, 0)
    back_middle = upstream + norm_back(back_second * gains[1], second_norm, second_inv)
    back_attn_out = back_middle.astype(jnp.bfloat16)
    back_mixed = dot_right(back_attn_out, w_out).astype(jnp.bfloat16).reshape(SEQ, HEADS, HD)
    back_attention = jnp.einsum(
        "qhd,khd->hqk", back_mixed, value_rows, preferred_element_type=jnp.float32
    )
    back_values = jnp.einsum(
        "hqk,qhd->khd", attention_low, back_mixed, preferred_element_type=jnp.float32
    )
    back_scores = (
        attention * (back_attention - jnp.sum(back_attention * attention, -1, keepdims=True))
    ).astype(jnp.bfloat16)
    back_queries = jnp.einsum(
        "hqk,khd->qhd", back_scores, key_rows, preferred_element_type=jnp.float32
    ) * HD ** (-0.5)
    back_keys = jnp.einsum(
        "hqk,qhd->khd", back_scores, query_rows, preferred_element_type=jnp.float32
    ) * HD ** (-0.5)
    back_packed = jnp.concatenate(
        [back_queries.reshape(-1, D), back_keys.reshape(-1, D), back_values.reshape(-1, D)], 1
    ).astype(jnp.bfloat16)
    back_normed = dot_right(back_packed, w_qkv)
    grad_gain_one = jnp.sum(back_normed * first_norm, 0)
    back_hidden = back_middle + norm_back(back_normed * gains[0], first_norm, first_inv)
    pairs = [
        (normed, back_packed), (mixed_heads, back_attn_out), (second, back_inner), (back_branch, upper_rows)
    ]
    return (back_hidden, pairs, [grad_gain_one, grad_gain_two])


def head_pass(
    blocks, edges, biases, cond_rows, clean_rows, noise_rows, step_rows, weight_rows, weight_total
):
    cond_t, time_two_t, shift_t, scale_t, time_one_t, in_t, out_t = edges
    token_count = cond_rows.shape[0]
    extra = biases[HB]
    half_freq = FREQ // 2
    frequencies = jnp.exp(-math.log(10000.0) * jnp.arange(half_freq, dtype=jnp.float32) / half_freq)
    step_times = step_rows.astype(jnp.float32)
    angles = step_times.reshape(-1)[:, None] * frequencies
    time_embed = jnp.concatenate([jnp.cos(angles), jnp.sin(angles)], -1).astype(jnp.bfloat16)
    time_inner = dot_right(time_embed, time_one_t) + extra[:HW]
    time_hidden = jax.nn.silu(time_inner).astype(jnp.bfloat16)
    time_vector = dot_right(time_hidden, time_two_t) + extra[HW : 2 * HW]
    projected = dot_right(cond_rows, cond_t)
    conditioning = (projected[:, None, :] + time_vector.reshape(token_count, COPIES, HW)).reshape(
        -1, HW
    )
    silu_cond = jax.nn.silu(conditioning).astype(jnp.bfloat16)
    phase_angle = (step_times / TSTEPS + 0.008) / 1.008 * (math.pi / 2)
    keep_part = jnp.cos(phase_angle)[..., None]
    noise_part = jnp.sin(phase_angle)[..., None]
    clean_copies = clean_rows.astype(jnp.float32)[:, None, :]
    fresh_noise = noise_rows.astype(jnp.float32).reshape(token_count, COPIES, CH)
    noisy_rows = (
        (keep_part * clean_copies + noise_part * fresh_noise).reshape(-1, CH).astype(jnp.bfloat16)
    )
    target = (keep_part * fresh_noise - noise_part * clean_copies).reshape(-1, CH)
    stream = dot_right(noisy_rows, in_t) + extra[4 * HW :]
    saved = []
    for block_number in range(HB):
        w_mod, w_up, w_down = blocks[block_number]
        bias_row = biases[block_number]
        modulation = dot_plain(silu_cond, w_mod) + bias_row[: 3 * HW]
        normed, inverse = normalize(stream)
        shaped = (normed * (1.0 + modulation[:, HW : 2 * HW]) + modulation[:, :HW]).astype(
            jnp.bfloat16
        )
        inner_rows = dot_plain(shaped, w_up) + bias_row[3 * HW : 4 * HW]
        hidden = jax.nn.silu(inner_rows).astype(jnp.bfloat16)
        branch = dot_right(hidden, w_down) + bias_row[4 * HW :]
        saved.append((modulation, normed, inverse, shaped, inner_rows, hidden, branch))
        stream = stream + modulation[:, 2 * HW :] * branch
    final_shift = dot_right(silu_cond, shift_t) + extra[2 * HW : 3 * HW]
    final_scale = dot_right(silu_cond, scale_t) + extra[3 * HW : 4 * HW]
    final_norm, final_inv = normalize(stream)
    final_low = (final_norm * (1.0 + final_scale) + final_shift).astype(jnp.bfloat16)
    predicted = dot_plain(final_low, out_t)
    flat_weights = weight_rows.reshape(-1)
    errors = jnp.mean((predicted - target) ** 2, -1)
    loss_local = jnp.sum(flat_weights * errors)
    back_pred = (flat_weights[:, None] * 2.0 * (predicted - target) / (CH * weight_total)).astype(
        jnp.bfloat16
    )
    grad_out_t = dot_left(final_low, back_pred)
    back_final = dot_right(back_pred, out_t)
    back_shift = back_final.astype(jnp.bfloat16)
    back_scale = (back_final * final_norm).astype(jnp.bfloat16)
    back_silu = dot_plain(back_shift, shift_t) + dot_plain(back_scale, scale_t)
    back_stream = norm_back(back_final * (1.0 + final_scale), final_norm, final_inv)
    block_pairs = [None] * HB
    bias_grads = [None] * (HB + 1)
    for block_number in reversed(range(HB)):
        w_mod, w_up, w_down = blocks[block_number]
        modulation, normed, inverse, shaped, inner_rows, hidden, branch = saved[block_number]
        back_branch = (back_stream * modulation[:, 2 * HW :]).astype(jnp.bfloat16)
        back_gate = back_stream * branch
        back_hidden = dot_plain(back_branch, w_down)
        back_inner = local_grad(jax.nn.silu, inner_rows, back_hidden).astype(jnp.bfloat16)
        back_shaped = dot_right(back_inner, w_up)
        back_stream = back_stream + norm_back(
            back_shaped * (1.0 + modulation[:, HW : 2 * HW]), normed, inverse
        )
        back_modulation = jnp.concatenate([back_shaped, back_shaped * normed, back_gate], 1).astype(
            jnp.bfloat16
        )
        back_silu = back_silu + dot_right(back_modulation, w_mod)
        block_pairs[block_number] = [
            (silu_cond, back_modulation), (shaped, back_inner), (back_branch, hidden)
        ]
        bias_grads[block_number] = jnp.concatenate(
            [column_sum(back_modulation), column_sum(back_inner), column_sum(back_branch)]
        )
    back_stream_low = back_stream.astype(jnp.bfloat16)
    grad_in_t = dot_left(back_stream_low, noisy_rows)
    back_conditioning = local_grad(jax.nn.silu, conditioning, back_silu)
    back_time = back_conditioning.astype(jnp.bfloat16)
    back_time_hidden = dot_plain(back_time, time_two_t)
    back_time_inner = local_grad(jax.nn.silu, time_inner, back_time_hidden).astype(jnp.bfloat16)
    grad_time_one_t = dot_left(back_time_inner, time_embed)
    back_cond = back_conditioning.reshape(token_count, COPIES, HW).sum(1).astype(jnp.bfloat16)
    grad_cond_t = dot_left(back_cond, cond_rows)
    back_tokens = dot_plain(back_cond, cond_t)
    bias_grads[HB] = jnp.concatenate(
        [
            column_sum(back_time_inner), column_sum(back_time), column_sum(back_shift),
            column_sum(back_scale), column_sum(back_stream_low),
        ]
    )
    pairs = [pair for group in block_pairs for pair in group] + [
        (back_time, time_hidden), (back_shift, silu_cond), (back_scale, silu_cond)
    ]
    small = (grad_cond_t, grad_time_one_t, grad_in_t, grad_out_t)
    return (loss_local, pairs, small, jnp.stack(bias_grads), back_tokens)


def adamw(master, first, second, gradient, factor, step_rate):
    clipped = gradient * factor
    first_new = BETA_ONE * first + (1.0 - BETA_ONE) * clipped
    second_new = BETA_TWO * second + (1.0 - BETA_TWO) * clipped * clipped
    mean_hat = first_new / (1.0 - BETA_ONE**ADAM_STEP)
    var_hat = second_new / (1.0 - BETA_TWO**ADAM_STEP)
    updated = master - step_rate * (mean_hat / (jnp.sqrt(var_hat) + ADAM_EPS) + DECAY_RATE * master)
    return (updated, first_new, second_new)


TRUNK_PARTS = (3 * D, D, FF, FF)
HEAD_PARTS = (3 * HW, HW, HW)
EDGE_PARTS = (D, HW, HW, HW, FREQ, 128)
TRUNK_WIDTH = 768
HEAD_WIDTH = 512


def gather_plan(part_sets, edge_parts, limit):
    chunks, widths = [], []
    for index, parts in enumerate(part_sets):
        column = 0
        for part in parts:
            for k in range(0, part, limit):
                chunks.append((0, index, column + k, len(widths), k, min(limit, part - k)))
            widths.append(part)
            column += part
    edge_chunks, column = [], 0
    for part in edge_parts:
        for k in range(0, part, limit):
            edge_chunks.append((1, None, column + k, len(widths), k, min(limit, part - k)))
        widths.append(part)
        column += part
    return edge_chunks + chunks, widths


def plain_gather(sources, chunks, widths):
    ends = {}
    for source, index, column, result, at, width in chunks:
        start, stop = ends.get(result, (source, index, column, column))[2:]
        ends[result] = (source, index, min(start, column), max(stop, column + width))
    wholes = {}
    results = []
    for number in range(len(widths)):
        source, index, start, stop = ends[number]
        if (source, index) not in wholes:
            block = sources[source] if index is None else sources[source][index]
            wholes[source, index] = lax.all_gather(block, AXES, axis=0, tiled=True)
        results.append(wholes[source, index][:, start:stop])
    return results


def scatter_sum(values):
    low = lax.psum_scatter(values, "dp", scatter_dimension=0, tiled=True)
    return lax.psum_scatter(low, "fsdp", scatter_dimension=0, tiled=True)


def on_device(
    mesh_shape,
    latents, orders, mask_counts, noise, timesteps, loss_weights,
    block_weights, block_gains, entry_table, head_weights, head_biases, head_edges,
    first_blocks, first_gains, first_entry, first_head, first_biases, first_edges,
    second_blocks, second_gains, second_entry, second_head, second_biases, second_edges,
):
    dp_count, nz = mesh_shape["dp"], mesh_shape["fsdp"]
    devices = dp_count * nz
    me = lax.axis_index("dp") * nz + lax.axis_index("fsdp")
    r0, r1 = D // devices, HW // devices
    direct = dp_count == 8 and nz > 1 and (D // 8) % 16 == 0
    bf = jnp.bfloat16

    low_blocks = block_weights.astype(bf)
    low_entry = jnp.concatenate(
        [entry_table.T.astype(bf), block_gains.reshape(4, r0).T.astype(bf), jnp.zeros((r0, 108), bf)], 1
    )
    low_head = head_weights.astype(bf)
    edge = head_edges.T.astype(bf)
    base = D + 2 * CH
    low_edges = jnp.concatenate(
        [
            edge[:, :D], edge[:, base + FREQ :], edge[:, base : base + FREQ], edge[:, D:base],
            head_biases.reshape((HB + 1) * 5, r1).T.astype(bf), jnp.zeros((r1, 81), bf),
        ],
        1,
    )
    trunk_chunks, trunk_widths = gather_plan([TRUNK_PARTS] * 2, (TRUNK_WIDTH,), TRUNK_WIDTH)
    head_chunks, head_widths = gather_plan([HEAD_PARTS] * HB, EDGE_PARTS, HEAD_WIDTH)
    if direct:
        trunk = [
            a.reshape(D, -1) for a in gather_rows([low_blocks, low_entry], trunk_chunks, trunk_widths, r0, nz, 1)
        ]
    else:
        trunk = plain_gather([low_blocks, low_entry], trunk_chunks, trunk_widths)
    if direct and HEAD_DIRECT:
        head = [
            a.reshape(HW, -1) for a in gather_rows([low_head, low_edges], head_chunks, head_widths, r1, nz, 2)
        ]
    else:
        head = plain_gather([low_head, low_edges], head_chunks, head_widths)

    local_total = jnp.sum(mask_counts)
    early = exchange(
        jnp.stack([local_total.astype(jnp.float32), jnp.sum(loss_weights)]), dp_count, nz, 3
    )
    counts = early[:, 0].astype(jnp.int32)
    weight_total = jnp.sum(early[:, 1])
    count_ends = jnp.cumsum(counts)
    count_starts = count_ends - counts
    offset = jnp.sum(jnp.where(jnp.arange(devices) == me, count_starts, 0))

    order_row = orders[0]
    clean = latents[0]
    ids = jnp.arange(LAT, dtype=jnp.int32)
    masked = jnp.any((order_row[:, None] == ids[None, :]) & (ids < local_total)[:, None], 0)
    key_keep = jnp.concatenate([jnp.ones((BUF,), jnp.float32), 1.0 - masked.astype(jnp.float32)])
    layers = (trunk[:4], trunk[4:8])
    entry = trunk[8].T
    entry_rows = entry[: 2 * SEQ].astype(jnp.float32)
    gain_rows = entry[2 * SEQ + CH : 2 * SEQ + CH + 4].astype(jnp.float32)
    projected = dot_plain(clean, entry[2 * SEQ : 2 * SEQ + CH])
    start_rows = entry_rows[:SEQ] + jnp.concatenate([jnp.zeros((BUF, D), jnp.float32), projected], 0)
    encoded, encoder_saved = layer_forward(start_rows, layers[0], gain_rows[:2], key_keep)
    decoder_input = encoded * key_keep[:, None] + entry_rows[SEQ : 2 * SEQ]
    top_rows, decoder_saved = layer_forward(decoder_input, layers[1], gain_rows[2:], None)

    capacity = (LAT + devices - 1) // devices
    slots = devices * capacity
    slot_ids = jnp.arange(slots, dtype=jnp.int32)
    slot_token = jnp.mod(slot_ids // capacity - offset, devices) + devices * (slot_ids % capacity)
    slot_position = jnp.sum(
        jnp.where(slot_token[:, None] == ids[None, :], order_row[None, :], 0), 1
    )
    pick = (
        (slot_position[:, None] == ids[None, :]) & (slot_token < local_total)[:, None]
    ).astype(bf)
    outgoing = dot_plain(
        pick, jnp.concatenate([top_rows[BUF:].astype(bf), clean, jnp.zeros((LAT, 112), bf)], 1)
    ).astype(bf)
    incoming = lax.all_to_all(
        outgoing.reshape(devices, capacity, -1), AXES, split_axis=0, concat_axis=0, tiled=True
    ).reshape(slots, -1)
    head_rows = noise.shape[0]
    token_ids = jnp.arange(head_rows, dtype=jnp.int32) * devices + me
    inside = (token_ids[:, None] >= count_starts[None, :]) & (token_ids[:, None] < count_ends[None, :])
    first_token = count_starts + jnp.mod(me - count_starts, devices)
    source_slot = (
        jnp.arange(devices, dtype=jnp.int32)[None, :] * capacity
        + (token_ids[:, None] - first_token[None, :]) // devices
    )
    row_slot = jnp.sum(jnp.where(inside, source_slot, 0), 1)
    place = (row_slot[:, None] == slot_ids[None, :]).astype(bf)
    received = dot_plain(place, incoming).astype(bf)

    head_blocks = [head[3 * b : 3 * b + 3] for b in range(HB)]
    edge_mats = head[3 * HB :]
    misc = edge_mats[5]
    biases = (
        misc[:, 2 * CH : 2 * CH + 5 * (HB + 1)]
        .reshape(devices, r1, HB + 1, 5)
        .transpose(2, 0, 3, 1)
        .reshape(HB + 1, 5 * HW)
        .astype(jnp.float32)
    )
    loss_local, head_pairs, small, bias_grad, back_tokens = head_pass(
        head_blocks,
        edge_mats[:5] + [misc[:, :CH], misc[:, CH : 2 * CH]],
        biases,
        received[:, :D],
        received[:, D : D + CH],
        noise,
        timesteps,
        loss_weights,
        weight_total,
    )
    grad_cond_t, grad_time_one_t, grad_in_t, grad_out_t = small
    bias_t = (
        bias_grad.reshape(HB + 1, devices, 5, r1).transpose(1, 3, 0, 2).reshape(HW, 5 * (HB + 1))
    )
    head_small = jnp.concatenate(
        [grad_cond_t, grad_time_one_t, grad_in_t, grad_out_t, bias_t, jnp.zeros((HW, 465), jnp.float32)], 1
    ).astype(bf)
    small_columns = head_small.shape[1]
    if direct:
        extras = jnp.stack(
            [head_small[:, k : k + HEAD_WIDTH] for k in range(0, small_columns, HEAD_WIDTH)]
        )
        tall = reduce_products(head_pairs, extras, HW, HEAD_WIDTH, (r1, HEAD_WIDTH), nz, 4)
        tall = tall.transpose(1, 0, 2).reshape(r1, -1)
    else:
        tall = jnp.concatenate(
            [scatter_sum(dot_left(x, y)) for x, y in head_pairs]
            + [scatter_sum(head_small.astype(jnp.float32))],
            1,
        )

    returning = dot_left(place, back_tokens.astype(bf)).astype(bf)
    returned = lax.all_to_all(
        returning.reshape(devices, capacity, D), AXES, split_axis=0, concat_axis=0, tiled=True
    ).reshape(slots, D)
    back_top = jnp.concatenate([jnp.zeros((BUF, D), jnp.float32), dot_left(pick, returned)], 0)
    back_decoder, decoder_pairs, decoder_gains = layer_backward(
        back_top, layers[1], gain_rows[2:], decoder_saved
    )
    back_encoded = back_decoder * key_keep[:, None]
    back_start, encoder_pairs, encoder_gains = layer_backward(
        back_encoded, layers[0], gain_rows[:2], encoder_saved
    )
    grad_input_t = dot_left(back_start[BUF:].astype(bf), clean)
    trunk_small = jnp.concatenate(
        [
            back_start.T, back_decoder.T, grad_input_t,
            jnp.stack(encoder_gains + decoder_gains, 1), jnp.zeros((D, 108), jnp.float32),
        ],
        1,
    ).astype(bf)
    trunk_pairs = encoder_pairs + decoder_pairs
    if direct:
        wide = reduce_products(
            trunk_pairs, trunk_small[None], D, TRUNK_WIDTH, (2 * r0, TRUNK_WIDTH // 2), nz, 5
        )
        wide = wide.transpose(1, 0, 2).reshape(r0, -1)
    else:
        wide = jnp.concatenate(
            [scatter_sum(dot_left(x, y)) for x, y in trunk_pairs]
            + [scatter_sum(trunk_small.astype(jnp.float32))],
            1,
        )
    block_columns, head_columns = sum(TRUNK_PARTS), sum(HEAD_PARTS)
    block_grad = jnp.stack([wide[:, l * block_columns : (l + 1) * block_columns] for l in range(2)])
    rest = wide[:, 2 * block_columns :]
    entry_grad = rest[:, : 2 * SEQ + CH].T
    gain_grad = rest[:, 2 * SEQ + CH : 2 * SEQ + CH + 4].T.reshape(2, 2, r0)
    head_grad = jnp.stack([tall[:, b * head_columns : (b + 1) * head_columns] for b in range(HB)])
    rest = tall[:, HB * head_columns :]
    shared = rest[:, 3 * HW :]
    edge_grad = jnp.concatenate(
        [
            shared[:, :D], shared[:, D + FREQ : D + FREQ + 2 * CH], shared[:, D : D + FREQ],
            rest[:, : 3 * HW],
        ],
        1,
    ).T
    bias_grad = (
        shared[:, D + FREQ + 2 * CH : D + FREQ + 2 * CH + 5 * (HB + 1)].T.reshape(HB + 1, 5 * r1)
    )
    squares = jnp.sum(wide * wide) + jnp.sum(tall * tall)
    late = exchange(jnp.stack([loss_local, squares]), dp_count, nz, 6)
    loss_sum = jnp.sum(late[:, 0])
    grad_norm = jnp.sqrt(jnp.sum(late[:, 1]))
    factor = CLIP_NORM / jnp.maximum(grad_norm, CLIP_NORM)
    new = [
        adamw(block_weights, first_blocks, second_blocks, block_grad, factor, LEARN_RATE),
        adamw(block_gains, first_gains, second_gains, gain_grad, factor, GAIN_RATE),
        adamw(entry_table, first_entry, second_entry, entry_grad, factor, LEARN_RATE),
        adamw(head_weights, first_head, second_head, head_grad, factor, LEARN_RATE),
        adamw(head_biases, first_biases, second_biases, bias_grad, factor, LEARN_RATE),
        adamw(head_edges, first_edges, second_edges, edge_grad, factor, LEARN_RATE),
    ]
    return tuple(new[i][k] for k in range(3) for i in range(6)) + (loss_sum, weight_total, grad_norm)


def solution(mesh):
    rows = [P(AXES, None, None), P(AXES, None), P(AXES), P(AXES, None), P(AXES, None), P(AXES, None)]
    state = [
        P(None, AXES, None), P(None, None, AXES), P(None, AXES),
        P(None, AXES, None), P(None, AXES), P(None, AXES),
    ]
    return jax.shard_map(
        functools.partial(on_device, dict(mesh.shape)),
        mesh=mesh,
        in_specs=tuple(rows + state * 3),
        out_specs=tuple(state * 3 + [P(), P(), P()]),
        check_vma=False,
    )
```

time: 2610 us -> 927 us (0.36)
  waiting for transfers between devices: 1450 us -> 10.5 us
  Pallas kernels: 0 us -> 486 us
  blocking collectives: 404 us -> 0 us
  other arithmetic: 206 us -> 72.2 us
  matrix products: 317 us -> 231 us
  local copies, waits for them, and re-layouts: 159 us -> 83.6 us
    reduce_scatter x2 -> x0, waiting for transfers between devices: 1360 us -> none  [the longest x1 883 us: on_device(): lax.psum_scatter(grad_head, ('dp', 'fsdp'), scatter_dimension=1, tiled=True)]
    pallas_call x0 -> x5, Pallas kernels: none -> 486 us  [the longest x2 288 us: reduce_products(): pl.pallas_call(functools.partial(rs_kernel, nz, row_count, width, jobs, e...]
    all_gather x3 -> x0, blocking collectives: 236 us -> none  [the longest x1 97 us: on_device(): lax.all_gather(low_entry, ('dp', 'fsdp'), axis=1, tiled=True)]
    another operation x13 -> x12, other arithmetic: 129 us -> 9.13 us  [the longest x3 76 us: on_device(): grad_blocks = jnp.stack([grad_encoder_block, grad_decoder_block])]
    unnamed x11 -> x3, waiting for transfers between devices: 88.6 us -> 0.71 us
    unnamed x2 -> x0, blocking collectives: 86.3 us -> none
    psum x2 -> x0, blocking collectives: 81.8 us -> none  [the longest x1 41 us: on_device(): weight_total = lax.psum(jnp.sum(loss_weights), ('dp', 'fsdp'))]
    dot_general x21 -> x7, matrix products: 90.3 us -> 10.2 us  [dot_left(): lax.dot_general(left, right, (((0,), (0,)), ((), ())), preferred_element_...]
  transfers between devices with their start and end apart: 12 -> 5, of which waited for: 5 -> 2; matrix products, arithmetic and copies ran while one was open for 19% -> 13% of each run, Pallas kernels for 0% -> 21%
where the time goes in v1:
time: 927 us; the launch traced here: 915 us
  Pallas kernels  486 us (52%)
  matrix products  231 us (25%)
  local copies, waits for them, and re-layouts  83.6 us (9%)
  other arithmetic  72.2 us (8%)
  between operations  21.4 us (2%)
  starting transfers between devices  11.1 us (1%)
  waiting for transfers between devices  10.5 us (1%)
    pallas_call x2, Pallas kernels, reduce_products(): pl.pallas_call(functools.partial(rs_kernel, nz, row_count, width, jobs, e...  288 us
    pallas_call x1, Pallas kernels, gather_rows(): pl.pallas_call(functools.partial(ag_kernel, nz, chunks, len(sources)), ou...  173 us
    dot_general x21, matrix products, dot_plain(): return jnp.dot(left, right, preferred_element_type=jnp.float32)  93.2 us
    dot_general x21, matrix products, dot_right(): lax.dot_general(left, right, (((1,), (1,)), ((), ())), preferred_element_...  90.5 us
    pallas_call x2, Pallas kernels, exchange(): pl.pallas_call(functools.partial(exchange_kernel, dp_count, nz), out_shap...  24.6 us
    unnamed x414, local copies, waits for them, and re-layouts  19.9 us
  transfers between devices with their start and end apart: 5, of which 2 were waited for; matrix products, arithmetic and copies ran while one was open for 13% of the time, Pallas kernels for 21%

profile of v1, /device:TPU:0, one launch (start us, length us, event | category | flops | bytes accessed | tf_op | source)
XLA Modules:
  0.0 915.2 jit_solution(13818445974514399722)
XLA Ops:
  13.9 173.3 %shard_map.391 = (bf16[2,2,2,4,24,2304]{5,4,3,2,1,0:T(8,128)(2,1)S(1)}, bf16[2,2,2,4,24,768]{5,4,3,2,1,0:T(8,128)(2,1)S(1)}, bf16[2,2,2,4,24,3072]{5,4,3,2,1,0:T...) custom-call(bf16[2,24,9216]{2,1,0:T(8,128)(2,1)S(1)} %convert_elemen, ...), custom_call_target="tpu_custom_call" | custom-call | tf_op jit(solution)/shard_map/pallas_call | solution.py:381
  207.2 6.2 fusion.241
  231.5 14.8 %shard_map.392 = f32[32,8,128]{2,1,0:T(8,128)S(1)} custom-call(f32[8,128]{1,0:T(8,128)S(1)} %broadcast_in_dim.46.in_ref), custom_call_target="tpu_custom_call" | custom-call | tf_op jit(solution)/shard_map/pallas_call | solution.py:436
  268.3 5.6 all-to-all-start
  304.7 6.0 multiply_convert_fusion.13
  316.4 8.0 fusion.11
  325.3 7.2 multiply_convert_fusion.12
  332.5 6.0 fusion.234
  339.0 8.0 fusion.14
  347.8 5.9 multiply_convert_fusion.11
  369.1 5.7 fusion.228
  374.8 7.4 fusion.247
  382.3 6.9 fusion.214
  392.2 6.9 fusion.248
  399.1 6.4 fusion.215
  413.9 6.7 fusion.2
  431.0 10.7 %fusion.230 = (bf16[1024]{0:T(1024)(128)(2,1)S(1)}, bf16[768,1024]{1,0:T(8,128)(2,1)}, f32[768,1024]{1,0:T(8,128)}) fusion(f32[768,1024]{1,0:T(8,128)} %get-tuple-element.171, bf16[768,3072]{1,0:T(8,128)(2,1)S(1)} %get-tuple-element.82.refs_9_, bf16[1024,5120]{1,0:T(8,128)(2,1)S(1)} %bitcast.329, f32[768,1024]{1,0:T(8,128)} %fusion.2, ...), kind=kOutput, calls=%fused_computation.431 | convolution fusion | flops 4842847232 | bytes 28313600 | tf_op jit(solution)/shard_map/dot_general | solution.py:460
  446.9 6.9 fusion.246
  472.2 145.6 %shard_map.394 = f32[29,32,512]{2,1,0:T(8,128)} custom-call(bf16[768,1024]{1,0:T(8,128)(2,1)} %copy-done.25, bf16[768,1024]{1,0:T(8,128)(2,1)} %copy-done.51, bf16[768,1024]{1,0:T(8,128)(2,1)} %copy-done.50, bf16[768,1024]{1,0:T(8,128)(2,1)} %copy-done.25, bf16[768,1024]{1,0:T(8,128)(2,1)} %copy-done.45, bf16[768,1024]{1,0:T(8,128)(2,1)} %copy-done.48, ...), custom_call_target="tpu_custom_call" | custom-call | tf_op jit(solution)/shard_map/pallas_call | solution.py:276
  632.9 8.6 all-to-all-done.1
  642.3 7.9 fusion.33.refs_14_
  683.0 7.8 fusion.26.refs_10_
  728.8 142.2 %shard_map.393 = f32[25,24,768]{2,1,0:T(8,128)} custom-call(bf16[320,768]{1,0:T(8,128)(2,1)} %copy.397.refs_0_, bf16[320,768]{1,0:T(8,128)(2,1)} %copy.398.refs_1_, bf16[320,768]{1,0:T(8,128)(2,1)} %copy.399.refs_2_, bf16[320,768]{1,0:T(8,128)(2,1)} %copy.400.refs_3_, bf16[320,768]{1,0:T(8,128)(2,1)} %copy.401.refs_4_, bf16[320,768]{1,0:T(8,128)(2,1)} %copy.402.refs_5_, ...), custom_call_target="tpu_custom_call" | custom-call | tf_op jit(solution)/shard_map/pallas_call | solution.py:276
  875.8 9.8 %shard_map.395 = f32[32,8,128]{2,1,0:T(8,128)S(1)} custom-call(f32[8,128]{1,0:T(8,128)S(1)} %broadcast_in_dim.55.in_ref), custom_call_target="tpu_custom_call" | custom-call | tf_op jit(solution)/shard_map/pallas_call | solution.py:436
  (692 shorter events, 273.4 us)
Async XLA Ops:
  7.2 282.4 %all-gather.6.cloned.1.call-start = ((), (), s32[]{:S(2)}) async-start(), calls=%async_computation.2 | async-start | bytes 8921088 | tf_op jit(solution)/shard_map/all_gather | solution.py:713
  10.4 305.9 %all-gather.8.cloned.1.call-start = ((), (), s32[]{:S(2)}) async-start(), calls=%async_computation.3 | async-start | bytes 10813440 | tf_op jit(solution)/shard_map/all_gather | solution.py:713
  12.7 326.3 %all-gather.10.cloned.1.call-start = ((), (), s32[]{:S(2)}) async-start(), calls=%async_computation.4 | async-start | bytes 10813440 | tf_op jit(solution)/shard_map/all_gather | solution.py:713
  13.5 180.1 %copy-start.132 = (bf16[1,256,16]{1,2,0:T(8,128)(2,1)S(1)}, bf16[1,256,16]{1,2,0:T(8,128)(2,1)}, u32[]{:S(2)}) copy-start(bf16[1,256,16]{1,2,0:T(8,128)(2,1)} %param.24) | copy-start | bytes 24580
  193.3 23.8 %copy-start = (bf16[2,2,2,4,24,768]{5,4,3,2,1,0:T(8,128)(2,1)}, bf16[2,2,2,4,24,768]{5,4,3,2,1,0:T(8,128)(2,1)S(1)}, u32[]{:S(2)}) copy-start(bf16[2,2,2,4,24,768]{5,4,3,2,1,0:T(8,128)(2,1)S(1)} %get-tuple-element.32) | copy-start | bytes 3538948
  193.3 64.2 %copy-start.2 = (bf16[2,2,2,4,24,768]{5,4,3,2,1,0:T(8,128)(2,1)}, bf16[2,2,2,4,24,768]{5,4,3,2,1,0:T(8,128)(2,1)S(1)}, u32[]{:S(2)}) copy-start(bf16[2,2,2,4,24,768]{5,4,3,2,1,0:T(8,128)(2,1)S(1)} %get-tuple-element.36) | copy-start | bytes 3538948
  194.6 23.6 %copy-start.129 = (f32[768]{0:T(1024)}, f32[768]{0:T(1024)S(1)}, u32[]{:S(2)}) copy-start(f32[768]{0:T(1024)S(1)} %get-tuple-element.59) | copy-start | bytes 9220
  194.6 31.9 %copy-start.122 = (f32[768]{0:T(1024)}, f32[768]{0:T(1024)S(1)}, u32[]{:S(2)}) copy-start(f32[768]{0:T(1024)S(1)} %get-tuple-element.58) | copy-start | bytes 9220
  194.6 64.0 %copy-start.116 = (f32[768]{0:T(1024)}, f32[768]{0:T(1024)S(1)}, u32[]{:S(2)}) copy-start(f32[768]{0:T(1024)S(1)} %get-tuple-element.57) | copy-start | bytes 9220
  207.2 15.9 %copy-start.158 = (f32[320]{0:T(512)}, f32[320]{0:T(512)S(1)}, u32[]{:S(2)}) copy-start(f32[320]{0:T(512)S(1)} %concatenate.90) | copy-start | bytes 3844
  229.7 24.0 %copy-start.79 = (bf16[320,768]{0,1:T(8,128)(2,1)}, bf16[320,768]{0,1:T(8,128)(2,1)S(1)}, u32[]{:S(2)}) copy-start(bf16[320,768]{0,1:T(8,128)(2,1)S(1)} %copy.354) | copy-start | bytes 1474564
  230.0 23.7 %copy-start.81 = (bf16[320,768]{0,1:T(8,128)(2,1)}, bf16[320,768]{0,1:T(8,128)(2,1)S(1)}, u32[]{:S(2)}) copy-start(bf16[320,768]{0,1:T(8,128)(2,1)S(1)} %copy.355) | copy-start | bytes 1474564
  248.6 18.5 %copy-start.177 = (pred[256]{0:T(512)(128)(4,1)}, pred[256]{0:T(512)(128)(4,1)S(1)}, u32[]{:S(2)}) copy-start(pred[256]{0:T(512)(128)(4,1)S(1)} %broadcast_compare_fusion.1) | copy-start | bytes 772
  249.4 17.6 %copy-start.164 = (s32[256]{0:T(256)}, s32[256]{0:T(256)S(1)}, u32[]{:S(2)}) copy-start(s32[256]{0:T(256)S(1)} %select_reduce_fusion) | copy-start | bytes 3076
  268.3 20.7 %all-to-all-start = ((bf16[32,8,896]{2,1,0:T(8,128)(2,1)}), bf16[32,8,896]{2,1,0:T(8,128)(2,1)S(1)}, u32[]{:S(2)}, u32[]{:S(2)}) async-start(bf16[32,8,896]{2,1,0:T(8,128)(2,1)} %fusion.128), calls=%async_computation | async-start | bytes 917504 | tf_op jit(solution)/shard_map/all_to_all | solution.py:804
  299.7 24.7 %copy-start.13 = (f32[768,1024]{1,0:T(8,128)}, f32[768,1024]{1,0:T(8,128)S(1)}, u32[]{:S(2)}) copy-start(f32[768,1024]{1,0:T(8,128)S(1)} %get-tuple-element.173) | copy-start | bytes 9437188
  369.1 20.1 %slice-start.12 = ((s8[9437184]{0:T(1024)(128)(4,1)}), s8[4194304]{0:T(1024)(128)(4,1)S(1)}, s32[]{:S(2)}) async-start(s8[9437184]{0:T(1024)(128)(4,1)} %bitcast.268), calls=%async_computation.17 | async-start | bytes 8388608
  374.8 51.0 %copy-start.47 = (bf16[768,1024]{1,0:T(8,128)(2,1)}, bf16[768,1024]{1,0:T(8,128)(2,1)S(1)}, u32[]{:S(2)}) copy-start(bf16[768,1024]{1,0:T(8,128)(2,1)S(1)} %get-tuple-element.94.refs_8_) | copy-start | bytes 4718596
  413.8 17.2 %copy-start.27 = (bf16[768,3072]{1,0:T(8,128)(2,1)}, bf16[768,3072]{1,0:T(8,128)(2,1)S(1)}, u32[]{:S(2)}) copy-start(bf16[768,3072]{1,0:T(8,128)(2,1)S(1)} %get-tuple-element.82.refs_9_) | copy-start | bytes 14155780
  624.5 17.0 %copy-start.165 = (s32[256]{0:T(256)S(1)}, s32[256]{0:T(256)}, u32[]{:S(2)}) copy-start(s32[256]{0:T(256)} %copy-done.164) | copy-start | bytes 3076
  624.5 17.0 %copy-start.178 = (pred[256]{0:T(512)(128)(4,1)S(1)}, pred[256]{0:T(512)(128)(4,1)}, u32[]{:S(2)}) copy-start(pred[256]{0:T(512)(128)(4,1)} %copy-done.177) | copy-start | bytes 772
  624.5 17.0 %all-to-all-start.1 = ((bf16[32,8,768]{2,1,0:T(8,128)(2,1)}), bf16[32,8,768]{2,1,0:T(8,128)(2,1)S(1)}, u32[]{:S(2)}, u32[]{:S(2)}) async-start(bf16[32,8,768]{2,1,0:T(8,128)(2,1)} %fusion.132), calls=%async_computation.1 | async-start | bytes 786432 | tf_op jit(solution)/shard_map/all_to_all | solution.py:862
  630.7 19.4 %slice-start.8 = ((s8[4718592]{0:T(1024)(128)(4,1)}), s8[524288]{0:T(1024)(128)(4,1)S(1)}, s32[]{:S(2)}) async-start(s8[4718592]{0:T(1024)(128)(4,1)} %bitcast.257), calls=%async_computation.13 | async-start | bytes 1048576
  871.0 16.1 %copy-start.35 = (f32[25,24,768]{2,1,0:T(8,128)S(1)}, f32[25,24,768]{2,1,0:T(8,128)}, u32[]{:S(2)}) copy-start(f32[25,24,768]{2,1,0:T(8,128)} %shard_map.393) | copy-start | bytes 5529604
  (185 other events, 947.6 us)
Sparse Core Ops, SparseCore 0:
  10.8 122.7 all-gather.5
  136.5 94.9 all-gather.7
  234.3 87.7 all-gather.9

commit v2 on v1

--- a/solution.py
+++ b/solution.py
@@ -32,7 +32,6 @@
 CLIP_NORM = 0.002
 NORM_EPS = 1e-06
 AXES = ("dp", "fsdp")
-HEAD_DIRECT = False
 MESH_IDS = pl.DeviceIdType.MESH
 
 
@@ -375,14 +374,14 @@
         across(k).wait_recv()
 
 
-def gather_rows(sources, chunks, widths, rows, nz, collective_id):
+def gather_rows(sources, chunks, shapes, nz, collective_id):
     dma = pltpu.SemaphoreType.DMA
     total = len(chunks)
     return pl.pallas_call(
         functools.partial(ag_kernel, nz, chunks, len(sources)),
-        out_shape=[jax.ShapeDtypeStruct((2, 2, 2, nz, rows, width), jnp.bfloat16) for width in widths],
+        out_shape=[jax.ShapeDtypeStruct((2, 2, 2, nz, *shape), jnp.bfloat16) for shape in shapes],
         in_specs=[pl.BlockSpec(memory_space=pl.ANY)] * len(sources),
-        out_specs=[pl.BlockSpec(memory_space=pl.ANY)] * len(widths),
+        out_specs=[pl.BlockSpec(memory_space=pl.ANY)] * len(shapes),
         scratch_shapes=[
             dma((total,)), dma((total, nz - 1)), dma((total, nz - 1)),
             dma((total,)), dma((total,)), dma((total,)), dma((total,)), dma((total,)), dma((total,)),
@@ -462,206 +461,680 @@
     )
 
 
-def normalize(values):
-    centred = values - jnp.mean(values, -1, keepdims=True)
-    inverse = lax.rsqrt(jnp.mean(centred * centred, -1, keepdims=True) + NORM_EPS)
-    return (centred * inverse, inverse)
-
-
-def norm_back(upstream, normed, inverse):
-    return inverse * (
-        upstream
-        - jnp.mean(upstream, -1, keepdims=True)
-        - normed * jnp.mean(upstream * normed, -1, keepdims=True)
-    )
-
-
-def local_grad(function, inputs, upstream):
-    return jax.vjp(function, inputs)[1](upstream)[0]
-
-
-def column_sum(values):
-    return jnp.sum(values.astype(jnp.float32), 0)
-
-
-def layer_forward(hidden, weights, gains, key_keep):
+KEPT = (
+    ("normed", D, jnp.bfloat16), ("packed", 3 * D, jnp.bfloat16), ("mixed", D, jnp.bfloat16),
+    ("second", D, jnp.bfloat16), ("upper", FF, jnp.bfloat16), ("inner", FF, jnp.float32),
+    ("norm_one", D, jnp.float32), ("norm_two", D, jnp.float32), ("inv_one", 128, jnp.float32),
+    ("inv_two", 128, jnp.float32),
+)
+KEPT_INDEX = {name: k for k, (name, _, _) in enumerate(KEPT)}
+BACK = (("back_packed", 3 * D), ("back_attn", D), ("back_inner", FF), ("back_branch", D))
+GELU_SCALE = math.sqrt(2.0 / math.pi)
+
+
+def in_nn(x, w):
+    return jnp.dot(x, w, preferred_element_type=jnp.float32)
+
+
+def in_nt(x, w):
+    return lax.dot_general(x, w, (((1,), (1,)), ((), ())), preferred_element_type=jnp.float32)
+
+
+def in_tn(x, w):
+    return lax.dot_general(x, w, (((0,), (0,)), ((), ())), preferred_element_type=jnp.float32)
+
+
+def softmax_rows(scores):
+    raised = jnp.exp(scores - jnp.max(scores, -1, keepdims=True))
+    return raised * (1.0 / jnp.sum(raised, -1, keepdims=True))
+
+
+def low_half():
+    return lax.broadcasted_iota(jnp.int32, (SEQ, 2 * HD), 1) < HD
+
+
+def forward_pieces(weights, entry, select_ref, mask_ref, hidden, kept, top_ref, need, leave):
+    bf = jnp.bfloat16
+    pieces = []
+    gain = lambda row: in_nt(select_ref[2 * SEQ :, :], entry[...])[row : row + 1, :]
+
+    def start():
+        need(entry)
+        hidden[...] = in_nt(select_ref[:SEQ, :], entry[...])
+    pieces.append(start)
+
+    def norm(layer, which):
+        value = hidden[...]
+        centred = value - jnp.mean(value, -1, keepdims=True)
+        inv = lax.rsqrt(jnp.mean(centred * centred, -1, keepdims=True) + NORM_EPS)
+        n = centred * inv
+        names = ("norm_one", "inv_one", "normed") if which == 0 else ("norm_two", "inv_two", "second")
+        kept[names[0]][layer] = n
+        kept[names[1]][layer] = jnp.broadcast_to(inv, (SEQ, 128))
+        kept[names[2]][layer] = (n * gain(2 * layer + which)).astype(bf)
+        for name in names:
+            leave(layer, name)
+
+    def project(layer):
+        norm(layer, 0)
+        need(weights[4 * layer])
+        kept["packed"][layer] = in_nn(kept["normed"][layer], weights[4 * layer][...]).astype(bf)
+        leave(layer, "packed")
+
+    def attend(layer, pair):
+        packed = kept["packed"]
+        cut = lambda k: packed[layer, :, k * D + pair * 2 * HD : k * D + (pair + 1) * 2 * HD]
+        q, k, v = cut(0), cut(1), cut(2)
+        low = low_half()
+        parts = []
+        for side in range(2):
+            one = jnp.where(low if side == 0 else ~low, q, jnp.zeros((), bf))
+            scores = in_nt(one, k) * HD ** (-0.5)
+            if layer == 0:
+                scores = jnp.where(mask_ref[...] > 0, scores, -1e30)
+            parts.append(in_nn(softmax_rows(scores).astype(bf), v))
+        kept["mixed"][layer, :, pair * 2 * HD : (pair + 1) * 2 * HD] = jnp.where(low, parts[0], parts[1]).astype(bf)
+
+    def close(layer):
+        leave(layer, "mixed")
+        need(weights[4 * layer + 1])
+        hidden[...] += in_nn(kept["mixed"][layer], weights[4 * layer + 1][...])
+        norm(layer, 1)
+        need(weights[4 * layer + 2])
+
+    def up(layer, part, parts):
+        columns = slice(part * FF // parts, (part + 1) * FF // parts)
+        inner = in_nn(kept["second"][layer], weights[4 * layer + 2][:, columns])
+        kept["inner"][layer, :, columns] = inner
+        kept["upper"][layer, :, columns] = (
+            0.5 * inner * (1.0 + jnp.tanh(GELU_SCALE * (inner + 0.044715 * inner * inner * inner)))
+        ).astype(bf)
+
+    def down(layer):
+        leave(layer, "inner")
+        leave(layer, "upper")
+        need(weights[4 * layer + 3])
+        hidden[...] += in_nt(kept["upper"][layer], weights[4 * layer + 3][...])
+
+    def between():
+        keep = mask_ref[...].reshape(1, SEQ)
+        hidden[...] = hidden[...] * keep_column(keep) + in_nt(select_ref[SEQ : 2 * SEQ, :], entry[...])
+
+    def keep_column(keep):
+        return jnp.transpose(jnp.broadcast_to(keep, (128, SEQ)))[:, :1]
+
+    for layer in range(2):
+        pieces.append(functools.partial(project, layer))
+        for pair in range(HEADS // 2):
+            pieces.append(functools.partial(attend, layer, pair))
+        pieces.append(functools.partial(close, layer))
+        for part in range(3):
+            pieces.append(functools.partial(up, layer, part, 3))
+        pieces.append(functools.partial(down, layer))
+        if layer == 0:
+            pieces.append(between)
+
+    def finish():
+        top_ref[...] = hidden[BUF:, :].astype(bf)
+    pieces.append(finish)
+    return pieces
+
+
+def forward_kernel(*refs):
+    entry_hbm, weight_hbm, (select_ref, mask_ref), refs = refs[0], refs[1:9], refs[9:11], refs[11:]
+    kept_hbm, (top_ref,), refs = refs[: len(KEPT)], refs[len(KEPT) : len(KEPT) + 1], refs[len(KEPT) + 1 :]
+    entry, weights, kept_refs, (hidden, weight_sem, kept_sem) = refs[0], refs[1:9], refs[9 : 9 + len(KEPT)], refs[9 + len(KEPT) :]
+    kept = {name: ref for (name, _, _), ref in zip(KEPT, kept_refs)}
+    local = [(entry_hbm, entry)] + list(zip(weight_hbm, weights))
+    fetches = {id(ref): pltpu.make_async_copy(hbm, ref, weight_sem.at[k]) for k, (hbm, ref) in enumerate(local)}
+    for copy in fetches.values():
+        copy.start()
+    leaving = []
+
+    def leave(layer, name):
+        k = KEPT_INDEX[name]
+        copy = pltpu.make_async_copy(kept_refs[k].at[layer], kept_hbm[k].at[layer], kept_sem.at[layer, k])
+        copy.start()
+        leaving.append(copy)
+
+    for piece in forward_pieces(
+        weights, entry, select_ref, mask_ref, hidden, kept, top_ref, lambda ref: fetches[id(ref)].wait(), leave
+    ):
+        piece()
+    for copy in leaving:
+        copy.wait()
+
+
+def trunk_forward(entry, weights, select, mask):
+    bf, f32 = jnp.bfloat16, jnp.float32
+    vmem, hbm = pl.BlockSpec(memory_space=pltpu.VMEM), pl.BlockSpec(memory_space=pl.ANY)
+    shapes = [(2, SEQ, columns) for _, columns, _ in KEPT]
+    outs = pl.pallas_call(
+        forward_kernel,
+        out_shape=[jax.ShapeDtypeStruct(s, dtype) for s, (_, _, dtype) in zip(shapes, KEPT)]
+        + [jax.ShapeDtypeStruct((LAT, D), bf)],
+        in_specs=[hbm] * 9 + [vmem] * 2,
+        out_specs=[hbm] * len(KEPT) + [vmem],
+        scratch_shapes=[pltpu.VMEM(w.shape, bf) for w in [entry] + weights]
+        + [pltpu.VMEM(s, dtype) for s, (_, _, dtype) in zip(shapes, KEPT)]
+        + [pltpu.VMEM((SEQ, D), f32), pltpu.SemaphoreType.DMA((9,)), pltpu.SemaphoreType.DMA((2, len(KEPT)))],
+        compiler_params=pltpu.CompilerParams(vmem_limit_bytes=60 * 2**20),
+    )(entry, *weights, select, mask)
+    return outs[-1], outs[:-1]
+
+
+def backward_pieces(layer, weights, gain, mask_ref, hidden, middle, kept, back, gain_grad, need, leave):
+    bf = jnp.bfloat16
     w_qkv, w_out, w_up, w_down = weights
-    first_norm, first_inv = normalize(hidden)
-    normed = (first_norm * gains[0]).astype(jnp.bfloat16)
-    packed = dot_plain(normed, w_qkv).astype(jnp.bfloat16)
-    query_rows = packed[:, :D].reshape(SEQ, HEADS, HD)
-    key_rows = packed[:, D : 2 * D].reshape(SEQ, HEADS, HD)
-    value_rows = packed[:, 2 * D :].reshape(SEQ, HEADS, HD)
-    scores = jnp.einsum(
-        "qhd,khd->hqk", query_rows, key_rows, preferred_element_type=jnp.float32
-    ) * HD ** (-0.5)
-    if key_keep is not None:
-        scores = jnp.where(key_keep[None, None, :] > 0, scores, -1e30)
-    attention = jax.nn.softmax(scores, -1)
-    attention_low = attention.astype(jnp.bfloat16)
-    mixed_heads = (
-        jnp.einsum("hqk,khd->qhd", attention_low, value_rows, preferred_element_type=jnp.float32)
-        .reshape(-1, D)
-        .astype(jnp.bfloat16)
-    )
-    middle = hidden + dot_plain(mixed_heads, w_out)
-    second_norm, second_inv = normalize(middle)
-    second = (second_norm * gains[1]).astype(jnp.bfloat16)
-    inner_rows = dot_plain(second, w_up)
-    upper_rows = jax.nn.gelu(inner_rows).astype(jnp.bfloat16)
-    output = middle + dot_right(upper_rows, w_down)
-    saved = (
-        first_norm, first_inv, normed, query_rows, key_rows, value_rows, attention,
-        attention_low, mixed_heads, second_norm, second_inv, second, inner_rows, upper_rows,
-    )
-    return (output, saved)
-
-
-def layer_backward(upstream, weights, gains, saved):
-    w_qkv, w_out, w_up, w_down = weights
+    pieces = []
+
+    def norm_step(upstream, n, inv):
+        return inv * (
+            upstream - jnp.mean(upstream, -1, keepdims=True) - n * jnp.mean(upstream * n, -1, keepdims=True)
+        )
+
+    def branch():
+        back["back_branch"][...] = hidden[...].astype(bf)
+        leave("back_branch")
+        need(w_down, "inner")
+
+    def widen(part, parts):
+        columns = slice(part * FF // parts, (part + 1) * FF // parts)
+        up = in_nn(back["back_branch"][...], w_down[:, columns])
+        x = kept["inner"][:, columns]
+        t = jnp.tanh(GELU_SCALE * (x + 0.044715 * x * x * x))
+        slope = 0.5 * (1.0 + t) + 0.5 * x * (1.0 - t * t) * (GELU_SCALE * (1.0 + 3.0 * 0.044715 * x * x))
+        back["back_inner"][:, columns] = (slope * up).astype(bf)
+
+    def narrow():
+        leave("back_inner")
+        need(w_up, "norm_two", "inv_two")
+        value = in_nt(back["back_inner"][...], w_up[...])
+        n = kept["norm_two"][...]
+        gain_grad[2 * layer + 1 : 2 * layer + 2, :] = jnp.sum(value * n, 0, keepdims=True)
+        middle[...] = hidden[...] + norm_step(value * gain(2 * layer + 1), n, kept["inv_two"][:, :1])
+        back["back_attn"][...] = middle[...].astype(bf)
+        leave("back_attn")
+
+    def unmix():
+        need(w_out, "packed")
+        back["mixed"][...] = in_nt(back["back_attn"][...], w_out[...]).astype(bf)
+
+    def attend(pair):
+        low = low_half()
+        at = lambda k: slice(k * D + pair * 2 * HD, k * D + (pair + 1) * 2 * HD)
+        q, k, v = (kept["packed"][:, at(i)] for i in range(3))
+        up = back["mixed"][:, at(0)]
+        zero = jnp.zeros((), bf)
+        parts = []
+        for side in range(2):
+            mine = low if side == 0 else ~low
+            scores = in_nt(jnp.where(mine, q, zero), k) * HD ** (-0.5)
+            if layer == 0:
+                scores = jnp.where(mask_ref[...] > 0, scores, -1e30)
+            attention = softmax_rows(scores)
+            back_attention = in_nt(jnp.where(mine, up, zero), v)
+            back_values = in_tn(attention.astype(bf), up)
+            back_scores = (
+                attention * (back_attention - jnp.sum(back_attention * attention, -1, keepdims=True))
+            ).astype(bf)
+            parts.append((in_nn(back_scores, k) * HD ** (-0.5), in_tn(back_scores, q) * HD ** (-0.5), back_values))
+        for i in range(3):
+            back["back_packed"][:, at(i)] = jnp.where(low, parts[0][i], parts[1][i]).astype(bf)
+
+    def close():
+        leave("back_packed")
+        need(w_qkv, "norm_one", "inv_one")
+        value = in_nt(back["back_packed"][...], w_qkv[...])
+        n = kept["norm_one"][...]
+        gain_grad[2 * layer : 2 * layer + 1, :] = jnp.sum(value * n, 0, keepdims=True)
+        hidden[...] = middle[...] + norm_step(value * gain(2 * layer), n, kept["inv_one"][:, :1])
+
+    pieces.append(branch)
+    for part in range(3):
+        pieces.append(functools.partial(widen, part, 3))
+    pieces += [narrow, unmix]
+    for pair in range(HEADS // 2):
+        pieces.append(functools.partial(attend, pair))
+    pieces.append(close)
+    return pieces
+
+
+BACK_KEPT = ("packed", "inner", "norm_one", "norm_two", "inv_one", "inv_two")
+
+
+def backward_kernel(*refs):
+    entry_ref, weight_hbm, (select_ref, mask_ref, top_ref), refs = refs[0], refs[1:9], refs[9:12], refs[12:]
+    kept_hbm, refs = refs[: len(BACK_KEPT)], refs[len(BACK_KEPT) :]
+    back_hbm, small_ref, refs = refs[: len(BACK)], refs[len(BACK)], refs[len(BACK) + 1 :]
+    weights, refs = refs[:4], refs[4:]
+    kept_refs, refs = refs[: len(BACK_KEPT)], refs[len(BACK_KEPT) :]
+    back_refs, (mixed, hidden, middle, decoder, gain_grad, weight_sem, kept_sem, back_sem) = refs[: len(BACK)], refs[len(BACK) :]
+    bf = jnp.bfloat16
+    gains = lambda row: in_nt(select_ref[2 * SEQ :, :], entry_ref[...])[row : row + 1, :]
+    hidden[...] = top_ref[...]
+    gain_grad[...] = jnp.zeros_like(gain_grad)
+    back = {name: ref for (name, _), ref in zip(BACK, back_refs)}
+    back["mixed"] = mixed
+    order = [3, 2, 1, 0]
+    kept_order = {3: ["inner"], 2: ["norm_two", "inv_two"], 1: ["packed"], 0: ["norm_one", "inv_one"]}
+
+    def fetches(layer):
+        moves = {}
+        for k in order:
+            moves[id(weights[k])] = pltpu.make_async_copy(weight_hbm[4 * layer + k], weights[k], weight_sem.at[k])
+            for name in kept_order[k]:
+                i = BACK_KEPT.index(name)
+                moves[name] = pltpu.make_async_copy(kept_hbm[i].at[layer], kept_refs[i], kept_sem.at[i])
+        return moves
+
+    moves = fetches(1)
+    for copy in moves.values():
+        copy.start()
+    for layer in (1, 0):
+        leaving = []
+
+        def need(*names):
+            for name in names:
+                moves[name if isinstance(name, str) else id(name)].wait()
+
+        def leave(name):
+            k = [n for n, _ in BACK].index(name)
+            copy = pltpu.make_async_copy(back_refs[k], back_hbm[k].at[layer], back_sem.at[k])
+            copy.start()
+            leaving.append(copy)
+
+        later = fetches(0) if layer == 1 else {}
+        kept = {name: ref for name, ref in zip(BACK_KEPT, kept_refs)}
+        for piece in backward_pieces(
+            layer, weights, gains, mask_ref, hidden, middle, kept, back, gain_grad, need, leave
+        ):
+            piece()
+            if layer == 1:
+                name = getattr(piece, "__name__", "")
+                if name == "narrow":
+                    free = [id(weights[3]), "inner", id(weights[2]), "norm_two", "inv_two"]
+                elif name == "unmix":
+                    free = [id(weights[1])]
+                elif name == "close":
+                    free = ["packed", id(weights[0]), "norm_one", "inv_one"]
+                else:
+                    free = []
+                for key in free:
+                    later[key].start()
+        for copy in leaving:
+            copy.wait()
+        if layer == 1:
+            moves = later
+            decoder[...] = hidden[...].astype(bf)
+            keep = jnp.transpose(jnp.broadcast_to(mask_ref[...], (128, SEQ)))[:, :1]
+            hidden[...] = hidden[...] * keep
+    small_ref[...] = (
+        in_tn(hidden[...].astype(bf), select_ref[:SEQ, :])
+        + in_tn(decoder[...], select_ref[SEQ : 2 * SEQ, :])
+        + in_tn(gain_grad[...].astype(bf), select_ref[2 * SEQ :, :])
+    ).astype(bf)
+
+
+def trunk_backward(entry, weights, select, mask, back_top, kept):
+    bf, f32 = jnp.bfloat16, jnp.float32
+    vmem, hbm = pl.BlockSpec(memory_space=pltpu.VMEM), pl.BlockSpec(memory_space=pl.ANY)
+    kept_in = [kept[KEPT_INDEX[name]] for name in BACK_KEPT]
+    outs = pl.pallas_call(
+        backward_kernel,
+        out_shape=[jax.ShapeDtypeStruct((2, SEQ, columns), bf) for _, columns in BACK]
+        + [jax.ShapeDtypeStruct((D, TRUNK_WIDTH), bf)],
+        in_specs=[vmem] + [hbm] * 8 + [vmem] * 3 + [hbm] * len(BACK_KEPT),
+        out_specs=[hbm] * len(BACK) + [vmem],
+        scratch_shapes=[pltpu.VMEM(w.shape, bf) for w in weights[:4]]
+        + [pltpu.VMEM(a.shape[1:], a.dtype) for a in kept_in]
+        + [pltpu.VMEM((SEQ, columns), bf) for _, columns in BACK]
+        + [
+            pltpu.VMEM((SEQ, D), bf), pltpu.VMEM((SEQ, D), f32), pltpu.VMEM((SEQ, D), f32), pltpu.VMEM((SEQ, D), bf),
+            pltpu.VMEM((16, D), f32),
+            pltpu.SemaphoreType.DMA((4,)), pltpu.SemaphoreType.DMA((len(BACK_KEPT),)),
+            pltpu.SemaphoreType.DMA((len(BACK),)),
+        ],
+        compiler_params=pltpu.CompilerParams(vmem_limit_bytes=60 * 2**20),
+    )(entry, *weights, select, mask, back_top, *kept_in)
+    back = dict(zip([name for name, _ in BACK], outs[:-1]))
+    pairs = []
+    for layer in range(2):
+        part = lambda name: kept[KEPT_INDEX[name]][layer]
+        pairs += [
+            (part("normed"), back["back_packed"][layer]), (part("mixed"), back["back_attn"][layer]),
+            (part("second"), back["back_inner"][layer]), (back["back_branch"][layer], part("upper")),
+        ]
+    return pairs, outs[-1]
+
+
+ROWS_AT_ONCE = 192
+HEAD_WEIGHTS = ((HW, 3 * HW), (HW, HW), (HW, HW)) * HB + (
+    (HW, D), (HW, HW), (HW, HW), (HW, HW), (HW, FREQ), (HW, 128), (HW, 128)
+)
+HEAD_LEFT = (3, 1, 1, 1, 1) * HB + (1, 1, 1, 1, 1, 1, 1, 1)
+
+
+def sigmoid(x):
+    return 0.5 + 0.5 * jnp.tanh(0.5 * x)
+
+
+def head_kernel(tokens, *refs):
+    (embed_ref, noisy_ref, target_ref, grad_col_ref, loss_col_ref, bias_ref, cond_ref), refs = refs[:7], refs[7:]
+    count = len(HEAD_WEIGHTS)
+    block_hbm, edge_hbm, refs = refs[:HB], refs[HB : HB + 7], refs[HB + 7 :]
+    weight_hbm = [
+        block.at[:, pl.ds(column, width)]
+        for block in block_hbm
+        for column, width in ((0, 3 * HW), (3 * HW, HW), (4 * HW, HW))
+    ] + list(edge_hbm)
+    left_hbm, refs = refs[: len(HEAD_LEFT)], refs[len(HEAD_LEFT) :]
+    (pred_ref, back_cond_ref, back_token_ref, bias_grad_ref, loss_ref), refs = refs[:5], refs[5:]
+    weights, refs = refs[:count], refs[count:]
+    left, refs = refs[: len(HEAD_LEFT)], refs[len(HEAD_LEFT) :]
     (
-        first_norm, first_inv, normed, query_rows, key_rows, value_rows, attention,
-        attention_low, mixed_heads, second_norm, second_inv, second, inner_rows, upper_rows,
-    ) = saved
-    back_branch = upstream.astype(jnp.bfloat16)
-    back_upper = dot_plain(back_branch, w_down)
-    back_inner = local_grad(jax.nn.gelu, inner_rows, back_upper).astype(jnp.bfloat16)
-    back_second = dot_right(back_inner, w_up)
-    grad_gain_two = jnp.sum(back_second * second_norm, 0)
-    back_middle = upstream + norm_back(back_second * gains[1], second_norm, second_inv)
-    back_attn_out = back_middle.astype(jnp.bfloat16)
-    back_mixed = dot_right(back_attn_out, w_out).astype(jnp.bfloat16).reshape(SEQ, HEADS, HD)
-    back_attention = jnp.einsum(
-        "qhd,khd->hqk", back_mixed, value_rows, preferred_element_type=jnp.float32
-    )
-    back_values = jnp.einsum(
-        "hqk,qhd->khd", attention_low, back_mixed, preferred_element_type=jnp.float32
-    )
-    back_scores = (
-        attention * (back_attention - jnp.sum(back_attention * attention, -1, keepdims=True))
-    ).astype(jnp.bfloat16)
-    back_queries = jnp.einsum(
-        "hqk,khd->qhd", back_scores, key_rows, preferred_element_type=jnp.float32
-    ) * HD ** (-0.5)
-    back_keys = jnp.einsum(
-        "hqk,qhd->khd", back_scores, query_rows, preferred_element_type=jnp.float32
-    ) * HD ** (-0.5)
-    back_packed = jnp.concatenate(
-        [back_queries.reshape(-1, D), back_keys.reshape(-1, D), back_values.reshape(-1, D)], 1
-    ).astype(jnp.bfloat16)
-    back_normed = dot_right(back_packed, w_qkv)
-    grad_gain_one = jnp.sum(back_normed * first_norm, 0)
-    back_hidden = back_middle + norm_back(back_normed * gains[0], first_norm, first_inv)
-    pairs = [
-        (normed, back_packed), (mixed_heads, back_attn_out), (second, back_inner), (back_branch, upper_rows)
+        time_inner, conditioning, projected, cond_sum, stream, back_silu, t0, t1, t2,
+        scale1, normed, inner, gate, branch, inverse, weight_sem, left_sem,
+    ) = refs
+    cond_t, time_two_t, shift_t, scale_t, time_one_t, in_t, out_t = weights[3 * HB :]
+    per_block = 5
+    silu_cond, time_hidden, back_time, back_time_inner, back_shift, back_scale, final_low, back_low = left[
+        per_block * HB :
     ]
-    return (back_hidden, pairs, [grad_gain_one, grad_gain_two])
+    bf = jnp.bfloat16
+
+    def fetch(k):
+        return pltpu.make_async_copy(weight_hbm[k], weights[k], weight_sem.at[k])
+
+    order = [3 * HB, 3 * HB + 4, 3 * HB + 1, 3 * HB + 5]
+    for b in range(HB):
+        order += [3 * b, 3 * b + 1, 3 * b + 2]
+    order += [3 * HB + 2, 3 * HB + 3, 3 * HB + 6]
+    for k in order:
+        fetch(k).start()
+
+    def nn(x, w):
+        return jnp.dot(x, w, preferred_element_type=jnp.float32)
+
+    def nt(x, w):
+        return lax.dot_general(x, w, (((1,), (1,)), ((), ())), preferred_element_type=jnp.float32)
+
+    def by_rows(body):
+        for i in range(0, tokens, ROWS_AT_ONCE):
+            body(slice(i, i + ROWS_AT_ONCE))
+
+    bias_grad_ref[...] = jnp.zeros_like(bias_grad_ref)
+    loss_ref[...] = jnp.zeros_like(loss_ref)
+    cond_sum[...] = jnp.zeros_like(cond_sum)
+
+    def bias(row):
+        return bias_ref[row : row + 1, :]
+
+    def add_bias_grad(row, value):
+        bias_grad_ref[row : row + 1, :] += jnp.sum(value.astype(jnp.float32), 0, keepdims=True)
+
+    @pl.loop(0, COPIES)
+    def _(c):
+        def need(*numbers):
+            @pl.when(c == 0)
+            def _():
+                for k in numbers:
+                    fetch(k).wait()
+
+        def leave(k):
+            return pltpu.make_async_copy(left[k], left_hbm[k].at[c], left_sem.at[k])
+
+        def room(*numbers):
+            @pl.when(c > 0)
+            def _():
+                for k in numbers:
+                    leave(k).wait()
+
+        base = per_block * HB
+        room(base, base + 1)
+        need(3 * HB)
+
+        @pl.when(c == 0)
+        def _():
+            projected[...] = nt(cond_ref[...], cond_t[...])
+
+        need(3 * HB + 4, 3 * HB + 1, 3 * HB + 5)
+        time_inner[...] = nt(embed_ref[c], time_one_t[...])
+
+        def _(r):
+            value = time_inner[r, :] + bias(10)
+            time_inner[r, :] = value
+            time_hidden[r, :] = (value * sigmoid(value)).astype(bf)
+        by_rows(_)
+        leave(base + 1).start()
+        t0[...] = nt(time_hidden[...], time_two_t[...])
+        stream[...] = nt(noisy_ref[c], in_t[...])
+
+        def _(r):
+            value = projected[r, :] + (t0[r, :] + bias(11))
+            conditioning[r, :] = value
+            silu_cond[r, :] = (value * sigmoid(value)).astype(bf)
+            stream[r, :] = stream[r, :] + bias(14)
+        by_rows(_)
+        leave(base).start()
+
+        for b in range(HB):
+            w_mod, w_up, w_down = weights[3 * b : 3 * b + 3]
+            bm, shaped, back_inner, back_branch, hidden = left[per_block * b : per_block * (b + 1)]
+            room(*range(per_block * b, per_block * (b + 1)))
+            need(3 * b)
+            t0[...] = nn(silu_cond[...], w_mod[:, :HW])
+            t1[...] = nn(silu_cond[...], w_mod[:, HW : 2 * HW])
+            gate[b] = nn(silu_cond[...], w_mod[:, 2 * HW :])
+
+            def _(r):
+                value = stream[r, :]
+                centred = value - jnp.mean(value, -1, keepdims=True)
+                inv = lax.rsqrt(jnp.mean(centred * centred, -1, keepdims=True) + NORM_EPS)
+                n = centred * inv
+                s = 1.0 + (t1[r, :] + bias(5 * b + 1))
+                inverse[b, r, :] = jnp.broadcast_to(inv, (ROWS_AT_ONCE, 128))
+                normed[b, r, :] = n
+                scale1[b, r, :] = s
+                shaped[r, :] = (n * s + (t0[r, :] + bias(5 * b))).astype(bf)
+            by_rows(_)
+            leave(per_block * b + 1).start()
+            need(3 * b + 1)
+            inner[b] = nn(shaped[...], w_up[...])
+
+            def _(r):
+                value = inner[b, r, :] + bias(5 * b + 3)
+                inner[b, r, :] = value
+                hidden[r, :] = (value * sigmoid(value)).astype(bf)
+            by_rows(_)
+            leave(per_block * b + 4).start()
+            need(3 * b + 2)
+            branch[b] = nt(hidden[...], w_down[...])
+
+            def _(r):
+                value = branch[b, r, :] + bias(5 * b + 4)
+                g = gate[b, r, :] + bias(5 * b + 2)
+                branch[b, r, :] = value
+                gate[b, r, :] = g
+                stream[r, :] = stream[r, :] + g * value
+            by_rows(_)
+
+        need(3 * HB + 2, 3 * HB + 3, 3 * HB + 6)
+        room(*range(base + 2, base + 8))
+        t0[...] = nt(silu_cond[...], shift_t[...])
+        t1[...] = nt(silu_cond[...], scale_t[...])
+        def _(r):
+            value = stream[r, :]
+            centred = value - jnp.mean(value, -1, keepdims=True)
+            inv = lax.rsqrt(jnp.mean(centred * centred, -1, keepdims=True) + NORM_EPS)
+            n = centred * inv
+            s = 1.0 + (t1[r, :] + bias(13))
+            inverse[HB, r, :] = jnp.broadcast_to(inv, (ROWS_AT_ONCE, 128))
+            t2[r, :] = n
+            t1[r, :] = s
+            final_low[r, :] = (n * s + (t0[r, :] + bias(12))).astype(bf)
+        by_rows(_)
+        leave(base + 6).start()
+        difference = nn(final_low[...], out_t[...]) - target_ref[c]
+        loss_ref[...] += loss_col_ref[c] * difference * difference
+        pred_ref[c] = (grad_col_ref[c] * difference).astype(bf)
+        t0[...] = nt(pred_ref[c], out_t[...])
+
+        def _(r):
+            back = t0[r, :]
+            n = t2[r, :]
+            low_shift, low_scale = back.astype(bf), (back * n).astype(bf)
+            back_shift[r, :] = low_shift
+            back_scale[r, :] = low_scale
+            up = back * t1[r, :]
+            add_bias_grad(12, low_shift)
+            add_bias_grad(13, low_scale)
+            stream[r, :] = inverse[HB, r, :1] * (
+                up - jnp.mean(up, -1, keepdims=True) - n * jnp.mean(up * n, -1, keepdims=True)
+            )
+        by_rows(_)
+        leave(base + 4).start()
+        leave(base + 5).start()
+        back_silu[...] = nn(back_shift[...], shift_t[...]) + nn(back_scale[...], scale_t[...])
+
+        for b in reversed(range(HB)):
+            w_mod, w_up, w_down = weights[3 * b : 3 * b + 3]
+            bm, shaped, back_inner, back_branch, hidden = left[per_block * b : per_block * (b + 1)]
+
+            def _(r):
+                back = stream[r, :]
+                low = (back * gate[b, r, :]).astype(bf)
+                low_gate = (back * branch[b, r, :]).astype(bf)
+                back_branch[r, :] = low
+                bm[r, 2 * HW :] = low_gate
+                add_bias_grad(5 * b + 4, low)
+                add_bias_grad(5 * b + 2, low_gate)
+            by_rows(_)
+            leave(per_block * b + 3).start()
+            t0[...] = nn(back_branch[...], w_down[...])
+
+            def _(r):
+                value = inner[b, r, :]
+                s = sigmoid(value)
+                low = (t0[r, :] * (s * (1.0 + value * (1.0 - s)))).astype(bf)
+                back_inner[r, :] = low
+                add_bias_grad(5 * b + 3, low)
+            by_rows(_)
+            leave(per_block * b + 2).start()
+            t0[...] = nt(back_inner[...], w_up[...])
+
+            def _(r):
+                back = t0[r, :]
+                n = normed[b, r, :]
+                low_shift, low_scale = back.astype(bf), (back * n).astype(bf)
+                bm[r, :HW] = low_shift
+                bm[r, HW : 2 * HW] = low_scale
+                add_bias_grad(5 * b, low_shift)
+                add_bias_grad(5 * b + 1, low_scale)
+                up = back * scale1[b, r, :]
+                stream[r, :] = stream[r, :] + inverse[b, r, :1] * (
+                    up - jnp.mean(up, -1, keepdims=True) - n * jnp.mean(up * n, -1, keepdims=True)
+                )
+            by_rows(_)
+            leave(per_block * b).start()
+            back_silu[...] += nt(bm[...], w_mod[...])
+
+        def _(r):
+            value = conditioning[r, :]
+            s = sigmoid(value)
+            back = back_silu[r, :] * (s * (1.0 + value * (1.0 - s)))
+            low, low_stream = back.astype(bf), stream[r, :].astype(bf)
+            cond_sum[r, :] = cond_sum[r, :] + back
+            back_time[r, :] = low
+            back_low[r, :] = low_stream
+            add_bias_grad(11, low)
+            add_bias_grad(14, low_stream)
+        by_rows(_)
+        leave(base + 2).start()
+        leave(base + 7).start()
+        t0[...] = nn(back_time[...], time_two_t[...])
+
+        def _(r):
+            value = time_inner[r, :]
+            s = sigmoid(value)
+            low = (t0[r, :] * (s * (1.0 + value * (1.0 - s)))).astype(bf)
+            back_time_inner[r, :] = low
+            add_bias_grad(10, low)
+        by_rows(_)
+        leave(base + 3).start()
+
+    back_cond_ref[...] = cond_sum[...].astype(bf)
+    back_token_ref[...] = nn(back_cond_ref[...], cond_t[...]).astype(bf)
+    for k in range(len(HEAD_LEFT)):
+        pltpu.make_async_copy(left[k], left_hbm[k].at[COPIES - 1], left_sem.at[k]).wait()
 
 
 def head_pass(
     blocks, edges, biases, cond_rows, clean_rows, noise_rows, step_rows, weight_rows, weight_total
 ):
-    cond_t, time_two_t, shift_t, scale_t, time_one_t, in_t, out_t = edges
-    token_count = cond_rows.shape[0]
-    extra = biases[HB]
+    bf = jnp.bfloat16
+    tokens = cond_rows.shape[0]
     half_freq = FREQ // 2
     frequencies = jnp.exp(-math.log(10000.0) * jnp.arange(half_freq, dtype=jnp.float32) / half_freq)
-    step_times = step_rows.astype(jnp.float32)
-    angles = step_times.reshape(-1)[:, None] * frequencies
-    time_embed = jnp.concatenate([jnp.cos(angles), jnp.sin(angles)], -1).astype(jnp.bfloat16)
-    time_inner = dot_right(time_embed, time_one_t) + extra[:HW]
-    time_hidden = jax.nn.silu(time_inner).astype(jnp.bfloat16)
-    time_vector = dot_right(time_hidden, time_two_t) + extra[HW : 2 * HW]
-    projected = dot_right(cond_rows, cond_t)
-    conditioning = (projected[:, None, :] + time_vector.reshape(token_count, COPIES, HW)).reshape(
-        -1, HW
-    )
-    silu_cond = jax.nn.silu(conditioning).astype(jnp.bfloat16)
+    step_times = step_rows.astype(jnp.float32).T
+    angles = step_times[..., None] * frequencies
+    time_embed = jnp.concatenate([jnp.cos(angles), jnp.sin(angles)], -1).astype(bf)
     phase_angle = (step_times / TSTEPS + 0.008) / 1.008 * (math.pi / 2)
     keep_part = jnp.cos(phase_angle)[..., None]
     noise_part = jnp.sin(phase_angle)[..., None]
-    clean_copies = clean_rows.astype(jnp.float32)[:, None, :]
-    fresh_noise = noise_rows.astype(jnp.float32).reshape(token_count, COPIES, CH)
-    noisy_rows = (
-        (keep_part * clean_copies + noise_part * fresh_noise).reshape(-1, CH).astype(jnp.bfloat16)
-    )
-    target = (keep_part * fresh_noise - noise_part * clean_copies).reshape(-1, CH)
-    stream = dot_right(noisy_rows, in_t) + extra[4 * HW :]
-    saved = []
-    for block_number in range(HB):
-        w_mod, w_up, w_down = blocks[block_number]
-        bias_row = biases[block_number]
-        modulation = dot_plain(silu_cond, w_mod) + bias_row[: 3 * HW]
-        normed, inverse = normalize(stream)
-        shaped = (normed * (1.0 + modulation[:, HW : 2 * HW]) + modulation[:, :HW]).astype(
-            jnp.bfloat16
-        )
-        inner_rows = dot_plain(shaped, w_up) + bias_row[3 * HW : 4 * HW]
-        hidden = jax.nn.silu(inner_rows).astype(jnp.bfloat16)
-        branch = dot_right(hidden, w_down) + bias_row[4 * HW :]
-        saved.append((modulation, normed, inverse, shaped, inner_rows, hidden, branch))
-        stream = stream + modulation[:, 2 * HW :] * branch
-    final_shift = dot_right(silu_cond, shift_t) + extra[2 * HW : 3 * HW]
-    final_scale = dot_right(silu_cond, scale_t) + extra[3 * HW : 4 * HW]
-    final_norm, final_inv = normalize(stream)
-    final_low = (final_norm * (1.0 + final_scale) + final_shift).astype(jnp.bfloat16)
-    predicted = dot_plain(final_low, out_t)
-    flat_weights = weight_rows.reshape(-1)
-    errors = jnp.mean((predicted - target) ** 2, -1)
-    loss_local = jnp.sum(flat_weights * errors)
-    back_pred = (flat_weights[:, None] * 2.0 * (predicted - target) / (CH * weight_total)).astype(
-        jnp.bfloat16
-    )
-    grad_out_t = dot_left(final_low, back_pred)
-    back_final = dot_right(back_pred, out_t)
-    back_shift = back_final.astype(jnp.bfloat16)
-    back_scale = (back_final * final_norm).astype(jnp.bfloat16)
-    back_silu = dot_plain(back_shift, shift_t) + dot_plain(back_scale, scale_t)
-    back_stream = norm_back(back_final * (1.0 + final_scale), final_norm, final_inv)
-    block_pairs = [None] * HB
-    bias_grads = [None] * (HB + 1)
-    for block_number in reversed(range(HB)):
-        w_mod, w_up, w_down = blocks[block_number]
-        modulation, normed, inverse, shaped, inner_rows, hidden, branch = saved[block_number]
-        back_branch = (back_stream * modulation[:, 2 * HW :]).astype(jnp.bfloat16)
-        back_gate = back_stream * branch
-        back_hidden = dot_plain(back_branch, w_down)
-        back_inner = local_grad(jax.nn.silu, inner_rows, back_hidden).astype(jnp.bfloat16)
-        back_shaped = dot_right(back_inner, w_up)
-        back_stream = back_stream + norm_back(
-            back_shaped * (1.0 + modulation[:, HW : 2 * HW]), normed, inverse
-        )
-        back_modulation = jnp.concatenate([back_shaped, back_shaped * normed, back_gate], 1).astype(
-            jnp.bfloat16
-        )
-        back_silu = back_silu + dot_right(back_modulation, w_mod)
-        block_pairs[block_number] = [
-            (silu_cond, back_modulation), (shaped, back_inner), (back_branch, hidden)
-        ]
-        bias_grads[block_number] = jnp.concatenate(
-            [column_sum(back_modulation), column_sum(back_inner), column_sum(back_branch)]
-        )
-    back_stream_low = back_stream.astype(jnp.bfloat16)
-    grad_in_t = dot_left(back_stream_low, noisy_rows)
-    back_conditioning = local_grad(jax.nn.silu, conditioning, back_silu)
-    back_time = back_conditioning.astype(jnp.bfloat16)
-    back_time_hidden = dot_plain(back_time, time_two_t)
-    back_time_inner = local_grad(jax.nn.silu, time_inner, back_time_hidden).astype(jnp.bfloat16)
-    grad_time_one_t = dot_left(back_time_inner, time_embed)
-    back_cond = back_conditioning.reshape(token_count, COPIES, HW).sum(1).astype(jnp.bfloat16)
-    grad_cond_t = dot_left(back_cond, cond_rows)
-    back_tokens = dot_plain(back_cond, cond_t)
-    bias_grads[HB] = jnp.concatenate(
-        [
-            column_sum(back_time_inner), column_sum(back_time), column_sum(back_shift),
-            column_sum(back_scale), column_sum(back_stream_low),
-        ]
-    )
-    pairs = [pair for group in block_pairs for pair in group] + [
-        (back_time, time_hidden), (back_shift, silu_cond), (back_scale, silu_cond)
-    ]
-    small = (grad_cond_t, grad_time_one_t, grad_in_t, grad_out_t)
-    return (loss_local, pairs, small, jnp.stack(bias_grads), back_tokens)
+    clean_copies = clean_rows.astype(jnp.float32)[None]
+    fresh_noise = noise_rows.astype(jnp.float32).reshape(tokens, COPIES, CH).transpose(1, 0, 2)
+    wide = ((0, 0), (0, 0), (0, 128 - CH))
+    noisy = jnp.pad((keep_part * clean_copies + noise_part * fresh_noise).astype(bf), wide)
+    target = jnp.pad(keep_part * fresh_noise - noise_part * clean_copies, wide)
+    by_copy = jnp.broadcast_to(weight_rows.T[..., None], (COPIES, tokens, 128))
+    f32 = jnp.float32
+    vmem, hbm = pl.BlockSpec(memory_space=pltpu.VMEM), pl.BlockSpec(memory_space=pl.ANY)
+    lefts = [(COPIES, tokens, k * HW) for k in HEAD_LEFT]
+    units = lambda *lead: pltpu.VMEM((*lead, tokens, HW), f32)
+    outs = pl.pallas_call(
+        functools.partial(head_kernel, tokens),
+        out_shape=[jax.ShapeDtypeStruct(shape, bf) for shape in lefts]
+        + [
+            jax.ShapeDtypeStruct((COPIES, tokens, 128), bf),
+            jax.ShapeDtypeStruct((tokens, HW), bf),
+            jax.ShapeDtypeStruct((tokens, D), bf),
+            jax.ShapeDtypeStruct((5 * (HB + 1) + 1, HW), f32),
+            jax.ShapeDtypeStruct((tokens, 128), f32),
+        ],
+        in_specs=[vmem] * 7 + [hbm] * (HB + 7),
+        out_specs=[hbm] * len(HEAD_LEFT) + [vmem] * 5,
+        scratch_shapes=[pltpu.VMEM(shape, bf) for shape in HEAD_WEIGHTS]
+        + [pltpu.VMEM((tokens, k * HW), bf) for k in HEAD_LEFT]
+        + [units()] * 9
+        + [units(HB)] * 5
+        + [
+            pltpu.VMEM((HB + 1, tokens, 128), f32),
+            pltpu.SemaphoreType.DMA((len(HEAD_WEIGHTS),)), pltpu.SemaphoreType.DMA((len(HEAD_LEFT),)),
+        ],
+        compiler_params=pltpu.CompilerParams(vmem_limit_bytes=60 * 2**20),
+    )(
+        time_embed, noisy, target, by_copy * (2.0 / (CH * weight_total)), by_copy * (1.0 / CH),
+        jnp.pad(biases.reshape(5 * (HB + 1), HW), ((0, 1), (0, 0))), cond_rows,
+        *blocks, *edges,
+    )
+    left = [a.reshape(COPIES * tokens, -1) for a in outs[: len(HEAD_LEFT)]]
+    back_pred, back_cond, back_tokens, bias_grad, loss_part = outs[len(HEAD_LEFT) :]
+    silu_cond, time_hidden, back_time, back_time_inner, back_shift, back_scale, final_low, back_low = left[5 * HB :]
+    pairs = []
+    for b in range(HB):
+        bm, shaped, back_inner, back_branch, hidden = left[5 * b : 5 * (b + 1)]
+        pairs += [(silu_cond, bm), (shaped, back_inner), (back_branch, hidden)]
+    pairs += [(back_time, time_hidden), (back_shift, silu_cond), (back_scale, silu_cond)]
+    flat = lambda a: a.reshape(COPIES * tokens, -1)
+    small = (
+        dot_left(back_cond, cond_rows),
+        dot_left(back_time_inner, flat(time_embed)),
+        dot_left(back_low, flat(noisy))[:, :CH],
+        dot_left(final_low, flat(back_pred))[:, :CH],
+    )
+    bias_grad = bias_grad[: 5 * (HB + 1)].reshape(HB + 1, 5 * HW)
+    return (jnp.sum(loss_part), pairs, small, bias_grad, back_tokens)
 
 
 def adamw(master, first, second, gradient, factor, step_rate):
@@ -681,32 +1154,26 @@
 HEAD_WIDTH = 512
 
 
-def gather_plan(part_sets, edge_parts, limit):
-    chunks, widths = [], []
-    for index, parts in enumerate(part_sets):
+def gather_plan(part_sets, limit):
+    chunks, shapes = [], []
+    for source, index, rows, parts in part_sets:
         column = 0
         for part in parts:
             for k in range(0, part, limit):
-                chunks.append((0, index, column + k, len(widths), k, min(limit, part - k)))
-            widths.append(part)
+                chunks.append((source, index, column + k, len(shapes), k, min(limit, part - k)))
+            shapes.append((rows, part))
             column += part
-    edge_chunks, column = [], 0
-    for part in edge_parts:
-        for k in range(0, part, limit):
-            edge_chunks.append((1, None, column + k, len(widths), k, min(limit, part - k)))
-        widths.append(part)
-        column += part
-    return edge_chunks + chunks, widths
-
-
-def plain_gather(sources, chunks, widths):
+    return chunks, shapes
+
+
+def plain_gather(sources, chunks, shapes):
     ends = {}
     for source, index, column, result, at, width in chunks:
         start, stop = ends.get(result, (source, index, column, column))[2:]
         ends[result] = (source, index, min(start, column), max(stop, column + width))
     wholes = {}
     results = []
-    for number in range(len(widths)):
+    for number in range(len(shapes)):
         source, index, start, stop = ends[number]
         if (source, index) not in wholes:
             block = sources[source] if index is None else sources[source][index]
@@ -748,20 +1215,17 @@
         ],
         1,
     )
-    trunk_chunks, trunk_widths = gather_plan([TRUNK_PARTS] * 2, (TRUNK_WIDTH,), TRUNK_WIDTH)
-    head_chunks, head_widths = gather_plan([HEAD_PARTS] * HB, EDGE_PARTS, HEAD_WIDTH)
+    chunks, shapes = gather_plan(
+        [(1, None, r0, (TRUNK_WIDTH,)), (0, 0, r0, TRUNK_PARTS), (0, 1, r0, TRUNK_PARTS), (2, None, r1, EDGE_PARTS)],
+        TRUNK_WIDTH,
+    )
+    sources = [low_blocks, low_entry, low_edges]
     if direct:
-        trunk = [
-            a.reshape(D, -1) for a in gather_rows([low_blocks, low_entry], trunk_chunks, trunk_widths, r0, nz, 1)
-        ]
+        gathered = [a.reshape(devices * a.shape[4], -1) for a in gather_rows(sources, chunks, shapes, nz, 1)]
     else:
-        trunk = plain_gather([low_blocks, low_entry], trunk_chunks, trunk_widths)
-    if direct and HEAD_DIRECT:
-        head = [
-            a.reshape(HW, -1) for a in gather_rows([low_head, low_edges], head_chunks, head_widths, r1, nz, 2)
-        ]
-    else:
-        head = plain_gather([low_head, low_edges], head_chunks, head_widths)
+        gathered = plain_gather(sources, chunks, shapes)
+    trunk, edge_mats = gathered[:9], gathered[9:]
+    head_blocks = [lax.all_gather(low_head[b], AXES, axis=0, tiled=True) for b in range(HB)]
 
     local_total = jnp.sum(mask_counts)
     early = exchange(
@@ -778,15 +1242,13 @@
     ids = jnp.arange(LAT, dtype=jnp.int32)
     masked = jnp.any((order_row[:, None] == ids[None, :]) & (ids < local_total)[:, None], 0)
     key_keep = jnp.concatenate([jnp.ones((BUF,), jnp.float32), 1.0 - masked.astype(jnp.float32)])
-    layers = (trunk[:4], trunk[4:8])
-    entry = trunk[8].T
-    entry_rows = entry[: 2 * SEQ].astype(jnp.float32)
-    gain_rows = entry[2 * SEQ + CH : 2 * SEQ + CH + 4].astype(jnp.float32)
-    projected = dot_plain(clean, entry[2 * SEQ : 2 * SEQ + CH])
-    start_rows = entry_rows[:SEQ] + jnp.concatenate([jnp.zeros((BUF, D), jnp.float32), projected], 0)
-    encoded, encoder_saved = layer_forward(start_rows, layers[0], gain_rows[:2], key_keep)
-    decoder_input = encoded * key_keep[:, None] + entry_rows[SEQ : 2 * SEQ]
-    top_rows, decoder_saved = layer_forward(decoder_input, layers[1], gain_rows[2:], None)
+    positions = jnp.arange(SEQ, dtype=jnp.int32)
+    columns = jnp.arange(TRUNK_WIDTH, dtype=jnp.int32)
+    pick_rows = jnp.concatenate([positions, SEQ + positions, 2 * SEQ + CH + jnp.arange(16, dtype=jnp.int32)])
+    select = (pick_rows[:, None] == columns[None, :]).astype(bf) + jnp.pad(
+        clean, ((BUF, SEQ + 16), (2 * SEQ, TRUNK_WIDTH - 2 * SEQ - CH))
+    )
+    top_rows, kept = trunk_forward(trunk[0], trunk[1:9], select, key_keep[None])
 
     capacity = (LAT + devices - 1) // devices
     slots = devices * capacity
@@ -799,7 +1261,7 @@
         (slot_position[:, None] == ids[None, :]) & (slot_token < local_total)[:, None]
     ).astype(bf)
     outgoing = dot_plain(
-        pick, jnp.concatenate([top_rows[BUF:].astype(bf), clean, jnp.zeros((LAT, 112), bf)], 1)
+        pick, jnp.concatenate([top_rows, clean, jnp.zeros((LAT, 112), bf)], 1)
     ).astype(bf)
     incoming = lax.all_to_all(
         outgoing.reshape(devices, capacity, -1), AXES, split_axis=0, concat_axis=0, tiled=True
@@ -816,8 +1278,6 @@
     place = (row_slot[:, None] == slot_ids[None, :]).astype(bf)
     received = dot_plain(place, incoming).astype(bf)
 
-    head_blocks = [head[3 * b : 3 * b + 3] for b in range(HB)]
-    edge_mats = head[3 * HB :]
     misc = edge_mats[5]
     biases = (
         misc[:, 2 * CH : 2 * CH + 5 * (HB + 1)]
@@ -828,7 +1288,11 @@
     )
     loss_local, head_pairs, small, bias_grad, back_tokens = head_pass(
         head_blocks,
-        edge_mats[:5] + [misc[:, :CH], misc[:, CH : 2 * CH]],
+        edge_mats[:5]
+        + [
+            jnp.pad(misc[:, :CH], ((0, 0), (0, 128 - CH))),
+            jnp.pad(misc[:, CH : 2 * CH], ((0, 0), (0, 128 - CH))),
+        ],
         biases,
         received[:, :D],
         received[:, D : D + CH],
@@ -863,22 +1327,7 @@
         returning.reshape(devices, capacity, D), AXES, split_axis=0, concat_axis=0, tiled=True
     ).reshape(slots, D)
     back_top = jnp.concatenate([jnp.zeros((BUF, D), jnp.float32), dot_left(pick, returned)], 0)
-    back_decoder, decoder_pairs, decoder_gains = layer_backward(
-        back_top, layers[1], gain_rows[2:], decoder_saved
-    )
-    back_encoded = back_decoder * key_keep[:, None]
-    back_start, encoder_pairs, encoder_gains = layer_backward(
-        back_encoded, layers[0], gain_rows[:2], encoder_saved
-    )
-    grad_input_t = dot_left(back_start[BUF:].astype(bf), clean)
-    trunk_small = jnp.concatenate(
-        [
-            back_start.T, back_decoder.T, grad_input_t,
-            jnp.stack(encoder_gains + decoder_gains, 1), jnp.zeros((D, 108), jnp.float32),
-        ],
-        1,
-    ).astype(bf)
-    trunk_pairs = encoder_pairs + decoder_pairs
+    trunk_pairs, trunk_small = trunk_backward(trunk[0], trunk[1:9], select, key_keep[None], back_top, kept)
     if direct:
         wide = reduce_products(
             trunk_pairs, trunk_small[None], D, TRUNK_WIDTH, (2 * r0, TRUNK_WIDTH // 2), nz, 5

time: 927 us -> 841 us (0.907)
  matrix products: 231 us -> 8.64 us
  Pallas kernels: 486 us -> 700 us
  other arithmetic: 72.2 us -> 33.1 us
  local copies, waits for them, and re-layouts: 83.6 us -> 54.6 us
    pallas_call x0 -> x3, Pallas kernels: none -> 154 us  [the longest x1 79.7 us: head_pass(): pl.pallas_call(functools.partial(head_kernel, tokens), out_shape=[jax.Sha...]
    dot_general x31 -> x0, matrix products: 117 us -> none  [the longest x21 90.5 us: dot_right(): lax.dot_general(left, right, (((1,), (1,)), ((), ())), preferred_element_...]
    dot_general x21 -> x2, matrix products: 93.2 us -> 2.44 us  [dot_plain(): return jnp.dot(left, right, preferred_element_type=jnp.float32)]
    pallas_call x1, Pallas kernels: 173 us -> 235 us  [gather_rows(): pl.pallas_call(functools.partial(ag_kernel, nz, chunks, len(sources)), ou...]
    reduce_sum x14 -> x1, other arithmetic: 22.3 us -> 0.62 us  [head_pass(): return (jnp.sum(loss_part), pairs, small, bias_grad, back_tokens)]
    reshape x10 -> x0, local copies, waits for them, and re-layouts: 18.2 us -> none  [the longest x1 5.19 us: head_pass(): back_conditioning.reshape(token_count, COPIES, HW).sum(1)]
    convert_element_type x14 -> x0, local copies, waits for them, and re-layouts: 14.3 us -> none  [the longest x3 3.55 us: layer_backward(): back_branch = upstream.astype(jnp.bfloat16)]
    squeeze x0 -> x8, local copies, waits for them, and re-layouts: none -> 13.6 us  [the longest x4 5.23 us: trunk_backward(): part = lambda name: kept[KEPT_INDEX[name]][layer]]
  transfers between devices with their start and end apart: 5 -> 4, of which waited for: 2 -> 2; matrix products, arithmetic and copies ran while one was open for 13% -> 3% of each run, Pallas kernels for 21% -> 33%
where the time goes in v2:
time: 841 us; the launch traced here: 837 us
  Pallas kernels  700 us (83%)
  local copies, waits for them, and re-layouts  54.6 us (6%)
  other arithmetic  33.1 us (4%)
  between operations  19.6 us (2%)
  waiting for transfers between devices  11.8 us (1%)
  starting transfers between devices  9.81 us (1%)
  matrix products  8.64 us (1%)
    pallas_call x2, Pallas kernels, reduce_products(): pl.pallas_call(functools.partial(rs_kernel, nz, row_count, width, jobs, e...  289 us
    pallas_call x1, Pallas kernels, gather_rows(): pl.pallas_call(functools.partial(ag_kernel, nz, chunks, len(sources)), ou...  235 us
    pallas_call x1, Pallas kernels, head_pass(): pl.pallas_call(functools.partial(head_kernel, tokens), out_shape=[jax.Sha...  79.7 us
    pallas_call x1, Pallas kernels, trunk_backward(): pl.pallas_call(backward_kernel, out_shape=[jax.ShapeDtypeStruct((2, SEQ,...  44.1 us
    pallas_call x1, Pallas kernels, trunk_forward(): pl.pallas_call(forward_kernel, out_shape=[jax.ShapeDtypeStruct(s, dtype)...  30 us
    unnamed x111, local copies, waits for them, and re-layouts  27.7 us
    pallas_call x2, Pallas kernels, exchange(): pl.pallas_call(functools.partial(exchange_kernel, dp_count, nz), out_shap...  21.9 us
  transfers between devices with their start and end apart: 4, of which 2 were waited for; matrix products, arithmetic and copies ran while one was open for 3% of the time, Pallas kernels for 33%

profile of v2, /device:TPU:0, one launch (start us, length us, event | category | flops | bytes accessed | tf_op | source)
XLA Modules:
  0.0 837.1 jit_solution(8464692226580978989)
XLA Ops:
  13.2 12.1 %shard_map.393 = f32[32,8,128]{2,1,0:T(8,128)S(1)} custom-call(f32[8,128]{1,0:T(8,128)S(1)} %broadcast_in_dim.41.in_ref), custom_call_target="tpu_custom_call" | custom-call | tf_op jit(solution)/shard_map/pallas_call | solution.py:435
  28.9 234.9 %shard_map.391 = (bf16[2,2,2,4,24,768]{5,4,3,2,1,0:T(8,128)(2,1)S(1)}, bf16[2,2,2,4,24,2304]{5,4,3,2,1,0:T(8,128)(2,1)S(1)}, bf16[2,2,2,4,24,768]{5,4,3,2,1,0:T(...) custom-call(bf16[2,24,9216]{2,1,0:T(8,128)(2,1)S(1)} %convert_elemen, ...), custom_call_target="tpu_custom_call" | custom-call | tf_op jit(solution)/shard_map/pallas_call | solution.py:380
  263.8 2.1 copy-done
  265.9 2.2 copy-done.1
  268.1 2.1 copy-done.2
  270.3 2.2 copy-done.3
  274.3 1.9 copy-done.5
  286.5 30.0 %shard_map.392 = (bf16[2,320,768]{2,1,0:T(8,128)(2,1)}, bf16[2,320,2304]{2,1,0:T(8,128)(2,1)}, bf16[2,320,768]{2,1,0:T(8,128)(2,1)}, bf16[2,320,768]{2,1,0:T(8,1...) custom-call(bf16[768,768]{1,0:T(8,128)(2,1)} %bitcast.198, ...), custom_call_target="tpu_custom_call" | custom-call | tf_op jit(solution)/shard_map/pallas_call | solution.py:612
  317.4 2.1 fusion.6
  319.5 5.4 all-to-all-start
  334.9 2.2 slice_bitcast_fusion
  342.8 79.7 %shard_map.394 = (bf16[4,192,3072]{2,1,0:T(8,128)(2,1)}, bf16[4,192,1024]{2,1,0:T(8,128)(2,1)}, bf16[4,192,1024]{2,1,0:T(8,128)(2,1)}, bf16[4,192,1024]{2,1,0:T(...) custom-call(bf16[4,192,256]{2,1,0:T(8,128)(2,1)} %pad_maximum_fusion, ...), custom_call_target="tpu_custom_call" | custom-call | tf_op jit(solution)/shard_map/pallas_call | solution.py:1095
  429.4 2.0 pad_maximum_fusion.refs_18_
  431.4 146.6 %shard_map.397 = f32[29,32,512]{2,1,0:T(8,128)} custom-call(bf16[768,1024]{1,0:T(8,128)(2,1)} %bitcast.211, bf16[768,1024]{1,0:T(8,128)(2,1)} %bitcast.230, bf16[768,1024]{1,0:T(8,128)(2,1)} %bitcast.232, bf16[768,1024]{1,0:T(8,128)(2,1)} %bitcast.212, bf16[768,1024]{1,0:T(8,128)(2,1)} %bitcast.234, bf16[768,1024]{1,0:T(8,128)(2,1)} %bitcast.236, ...), custom_call_target="tpu_custom_call" | custom-call | tf_op jit(solution)/shard_map/pallas_call | solution.py:275
  582.3 4.3 all-to-all-start.1
  588.3 10.1 %all-to-all-done.1 = bf16[32,8,768]{2,1,0:T(8,128)(2,1)} async-done(((bf16[32,8,768]{2,1,0:T(8,128)(2,1)}), bf16[32,8,768]{2,1,0:T(8,128)(2,1)}, u32[]{:S(2)}, u32[]{:S(2)}) %all-to-all-start.1) | async-done | bytes 393248 | tf_op jit(solution)/shard_map/all_to_all | solution.py:1326
  600.9 44.1 %shard_map.395 = (bf16[2,320,2304]{2,1,0:T(8,128)(2,1)}, bf16[2,320,768]{2,1,0:T(8,128)(2,1)}, bf16[2,320,3072]{2,1,0:T(8,128)(2,1)}, bf16[2,320,768]{2,1,0:T(8,128)(2,1)}, bf16[768,768]{1,0:T(8,128)(2,1)}) custom-call(bf16[768,768]{1,0:T(8,128)(2,1)} %bitcast.199, bf16[768,2304]{1,0:T(8,128)(2,1)} %bitcast.195, bf16[768,768]{1,0:T(8,128)(2,1)} %bitcast.201, ...), custom_call_target="tpu_custom_call" | custom-call | tf_op jit(solution)/shard_map/pallas_call | solution.py:783
  645.0 4.5 slice_bitcast_fusion.1
  653.9 142.3 %shard_map.396 = f32[25,24,768]{2,1,0:T(8,128)} custom-call(bf16[320,768]{1,0:T(8,128)(2,1)} %get-tuple-element.172.refs_0_, bf16[320,768]{1,0:T(8,128)(2,1)} %get-tuple-element.170.refs_1_, bf16[320,768]{1,0:T(8,128)(2,1)} %get-tuple-element.168.refs_2_, bf16[320,768]{1,0:T(8,128)(2,1)} %get-tuple-element.166.refs_3_, ...), custom_call_target="tpu_custom_call" | custom-call | tf_op jit(solution)/shard_map/pallas_call | solution.py:275
  796.2 2.7 fusion.2
  801.0 9.8 %shard_map.398 = f32[32,8,128]{2,1,0:T(8,128)S(1)} custom-call(f32[8,128]{1,0:T(8,128)S(1)} %broadcast_in_dim.88.in_ref), custom_call_target="tpu_custom_call" | custom-call | tf_op jit(solution)/shard_map/pallas_call | solution.py:435
  817.1 3.1 multiply_subtract_fusion.2
  821.5 2.7 multiply_subtract_fusion.1
  825.5 3.4 multiply_subtract_fusion
  (230 shorter events, 64.9 us)
Async XLA Ops:
  7.2 3.2 copy-start.23
  7.2 333.7 %all-gather.5.cloned.1.call-start = ((), (), s32[]{:S(2)}) async-start(), calls=%async_computation.2 | async-start | bytes 10813440 | tf_op jit(solution)/shard_map/all_gather | solution.py:1228
  9.6 331.3 %all-gather.7.cloned.1.call-start = ((), (), s32[]{:S(2)}) async-start(), calls=%async_computation.3 | async-start | bytes 10813440 | tf_op jit(solution)/shard_map/all_gather | solution.py:1228
  10.5 17.1 %copy-start.47 = (s32[1,256]{1,0:T(1,128)S(1)}, s32[1,256]{1,0:T(1,128)}, u32[]{:S(2)}) copy-start(s32[1,256]{1,0:T(1,128)} %param.25) | copy-start | bytes 3076
  10.5 17.9 %copy-start.43 = (bf16[1,256,16]{1,2,0:T(8,128)(2,1)S(1)}, bf16[1,256,16]{1,2,0:T(8,128)(2,1)}, u32[]{:S(2)}) copy-start(bf16[1,256,16]{1,2,0:T(8,128)(2,1)} %param.24) | copy-start | bytes 24580
  10.9 17.9 %copy-start.33 = (f32[656,24]{0,1:T(8,128)S(1)}, f32[656,24]{0,1:T(8,128)}, u32[]{:S(2)}) copy-start(f32[656,24]{0,1:T(8,128)} %param.32) | copy-start | bytes 188932
  316.5 8.7 %copy-start.38 = (bf16[192,64]{0,1:T(8,128)(2,1)S(1)}, bf16[192,64]{0,1:T(8,128)(2,1)}, u32[]{:S(2)}) copy-start(bf16[192,64]{0,1:T(8,128)(2,1)} %param.27) | copy-start | bytes 73732
  319.5 8.1 copy-start.39
  319.5 18.6 %all-to-all-start = ((bf16[32,8,896]{2,1,0:T(8,128)(2,1)}), bf16[32,8,896]{2,1,0:T(8,128)(2,1)S(1)}, u32[]{:S(2)}, u32[]{:S(2)}) async-start(bf16[32,8,896]{2,1,0:T(8,128)(2,1)} %fusion.6), calls=%async_computation | async-start | bytes 917504 | tf_op jit(solution)/shard_map/all_to_all | solution.py:1266
  325.1 5.1 copy-start.50
  325.3 5.7 copy-start.30
  327.7 4.3 copy-start.29
  579.9 8.4 %copy-start.16 = (f32[29,4,8,512]{3,2,0,1:T(8,128)}, f32[29,4,8,512]{3,2,0,1:T(8,128)S(1)}, u32[]{:S(2)}) copy-start(f32[29,4,8,512]{3,2,0,1:T(8,128)S(1)} %copy.103) | copy-start | bytes 5701636
  579.9 6.7 copy-start.35
  582.3 16.1 %all-to-all-start.1 = ((bf16[32,8,768]{2,1,0:T(8,128)(2,1)}), bf16[32,8,768]{2,1,0:T(8,128)(2,1)}, u32[]{:S(2)}, u32[]{:S(2)}) async-start(bf16[32,8,768]{2,1,0:T(8,128)(2,1)} %fusion.7), calls=%async_computation.1 | async-start | bytes 786432 | tf_op jit(solution)/shard_map/all_to_all | solution.py:1326
  645.0 4.6 copy-start.22
  796.2 16.8 %copy-start.15 = (f32[25,24,768]{2,1,0:T(8,128)S(1)}, f32[25,24,768]{2,1,0:T(8,128)}, u32[]{:S(2)}) copy-start(f32[25,24,768]{2,1,0:T(8,128)} %shard_map.396) | copy-start | bytes 5529604
  815.4 6.1 copy-start.27
  817.1 3.8 copy-start.48
  817.1 3.8 copy-start.49
  817.1 4.4 copy-start.20
  817.1 4.4 copy-start.26
  821.5 3.2 copy-start.24
  821.5 3.9 copy-start.25
  (35 other events, 59.0 us)
Sparse Core Ops, SparseCore 0:
  10.9 136.2 all-gather.4
  150.0 118.7 all-gather.6

commit v3 on v2

--- a/solution.py
+++ b/solution.py
@@ -35,9 +35,15 @@
 MESH_IDS = pl.DeviceIdType.MESH
 
 
-def rs_kernel(nz, row_count, width, jobs, extra_count, *refs):
+REDUCE_LAGS = (0, 1, 3, 5, 7)
+REDUCE_DEPTH = 3
+
+
+def reduce_program(nz, row_count, width, jobs, extra_count, refs, between=None):
     job_count = len(jobs)
-    x_refs, y_refs = refs[:job_count], refs[job_count : 2 * job_count]
+    picked = lambda ref, index: ref if index is None else ref.at[index]
+    x_refs = [picked(ref, job[2]) for ref, job in zip(refs[:job_count], jobs)]
+    y_refs = [picked(ref, job[3]) for ref, job in zip(refs[job_count : 2 * job_count], jobs)]
     position = 2 * job_count
     extra_ref = None
     if extra_count:
@@ -46,7 +52,7 @@
     out_ref = refs[position]
     (
         x_buf, y_buf, whole, land_core, first, land_first, second, land_second,
-        last, last_low, land_last,
+        last, last_low, land_last, extra_sem,
         load_sem, core_send, core_recv, first_send, first_recv, second_send, second_recv,
         last_send, last_recv, credit,
     ) = refs[position + 1 :]
@@ -55,7 +61,7 @@
     group = row_count // 8
     part = group // nz
     starts, total = [], 0
-    for _, columns in jobs:
+    for _, columns, _, _ in jobs:
         starts.append(total)
         total += columns // width
     computed = total
@@ -78,7 +84,7 @@
         )
 
     def prefetch(g):
-        for number, (_, columns) in enumerate(jobs):
+        for number, (_, columns, _, _) in enumerate(jobs):
             start, stop = starts[number], starts[number] + columns // width
 
             @pl.when((g >= start) & (g < stop))
@@ -96,13 +102,15 @@
             device_id_type=MESH_IDS,
         )
 
+    depth = REDUCE_DEPTH
+
     def first_copy(g):
         p = lax.rem(g, 2)
         mine = (1 - p) * xb + p * yb
         return pltpu.make_async_remote_copy(
-            src_ref=first.at[lax.rem(g, 3), 1 - mine],
+            src_ref=first.at[lax.rem(g, depth), 1 - mine],
             dst_ref=land_first.at[g],
-            send_sem=first_send.at[lax.rem(g, 3)],
+            send_sem=first_send.at[lax.rem(g, depth)],
             recv_sem=first_recv.at[g],
             device_id=(dp + (1 - p) * x_step + p * y_step, z),
             device_id_type=MESH_IDS,
@@ -112,9 +120,9 @@
         p = lax.rem(g, 2)
         mine = (1 - p) * yb + p * xb
         return pltpu.make_async_remote_copy(
-            src_ref=second.at[lax.rem(g, 3), 1 - mine],
+            src_ref=second.at[lax.rem(g, depth), 1 - mine],
             dst_ref=land_second.at[g],
-            send_sem=second_send.at[lax.rem(g, 3)],
+            send_sem=second_send.at[lax.rem(g, depth)],
             recv_sem=second_recv.at[g],
             device_id=(dp + (1 - p) * y_step + p * x_step, z),
             device_id_type=MESH_IDS,
@@ -123,9 +131,9 @@
     def last_copies(g):
         return [
             pltpu.make_async_remote_copy(
-                src_ref=last_low.at[lax.rem(g, 3), lax.rem(z + s, nz)],
+                src_ref=last_low.at[lax.rem(g, depth), lax.rem(z + s, nz)],
                 dst_ref=land_last.at[g, s - 1],
-                send_sem=last_send.at[lax.rem(g, 3), s - 1],
+                send_sem=last_send.at[lax.rem(g, depth), s - 1],
                 recv_sem=last_recv.at[g, s - 1],
                 device_id=z_peers[s - 1],
                 device_id_type=MESH_IDS,
@@ -154,17 +162,27 @@
         def _():
             for copy in loads(x_refs[0], y_refs[0], 0, slot):
                 copy.wait()
+            product = lax.dot_general(
+                x_buf[slot], y_buf[slot], (((0,), (0,)), ((), ())), preferred_element_type=jnp.float32
+            )
             for number in range(8):
-                put(number, lax.dot_general(
-                    x_buf[slot, :, pl.ds(number * group, group)], y_buf[slot],
-                    (((0,), (0,)), ((), ())), preferred_element_type=jnp.float32,
-                ).astype(jnp.bfloat16))
+                put(number, product[number * group : (number + 1) * group].astype(jnp.bfloat16))
 
         if extra_count:
             @pl.when(g >= computed)
             def _():
-                for number in range(8):
-                    put(number, extra_ref[g - computed, pl.ds(number * group, group), :])
+                copies = [
+                    pltpu.make_async_copy(
+                        extra_ref.at[g - computed, pl.ds(number * group, group), :],
+                        whole.at[slot, number % 2, number // 2],
+                        extra_sem.at[number],
+                    )
+                    for number in range(8)
+                ]
+                for copy in copies:
+                    copy.start()
+                for copy in copies:
+                    copy.wait()
 
         @pl.when(g >= 4)
         def _():
@@ -174,14 +192,14 @@
     def stage_first(g):
         p = lax.rem(g, 2)
 
-        @pl.when(g >= 3)
+        @pl.when(g >= depth)
         def _():
-            first_copy(g - 3).wait_send()
+            first_copy(g - depth).wait_send()
         core_copy(g).wait_recv()
         for f in range(2):
             for s in range(2):
                 yx = (1 - p) * (2 * s + f) + p * (2 * f + s)
-                first[lax.rem(g, 3), f, s] = (
+                first[lax.rem(g, depth), f, s] = (
                     whole[lax.rem(g, 2), core, yx].astype(jnp.float32)
                     + land_core[lax.rem(g, 4), yx].astype(jnp.float32)
                 ).astype(jnp.bfloat16)
@@ -195,13 +213,13 @@
         p = lax.rem(g, 2)
         mine = (1 - p) * xb + p * yb
 
-        @pl.when(g >= 3)
+        @pl.when(g >= depth)
         def _():
-            second_copy(g - 3).wait_send()
+            second_copy(g - depth).wait_send()
         first_copy(g).wait_recv()
         for s in range(2):
-            second[lax.rem(g, 3), s] = (
-                first[lax.rem(g, 3), mine, s].astype(jnp.float32) + land_first[g, s].astype(jnp.float32)
+            second[lax.rem(g, depth), s] = (
+                first[lax.rem(g, depth), mine, s].astype(jnp.float32) + land_first[g, s].astype(jnp.float32)
             ).astype(jnp.bfloat16)
         second_copy(g).start()
 
@@ -209,29 +227,29 @@
         p = lax.rem(g, 2)
         mine = (1 - p) * yb + p * xb
 
-        @pl.when(g >= 3)
+        @pl.when(g >= depth)
         def _():
-            for copy in last_copies(g - 3):
+            for copy in last_copies(g - depth):
                 copy.wait_send()
         second_copy(g).wait_recv()
-        summed = second[lax.rem(g, 3), mine].astype(jnp.float32) + land_second[g].astype(jnp.float32)
+        summed = second[lax.rem(g, depth), mine].astype(jnp.float32) + land_second[g].astype(jnp.float32)
         for k in range(nz):
             block = fold(summed[k * part : (k + 1) * part])
-            last[lax.rem(g, 3), k] = block
-            last_low[lax.rem(g, 3), k] = block.astype(jnp.bfloat16)
+            last[lax.rem(g, depth), k] = block
+            last_low[lax.rem(g, depth), k] = block.astype(jnp.bfloat16)
         for copy in last_copies(g):
             copy.start()
 
     def stage_out(g):
         for copy in last_copies(g):
             copy.wait_recv()
-        value = last[lax.rem(g, 3), z]
+        value = last[lax.rem(g, depth), z]
         for s in range(1, nz):
             value = value + land_last[g, s - 1].astype(jnp.float32)
         for k in range(folds):
             out_ref[g, :, pl.ds(k * low_width, low_width)] = value[k * part : (k + 1) * part]
 
-    lags = (0, 1, 3, 5, 7)
+    lags = REDUCE_LAGS
     prefetch(0)
 
     @pl.loop(0, total + lags[-1])
@@ -249,59 +267,72 @@
         def _():
             stage_core(i)
 
+        if between is not None:
+            between(i)
+
     for g in range(max(total - 2, 0), total):
         core_copy(g).wait_send()
-    for g in range(max(total - 3, 0), total):
+    for g in range(max(total - depth, 0), total):
         first_copy(g).wait_send()
         second_copy(g).wait_send()
         for copy in last_copies(g):
             copy.wait_send()
 
 
-def reduce_products(pairs, extras, row_count, width, low_shape, nz, collective_id):
-    bf, tokens = jnp.bfloat16, pairs[0][0].shape[0]
+def reduce_kernel(nz, row_count, width, jobs, extra_count, *refs):
+    reduce_program(nz, row_count, width, jobs, extra_count, refs)
+
+
+def reduce_setup(pairs, extras, row_count, width, low_shape, nz):
+    bf = jnp.bfloat16
+    xs, ys = ([a if isinstance(a, tuple) else (a, None) for a in side] for side in zip(*pairs))
+    tokens = xs[0][0].shape[-2]
     group, part = row_count // 8, row_count // 8 // nz
-    jobs = [(x.shape[1], y.shape[1]) for x, y in pairs]
-    total = sum(columns // width for _, columns in jobs)
-    extra_count = 0 if extras is None else extras.shape[0]
-    total += extra_count
+    jobs = [(x.shape[-1], y.shape[-1], i, j) for (x, i), (y, j) in zip(xs, ys)]
+    total = sum(job[1] // width for job in jobs) + extras.shape[0]
     low_rows, low_width = low_shape
     dma, reg = pltpu.SemaphoreType.DMA, pltpu.SemaphoreType.REGULAR
-    operands = [x for x, _ in pairs] + [y for _, y in pairs]
-    specs = [pl.BlockSpec(memory_space=pl.ANY)] * len(operands)
-    if extra_count:
-        operands.append(extras)
-        specs.append(pl.BlockSpec(memory_space=pltpu.VMEM))
+    operands = [x for x, _ in xs] + [y for y, _ in ys] + [extras]
+    scratch = [
+        pltpu.VMEM((2, tokens, row_count), bf),
+        pltpu.VMEM((2, tokens, width), bf),
+        pltpu.VMEM((2, 2, 4, group, width), bf),
+        pltpu.VMEM((4, 4, group, width), bf),
+        pltpu.VMEM((REDUCE_DEPTH, 2, 2, group, width), bf),
+        pltpu.VMEM((total, 2, group, width), bf),
+        pltpu.VMEM((REDUCE_DEPTH, 2, group, width), bf),
+        pltpu.VMEM((total, group, width), bf),
+        pltpu.VMEM((REDUCE_DEPTH, nz, low_rows, low_width), jnp.float32),
+        pltpu.VMEM((REDUCE_DEPTH, nz, low_rows, low_width), bf),
+        pltpu.VMEM((total, nz - 1, low_rows, low_width), bf),
+        dma((8,)),
+        dma((2, 2)), dma((2,)), dma((4,)), dma((REDUCE_DEPTH,)), dma((total,)), dma((REDUCE_DEPTH,)), dma((total,)),
+        dma((REDUCE_DEPTH, nz - 1)), dma((total, nz - 1)), reg,
+    ]
+    return (
+        (nz, row_count, width, jobs, extras.shape[0]),
+        operands,
+        [pl.BlockSpec(memory_space=pl.ANY)] * len(operands),
+        jax.ShapeDtypeStruct((total, part, width), jnp.float32),
+        scratch,
+    )
+
+
+def reduce_products(pairs, extras, row_count, width, low_shape, nz, collective_id):
+    static, operands, specs, shape, scratch = reduce_setup(pairs, extras, row_count, width, low_shape, nz)
     return pl.pallas_call(
-        functools.partial(rs_kernel, nz, row_count, width, jobs, extra_count),
-        out_shape=jax.ShapeDtypeStruct((total, part, width), jnp.float32),
+        functools.partial(reduce_kernel, *static),
+        out_shape=shape,
         in_specs=specs,
         out_specs=pl.BlockSpec(memory_space=pltpu.VMEM),
-        scratch_shapes=[
-            pltpu.VMEM((2, tokens, row_count), bf),
-            pltpu.VMEM((2, tokens, width), bf),
-            pltpu.VMEM((2, 2, 4, group, width), bf),
-            pltpu.VMEM((4, 4, group, width), bf),
-            pltpu.VMEM((3, 2, 2, group, width), bf),
-            pltpu.VMEM((total, 2, group, width), bf),
-            pltpu.VMEM((3, 2, group, width), bf),
-            pltpu.VMEM((total, group, width), bf),
-            pltpu.VMEM((3, nz, low_rows, low_width), jnp.float32),
-            pltpu.VMEM((3, nz, low_rows, low_width), bf),
-            pltpu.VMEM((total, nz - 1, low_rows, low_width), bf),
-            dma((2, 2)), dma((2,)), dma((4,)), dma((3,)), dma((total,)), dma((3,)), dma((total,)),
-            dma((3, nz - 1)), dma((total, nz - 1)), reg,
-        ],
+        scratch_shapes=scratch,
         compiler_params=pltpu.CompilerParams(
-            collective_id=collective_id, has_side_effects=True, vmem_limit_bytes=56 * 2**20
+            collective_id=collective_id, has_side_effects=True, vmem_limit_bytes=60 * 2**20
         ),
     )(*operands)
 
 
-def ag_kernel(nz, chunks, source_count, *refs):
-    sources, refs = refs[:source_count], refs[source_count:]
-    result_count = 1 + max(chunk[3] for chunk in chunks)
-    results, sems = refs[:result_count], refs[result_count:]
+def gather_program(nz, chunks, sources, results, sems):
     own_sem, last_send, last_recv, first_send, first_recv, second_send, second_recv, core_send, core_recv = sems
     dp, z = lax.axis_index("dp"), lax.axis_index("fsdp")
     core, xb, yb = lax.rem(dp, 2), lax.rem(dp // 2, 2), dp // 4
@@ -330,64 +361,81 @@
     def own(k):
         return pltpu.make_async_copy(source_of(k), result_of(k).at[yb, xb, core, z], own_sem.at[k])
 
-    def z_copies(k):
+    def to_z(k, source, target):
         return [
-            remote(source_of(k), result_of(k).at[yb, xb, core, z], last_send.at[k, s], last_recv.at[k, s], z_peers[s])
-            for s in range(nz - 1)
+            remote(source, target, last_send.at[k, s], last_recv.at[k, s], z_peers[s]) for s in range(nz - 1)
         ]
 
-    def first(k):
-        ref = result_of(k).at[yb, xb, core]
-        return remote(ref, ref, first_send.at[k], first_recv.at[k], y_peer if k % 2 else x_peer)
-
-    def second(k):
-        ref = result_of(k).at[:, xb, core] if k % 2 else result_of(k).at[yb, :, core]
-        return remote(ref, ref, second_send.at[k], second_recv.at[k], x_peer if k % 2 else y_peer)
+    def to_pair(k, late, along_y, source, target):
+        send, recv = (second_send, second_recv) if late else (first_send, first_recv)
+        return [remote(source, target, send.at[k], recv.at[k], y_peer if along_y else x_peer)]
+
+    def stage(k, number):
+        result = result_of(k)
+        block = result.at[yb, xb, core, z]
+        if number == 0:
+            return to_z(k, source_of(k), block)
+        if number == 1:
+            ref = result.at[yb, xb, core]
+            return to_pair(k, False, k % 2, ref, ref)
+        ref = result.at[:, xb, core] if k % 2 else result.at[yb, :, core]
+        return to_pair(k, True, 1 - k % 2, ref, ref)
 
     def across(k):
         ref = result_of(k).at[:, :, core]
         return remote(ref, ref, core_send.at[k], core_recv.at[k], core_peer)
 
     total = len(chunks)
-    for i in range(total + 6):
-        k = i - 6
-        if k >= 0:
-            second(k).wait_recv()
-            across(k).start()
-        k = i - 4
-        if 0 <= k < total:
-            first(k).wait_recv()
-            second(k).start()
-        k = i - 2
-        if 0 <= k < total:
+
+    def pass_on(k, number):
+        if number == 0:
             own(k).wait()
-            for copy in z_copies(k):
-                copy.wait_recv()
-            first(k).start()
+        for copy in stage(k, number):
+            copy.wait_recv()
+        for copy in stage(k, number + 1) if number < 2 else [across(k)]:
+            copy.start()
+
+    def step(i):
+        for number in (2, 1, 0):
+            if 0 <= i - 2 * (number + 1) < total:
+                pass_on(i - 2 * (number + 1), number)
         if i < total:
             own(i).start()
-            for copy in z_copies(i):
+            for copy in stage(i, 0):
                 copy.start()
-    for k in range(total):
-        for copy in z_copies(k) + [first(k), second(k), across(k)]:
-            copy.wait_send()
-        across(k).wait_recv()
+
+    def finish():
+        for k in range(total):
+            for copy in stage(k, 0) + stage(k, 1) + stage(k, 2) + [across(k)]:
+                copy.wait_send()
+            across(k).wait_recv()
+
+    return total + 6, step, finish
+
+
+def gather_sems(total, nz):
+    dma = pltpu.SemaphoreType.DMA
+    return [dma((total,)), dma((total, nz - 1)), dma((total, nz - 1))] + [dma((total,))] * 6
+
+
+def gather_kernel(nz, chunks, source_count, *refs):
+    sources, refs = refs[:source_count], refs[source_count:]
+    result_count = 1 + max(chunk[3] for chunk in chunks)
+    steps, step, finish = gather_program(nz, chunks, sources, refs[:result_count], refs[result_count:])
+    for i in range(steps):
+        step(i)
+    finish()
 
 
 def gather_rows(sources, chunks, shapes, nz, collective_id):
-    dma = pltpu.SemaphoreType.DMA
-    total = len(chunks)
     return pl.pallas_call(
-        functools.partial(ag_kernel, nz, chunks, len(sources)),
+        functools.partial(gather_kernel, nz, chunks, len(sources)),
         out_shape=[jax.ShapeDtypeStruct((2, 2, 2, nz, *shape), jnp.bfloat16) for shape in shapes],
         in_specs=[pl.BlockSpec(memory_space=pl.ANY)] * len(sources),
         out_specs=[pl.BlockSpec(memory_space=pl.ANY)] * len(shapes),
-        scratch_shapes=[
-            dma((total,)), dma((total, nz - 1)), dma((total, nz - 1)),
-            dma((total,)), dma((total,)), dma((total,)), dma((total,)), dma((total,)), dma((total,)),
-        ],
+        scratch_shapes=gather_sems(len(chunks), nz),
         compiler_params=pltpu.CompilerParams(
-            collective_id=collective_id, has_side_effects=True, vmem_limit_bytes=4 * 2**20
+            collective_id=collective_id, has_side_effects=True, vmem_limit_bytes=60 * 2**20
         ),
     )(*sources)
 
@@ -493,13 +541,14 @@
     return lax.broadcasted_iota(jnp.int32, (SEQ, 2 * HD), 1) < HD
 
 
-def forward_pieces(weights, entry, select_ref, mask_ref, hidden, kept, top_ref, need, leave):
+def forward_pieces(weights, entry, select_ref, mask_ref, hidden, kept, top_ref, gains_ref, need, leave):
     bf = jnp.bfloat16
     pieces = []
-    gain = lambda row: in_nt(select_ref[2 * SEQ :, :], entry[...])[row : row + 1, :]
+    gain = lambda row: gains_ref[row : row + 1, :]
 
     def start():
         need(entry)
+        gains_ref[...] = in_nt(select_ref[2 * SEQ :, :], entry[...])
         hidden[...] = in_nt(select_ref[:SEQ, :], entry[...])
     pieces.append(start)
 
@@ -580,10 +629,16 @@
     return pieces
 
 
-def forward_kernel(*refs):
+def forward_kernel(gather, *refs):
     entry_hbm, weight_hbm, (select_ref, mask_ref), refs = refs[0], refs[1:9], refs[9:11], refs[11:]
-    kept_hbm, (top_ref,), refs = refs[: len(KEPT)], refs[len(KEPT) : len(KEPT) + 1], refs[len(KEPT) + 1 :]
-    entry, weights, kept_refs, (hidden, weight_sem, kept_sem) = refs[0], refs[1:9], refs[9 : 9 + len(KEPT)], refs[9 + len(KEPT) :]
+    sources, refs = (refs[:1], refs[1:]) if gather else ((), refs)
+    kept_hbm, (top_ref, gains_ref), refs = refs[: len(KEPT)], refs[len(KEPT) : len(KEPT) + 2], refs[len(KEPT) + 2 :]
+    results = ()
+    if gather:
+        count = 1 + max(chunk[3] for chunk in gather[1])
+        results, refs = refs[:count], refs[count:]
+    entry, weights, kept_refs, refs = refs[0], refs[1:9], refs[9 : 9 + len(KEPT)], refs[9 + len(KEPT) :]
+    hidden, weight_sem, kept_sem = refs[:3]
     kept = {name: ref for (name, _, _), ref in zip(KEPT, kept_refs)}
     local = [(entry_hbm, entry)] + list(zip(weight_hbm, weights))
     fetches = {id(ref): pltpu.make_async_copy(hbm, ref, weight_sem.at[k]) for k, (hbm, ref) in enumerate(local)}
@@ -597,74 +652,153 @@
         copy.start()
         leaving.append(copy)
 
-    for piece in forward_pieces(
-        weights, entry, select_ref, mask_ref, hidden, kept, top_ref, lambda ref: fetches[id(ref)].wait(), leave
-    ):
-        piece()
+    steps = 0
+    if gather:
+        steps, step, finish = gather_program(*gather, sources, results, refs[3:])
+    pieces = forward_pieces(
+        weights, entry, select_ref, mask_ref, hidden, kept, top_ref, gains_ref, lambda ref: fetches[id(ref)].wait(), leave
+    )
+    for i in range(max(steps, len(pieces))):
+        if i < steps:
+            step(i)
+        if i < len(pieces):
+            pieces[i]()
+    if gather:
+        finish()
     for copy in leaving:
         copy.wait()
 
 
-def trunk_forward(entry, weights, select, mask):
+def trunk_forward(entry, weights, select, mask, gather=None, sources=(), shapes=(), collective_id=None):
     bf, f32 = jnp.bfloat16, jnp.float32
     vmem, hbm = pl.BlockSpec(memory_space=pltpu.VMEM), pl.BlockSpec(memory_space=pl.ANY)
-    shapes = [(2, SEQ, columns) for _, columns, _ in KEPT]
+    kept_shapes = [(2, SEQ, columns) for _, columns, _ in KEPT]
+    more = {} if gather is None else {"collective_id": collective_id, "has_side_effects": True}
     outs = pl.pallas_call(
-        forward_kernel,
-        out_shape=[jax.ShapeDtypeStruct(s, dtype) for s, (_, _, dtype) in zip(shapes, KEPT)]
-        + [jax.ShapeDtypeStruct((LAT, D), bf)],
-        in_specs=[hbm] * 9 + [vmem] * 2,
-        out_specs=[hbm] * len(KEPT) + [vmem],
+        functools.partial(forward_kernel, gather),
+        out_shape=[jax.ShapeDtypeStruct(s, dtype) for s, (_, _, dtype) in zip(kept_shapes, KEPT)]
+        + [jax.ShapeDtypeStruct((LAT, D), bf), jax.ShapeDtypeStruct((16, D), f32)]
+        + [jax.ShapeDtypeStruct((2, 2, 2, gather[0], *shape), bf) for shape in shapes],
+        in_specs=[hbm] * 9 + [vmem] * 2 + [hbm] * len(sources),
+        out_specs=[hbm] * len(KEPT) + [vmem] * 2 + [hbm] * len(shapes),
         scratch_shapes=[pltpu.VMEM(w.shape, bf) for w in [entry] + weights]
-        + [pltpu.VMEM(s, dtype) for s, (_, _, dtype) in zip(shapes, KEPT)]
-        + [pltpu.VMEM((SEQ, D), f32), pltpu.SemaphoreType.DMA((9,)), pltpu.SemaphoreType.DMA((2, len(KEPT)))],
-        compiler_params=pltpu.CompilerParams(vmem_limit_bytes=60 * 2**20),
-    )(entry, *weights, select, mask)
-    return outs[-1], outs[:-1]
-
-
-def backward_pieces(layer, weights, gain, mask_ref, hidden, middle, kept, back, gain_grad, need, leave):
+        + [pltpu.VMEM(s, dtype) for s, (_, _, dtype) in zip(kept_shapes, KEPT)]
+        + [pltpu.VMEM((SEQ, D), f32), pltpu.SemaphoreType.DMA((9,)), pltpu.SemaphoreType.DMA((2, len(KEPT)))]
+        + ([] if gather is None else gather_sems(len(gather[1]), gather[0])),
+        compiler_params=pltpu.CompilerParams(vmem_limit_bytes=60 * 2**20, **more),
+    )(entry, *weights, select, mask, *sources)
+    count = len(KEPT)
+    return outs[count], outs[count + 1], outs[:count], outs[count + 2 :]
+
+
+BACK_KEPT = ("packed", "inner", "norm_one", "norm_two", "inv_one", "inv_two")
+
+
+def backward_pieces(refs):
+    weight_hbm, (gains_ref, select_ref, mask_ref, top_ref), refs = refs[:8], refs[8:12], refs[12:]
+    kept_hbm, refs = refs[: len(BACK_KEPT)], refs[len(BACK_KEPT) :]
+    back_hbm, small_ref, refs = refs[: len(BACK)], refs[len(BACK)], refs[len(BACK) + 1 :]
+    buffers, kept_refs, refs = refs[:2], refs[2 : 2 + len(BACK_KEPT)], refs[2 + len(BACK_KEPT) :]
+    back_refs, (mixed, hidden, middle, decoder, gain_grad, weight_sem, kept_sem, back_sem) = refs[: len(BACK)], refs[len(BACK) :]
     bf = jnp.bfloat16
-    w_qkv, w_out, w_up, w_down = weights
-    pieces = []
+    back = {name: ref for (name, _), ref in zip(BACK, back_refs)}
+    kept = {name: ref for name, ref in zip(BACK_KEPT, kept_refs)}
+    places = []
+    for layer in (1, 0):
+        turn = 1 - layer
+        places += [
+            (turn, 0, FF, 4 * layer + 3), (1 - turn, 0, FF, 4 * layer + 2),
+            (turn, 0, D, 4 * layer + 1), (turn, D, 3 * D, 4 * layer),
+        ]
+    place_of = {place[3]: k for k, place in enumerate(places)}
+
+    def view(weight):
+        buffer, column, columns, _ = places[place_of[weight]]
+        return buffers[buffer].at[:, pl.ds(column, columns)]
+
+    def fetch(weight):
+        return pltpu.make_async_copy(weight_hbm[weight], view(weight), weight_sem.at[weight])
+
+    def fetch_kept(layer, name):
+        k = BACK_KEPT.index(name)
+        return pltpu.make_async_copy(kept_hbm[k].at[layer], kept_refs[k], kept_sem.at[k])
+
+    def leave(layer, name):
+        k = [n for n, _ in BACK].index(name)
+        return pltpu.make_async_copy(back_refs[k], back_hbm[k].at[layer], back_sem.at[k])
+
+    def gain(row):
+        return gains_ref[row : row + 1, :]
 
     def norm_step(upstream, n, inv):
         return inv * (
             upstream - jnp.mean(upstream, -1, keepdims=True) - n * jnp.mean(upstream * n, -1, keepdims=True)
         )
 
-    def branch():
+    def begin():
+        fetch(7).start()
+        fetch_kept(1, "inner").start()
+        fetch(6).start()
+        for name in ("norm_two", "inv_two", "packed", "norm_one", "inv_one"):
+            fetch_kept(1, name).start()
+        hidden[...] = top_ref[...]
+        gain_grad[...] = jnp.zeros_like(gain_grad)
+
+    def branch(layer):
+        if layer == 0:
+            leave(1, "back_branch").wait()
         back["back_branch"][...] = hidden[...].astype(bf)
-        leave("back_branch")
-        need(w_down, "inner")
-
-    def widen(part, parts):
+        leave(layer, "back_branch").start()
+        fetch(4 * layer + 3).wait()
+        fetch_kept(layer, "inner").wait()
+        if layer == 0:
+            leave(1, "back_inner").wait()
+
+    def widen(layer, part, parts):
         columns = slice(part * FF // parts, (part + 1) * FF // parts)
-        up = in_nn(back["back_branch"][...], w_down[:, columns])
+        up = in_nn(back["back_branch"][...], view(4 * layer + 3)[:, columns])
         x = kept["inner"][:, columns]
         t = jnp.tanh(GELU_SCALE * (x + 0.044715 * x * x * x))
         slope = 0.5 * (1.0 + t) + 0.5 * x * (1.0 - t * t) * (GELU_SCALE * (1.0 + 3.0 * 0.044715 * x * x))
         back["back_inner"][:, columns] = (slope * up).astype(bf)
 
-    def narrow():
-        leave("back_inner")
-        need(w_up, "norm_two", "inv_two")
-        value = in_nt(back["back_inner"][...], w_up[...])
+    def narrow(layer):
+        fetch(4 * layer + 1).start()
+        fetch(4 * layer).start()
+        if layer == 1:
+            fetch_kept(0, "inner").start()
+        leave(layer, "back_inner").start()
+        fetch(4 * layer + 2).wait()
+        fetch_kept(layer, "norm_two").wait()
+        fetch_kept(layer, "inv_two").wait()
+        middle[...] = in_nt(back["back_inner"][...], view(4 * layer + 2)[...])
+
+    def renorm(layer):
+        value = middle[...]
         n = kept["norm_two"][...]
         gain_grad[2 * layer + 1 : 2 * layer + 2, :] = jnp.sum(value * n, 0, keepdims=True)
         middle[...] = hidden[...] + norm_step(value * gain(2 * layer + 1), n, kept["inv_two"][:, :1])
+        if layer == 0:
+            leave(1, "back_attn").wait()
         back["back_attn"][...] = middle[...].astype(bf)
-        leave("back_attn")
-
-    def unmix():
-        need(w_out, "packed")
-        back["mixed"][...] = in_nt(back["back_attn"][...], w_out[...]).astype(bf)
-
-    def attend(pair):
+        leave(layer, "back_attn").start()
+        if layer == 1:
+            fetch(3).start()
+            fetch_kept(0, "norm_two").start()
+            fetch_kept(0, "inv_two").start()
+
+    def unmix(layer):
+        fetch(4 * layer + 1).wait()
+        fetch_kept(layer, "packed").wait()
+        if layer == 0:
+            leave(1, "back_packed").wait()
+        mixed[...] = in_nt(back["back_attn"][...], view(4 * layer + 1)[...]).astype(bf)
+
+    def attend(layer, pair):
         low = low_half()
         at = lambda k: slice(k * D + pair * 2 * HD, k * D + (pair + 1) * 2 * HD)
         q, k, v = (kept["packed"][:, at(i)] for i in range(3))
-        up = back["mixed"][:, at(0)]
+        up = mixed[:, at(0)]
         zero = jnp.zeros((), bf)
         parts = []
         for side in range(2):
@@ -682,130 +816,108 @@
         for i in range(3):
             back["back_packed"][:, at(i)] = jnp.where(low, parts[0][i], parts[1][i]).astype(bf)
 
-    def close():
-        leave("back_packed")
-        need(w_qkv, "norm_one", "inv_one")
-        value = in_nt(back["back_packed"][...], w_qkv[...])
+    def close(layer):
+        leave(layer, "back_packed").start()
+        fetch(4 * layer).wait()
+        fetch_kept(layer, "norm_one").wait()
+        fetch_kept(layer, "inv_one").wait()
+        value = in_nt(back["back_packed"][...], view(4 * layer)[...])
         n = kept["norm_one"][...]
         gain_grad[2 * layer : 2 * layer + 1, :] = jnp.sum(value * n, 0, keepdims=True)
         hidden[...] = middle[...] + norm_step(value * gain(2 * layer), n, kept["inv_one"][:, :1])
-
-    pieces.append(branch)
-    for part in range(3):
-        pieces.append(functools.partial(widen, part, 3))
-    pieces += [narrow, unmix]
-    for pair in range(HEADS // 2):
-        pieces.append(functools.partial(attend, pair))
-    pieces.append(close)
-    return pieces
-
-
-BACK_KEPT = ("packed", "inner", "norm_one", "norm_two", "inv_one", "inv_two")
-
-
-def backward_kernel(*refs):
-    entry_ref, weight_hbm, (select_ref, mask_ref, top_ref), refs = refs[0], refs[1:9], refs[9:12], refs[12:]
-    kept_hbm, refs = refs[: len(BACK_KEPT)], refs[len(BACK_KEPT) :]
-    back_hbm, small_ref, refs = refs[: len(BACK)], refs[len(BACK)], refs[len(BACK) + 1 :]
-    weights, refs = refs[:4], refs[4:]
-    kept_refs, refs = refs[: len(BACK_KEPT)], refs[len(BACK_KEPT) :]
-    back_refs, (mixed, hidden, middle, decoder, gain_grad, weight_sem, kept_sem, back_sem) = refs[: len(BACK)], refs[len(BACK) :]
-    bf = jnp.bfloat16
-    gains = lambda row: in_nt(select_ref[2 * SEQ :, :], entry_ref[...])[row : row + 1, :]
-    hidden[...] = top_ref[...]
-    gain_grad[...] = jnp.zeros_like(gain_grad)
-    back = {name: ref for (name, _), ref in zip(BACK, back_refs)}
-    back["mixed"] = mixed
-    order = [3, 2, 1, 0]
-    kept_order = {3: ["inner"], 2: ["norm_two", "inv_two"], 1: ["packed"], 0: ["norm_one", "inv_one"]}
-
-    def fetches(layer):
-        moves = {}
-        for k in order:
-            moves[id(weights[k])] = pltpu.make_async_copy(weight_hbm[4 * layer + k], weights[k], weight_sem.at[k])
-            for name in kept_order[k]:
-                i = BACK_KEPT.index(name)
-                moves[name] = pltpu.make_async_copy(kept_hbm[i].at[layer], kept_refs[i], kept_sem.at[i])
-        return moves
-
-    moves = fetches(1)
-    for copy in moves.values():
-        copy.start()
-    for layer in (1, 0):
-        leaving = []
-
-        def need(*names):
-            for name in names:
-                moves[name if isinstance(name, str) else id(name)].wait()
-
-        def leave(name):
-            k = [n for n, _ in BACK].index(name)
-            copy = pltpu.make_async_copy(back_refs[k], back_hbm[k].at[layer], back_sem.at[k])
-            copy.start()
-            leaving.append(copy)
-
-        later = fetches(0) if layer == 1 else {}
-        kept = {name: ref for name, ref in zip(BACK_KEPT, kept_refs)}
-        for piece in backward_pieces(
-            layer, weights, gains, mask_ref, hidden, middle, kept, back, gain_grad, need, leave
-        ):
-            piece()
-            if layer == 1:
-                name = getattr(piece, "__name__", "")
-                if name == "narrow":
-                    free = [id(weights[3]), "inner", id(weights[2]), "norm_two", "inv_two"]
-                elif name == "unmix":
-                    free = [id(weights[1])]
-                elif name == "close":
-                    free = ["packed", id(weights[0]), "norm_one", "inv_one"]
-                else:
-                    free = []
-                for key in free:
-                    later[key].start()
-        for copy in leaving:
-            copy.wait()
         if layer == 1:
-            moves = later
+            fetch(2).start()
+            for name in ("packed", "norm_one", "inv_one"):
+                fetch_kept(0, name).start()
             decoder[...] = hidden[...].astype(bf)
             keep = jnp.transpose(jnp.broadcast_to(mask_ref[...], (128, SEQ)))[:, :1]
             hidden[...] = hidden[...] * keep
-    small_ref[...] = (
-        in_tn(hidden[...].astype(bf), select_ref[:SEQ, :])
-        + in_tn(decoder[...], select_ref[SEQ : 2 * SEQ, :])
-        + in_tn(gain_grad[...].astype(bf), select_ref[2 * SEQ :, :])
-    ).astype(bf)
-
-
-def trunk_backward(entry, weights, select, mask, back_top, kept):
+
+    def small():
+        hidden_low = hidden[...].astype(bf)
+        small_ref[...] = (
+            in_tn(hidden_low, select_ref[:SEQ, :])
+            + in_tn(decoder[...], select_ref[SEQ : 2 * SEQ, :])
+            + in_tn(gain_grad[...].astype(bf), select_ref[2 * SEQ :, :])
+        ).astype(bf)
+        for name, _ in BACK:
+            leave(0, name).wait()
+
+    pieces = [begin]
+    for layer in (1, 0):
+        pieces.append(functools.partial(branch, layer))
+        for part in range(3):
+            pieces.append(functools.partial(widen, layer, part, 3))
+        pieces += [functools.partial(f, layer) for f in (narrow, renorm, unmix)]
+        for pair in range(HEADS // 2):
+            pieces.append(functools.partial(attend, layer, pair))
+        pieces.append(functools.partial(close, layer))
+    pieces.append(small)
+    return pieces
+
+
+def backward_kernel(reduction, operand_count, *refs):
+    fixed = 12 + len(BACK_KEPT)
+    results = len(BACK) + 1
+    if reduction is None:
+        for piece in backward_pieces(refs):
+            piece()
+        return
+    mine, refs = refs[:fixed], refs[fixed:]
+    operands, refs = refs[:operand_count], refs[operand_count:]
+    mine, refs = mine + refs[:results], refs[results:]
+    summed, refs = refs[0], refs[1:]
+    count = 2 + len(BACK_KEPT) + len(BACK) + 8
+    pieces = backward_pieces(mine + refs[:count])
+    chunks = summed.shape[0]
+    start = 0
+    per_turn = -(-len(pieces) // (chunks - start))
+
+    def between(i):
+        for turn in range(-(-len(pieces) // per_turn)):
+            @pl.when(i == start + turn)
+            def _():
+                for piece in pieces[turn * per_turn : (turn + 1) * per_turn]:
+                    piece()
+
+    reduce_program(*reduction, operands + (summed,) + refs[count:], between)
+
+
+def trunk_backward(gains, weights, select, mask, back_top, kept, reduction=None, collective_id=None):
     bf, f32 = jnp.bfloat16, jnp.float32
     vmem, hbm = pl.BlockSpec(memory_space=pltpu.VMEM), pl.BlockSpec(memory_space=pl.ANY)
     kept_in = [kept[KEPT_INDEX[name]] for name in BACK_KEPT]
+    static, operands, specs, shape, scratch = reduction or (None, [], [], None, [])
+    more = {} if reduction is None else {"collective_id": collective_id, "has_side_effects": True}
     outs = pl.pallas_call(
-        backward_kernel,
+        functools.partial(backward_kernel, static, len(operands)),
         out_shape=[jax.ShapeDtypeStruct((2, SEQ, columns), bf) for _, columns in BACK]
-        + [jax.ShapeDtypeStruct((D, TRUNK_WIDTH), bf)],
-        in_specs=[vmem] + [hbm] * 8 + [vmem] * 3 + [hbm] * len(BACK_KEPT),
-        out_specs=[hbm] * len(BACK) + [vmem],
-        scratch_shapes=[pltpu.VMEM(w.shape, bf) for w in weights[:4]]
+        + [jax.ShapeDtypeStruct((D, TRUNK_WIDTH), bf)]
+        + ([] if reduction is None else [shape]),
+        in_specs=[hbm] * 8 + [vmem] * 4 + [hbm] * len(BACK_KEPT) + specs,
+        out_specs=[hbm] * len(BACK) + [vmem] * (1 if reduction is None else 2),
+        scratch_shapes=[pltpu.VMEM((D, FF), bf)] * 2
         + [pltpu.VMEM(a.shape[1:], a.dtype) for a in kept_in]
         + [pltpu.VMEM((SEQ, columns), bf) for _, columns in BACK]
         + [
             pltpu.VMEM((SEQ, D), bf), pltpu.VMEM((SEQ, D), f32), pltpu.VMEM((SEQ, D), f32), pltpu.VMEM((SEQ, D), bf),
             pltpu.VMEM((16, D), f32),
-            pltpu.SemaphoreType.DMA((4,)), pltpu.SemaphoreType.DMA((len(BACK_KEPT),)),
+            pltpu.SemaphoreType.DMA((8,)), pltpu.SemaphoreType.DMA((len(BACK_KEPT),)),
             pltpu.SemaphoreType.DMA((len(BACK),)),
-        ],
-        compiler_params=pltpu.CompilerParams(vmem_limit_bytes=60 * 2**20),
-    )(entry, *weights, select, mask, back_top, *kept_in)
-    back = dict(zip([name for name, _ in BACK], outs[:-1]))
+        ]
+        + scratch,
+        compiler_params=pltpu.CompilerParams(vmem_limit_bytes=60 * 2**20, **more),
+    )(*weights, gains, select, mask, back_top, *kept_in, *operands)
+    back = dict(zip([name for name, _ in BACK], outs))
     pairs = []
     for layer in range(2):
-        part = lambda name: kept[KEPT_INDEX[name]][layer]
+        left = lambda name: (kept[KEPT_INDEX[name]], layer)
+        right = lambda name: (back[name], layer)
         pairs += [
-            (part("normed"), back["back_packed"][layer]), (part("mixed"), back["back_attn"][layer]),
-            (part("second"), back["back_inner"][layer]), (back["back_branch"][layer], part("upper")),
+            (left("normed"), right("back_packed")), (left("mixed"), right("back_attn")),
+            (left("second"), right("back_inner")), (right("back_branch"), left("upper")),
         ]
-    return pairs, outs[-1]
+    return pairs, outs[len(BACK)], outs[len(BACK) + 1 :]
 
 
 ROWS_AT_ONCE = 192
@@ -1202,8 +1314,17 @@
     bf = jnp.bfloat16
 
     low_blocks = block_weights.astype(bf)
+    local_total = jnp.sum(mask_counts)
+    terms, rest = [local_total.astype(bf)], jnp.sum(loss_weights)
+    for _ in range(3):
+        terms.append(lax.reduce_precision(rest, 8, 7).astype(bf))
+        rest = rest - terms[-1].astype(jnp.float32)
     low_entry = jnp.concatenate(
-        [entry_table.T.astype(bf), block_gains.reshape(4, r0).T.astype(bf), jnp.zeros((r0, 108), bf)], 1
+        [
+            entry_table.T.astype(bf), block_gains.reshape(4, r0).T.astype(bf),
+            jnp.broadcast_to(jnp.stack(terms), (r0, 4)), jnp.zeros((r0, 104), bf),
+        ],
+        1,
     )
     low_head = head_weights.astype(bf)
     edge = head_edges.T.astype(bf)
@@ -1216,23 +1337,21 @@
         1,
     )
     chunks, shapes = gather_plan(
-        [(1, None, r0, (TRUNK_WIDTH,)), (0, 0, r0, TRUNK_PARTS), (0, 1, r0, TRUNK_PARTS), (2, None, r1, EDGE_PARTS)],
-        TRUNK_WIDTH,
-    )
-    sources = [low_blocks, low_entry, low_edges]
+        [(1, None, r0, (TRUNK_WIDTH,)), (0, 0, r0, TRUNK_PARTS), (0, 1, r0, TRUNK_PARTS)], TRUNK_WIDTH
+    )
+    later = [(0, None, r1, EDGE_PARTS)]
+    edge_chunks, edge_shapes = gather_plan(later, HEAD_WIDTH)
+    whole = lambda arrays: [a.reshape(devices * a.shape[4], -1) for a in arrays]
     if direct:
-        gathered = [a.reshape(devices * a.shape[4], -1) for a in gather_rows(sources, chunks, shapes, nz, 1)]
+        trunk = whole(gather_rows([low_blocks, low_entry], chunks, shapes, nz, 1))
     else:
-        gathered = plain_gather(sources, chunks, shapes)
-    trunk, edge_mats = gathered[:9], gathered[9:]
+        trunk = plain_gather([low_blocks, low_entry], chunks, shapes)
+        edge_mats = plain_gather([low_edges], edge_chunks, edge_shapes)
     head_blocks = [lax.all_gather(low_head[b], AXES, axis=0, tiled=True) for b in range(HB)]
 
-    local_total = jnp.sum(mask_counts)
-    early = exchange(
-        jnp.stack([local_total.astype(jnp.float32), jnp.sum(loss_weights)]), dp_count, nz, 3
-    )
+    early = trunk[0][::r0, 2 * SEQ + CH + 4 : 2 * SEQ + CH + 8].astype(jnp.float32)
     counts = early[:, 0].astype(jnp.int32)
-    weight_total = jnp.sum(early[:, 1])
+    weight_total = jnp.sum(early[:, 1:])
     count_ends = jnp.cumsum(counts)
     count_starts = count_ends - counts
     offset = jnp.sum(jnp.where(jnp.arange(devices) == me, count_starts, 0))
@@ -1248,7 +1367,13 @@
     select = (pick_rows[:, None] == columns[None, :]).astype(bf) + jnp.pad(
         clean, ((BUF, SEQ + 16), (2 * SEQ, TRUNK_WIDTH - 2 * SEQ - CH))
     )
-    top_rows, kept = trunk_forward(trunk[0], trunk[1:9], select, key_keep[None])
+    if direct:
+        top_rows, gains, kept, edge_mats = trunk_forward(
+            trunk[0], trunk[1:9], select, key_keep[None], (nz, edge_chunks), [low_edges], edge_shapes, 2
+        )
+        edge_mats = whole(edge_mats)
+    else:
+        top_rows, gains, kept, _ = trunk_forward(trunk[0], trunk[1:9], select, key_keep[None])
 
     capacity = (LAT + devices - 1) // devices
     slots = devices * capacity
@@ -1308,26 +1433,28 @@
     head_small = jnp.concatenate(
         [grad_cond_t, grad_time_one_t, grad_in_t, grad_out_t, bias_t, jnp.zeros((HW, 465), jnp.float32)], 1
     ).astype(bf)
-    small_columns = head_small.shape[1]
+    returning = dot_left(place, back_tokens.astype(bf)).astype(bf)
+    returned = lax.all_to_all(
+        returning.reshape(devices, capacity, D), AXES, split_axis=0, concat_axis=0, tiled=True
+    ).reshape(slots, D)
+    back_top = jnp.concatenate([jnp.zeros((BUF, D), jnp.float32), dot_left(pick, returned)], 0)
+    reduction = None
     if direct:
         extras = jnp.stack(
-            [head_small[:, k : k + HEAD_WIDTH] for k in range(0, small_columns, HEAD_WIDTH)]
+            [head_small[:, k : k + HEAD_WIDTH] for k in range(0, head_small.shape[1], HEAD_WIDTH)]
         )
-        tall = reduce_products(head_pairs, extras, HW, HEAD_WIDTH, (r1, HEAD_WIDTH), nz, 4)
-        tall = tall.transpose(1, 0, 2).reshape(r1, -1)
+        reduction = reduce_setup(head_pairs, extras, HW, HEAD_WIDTH, (r1, HEAD_WIDTH), nz)
+    trunk_pairs, trunk_small, tall = trunk_backward(
+        gains, trunk[1:9], select, key_keep[None], back_top, kept, reduction, 4
+    )
+    if direct:
+        tall = tall[0].transpose(1, 0, 2).reshape(r1, -1)
     else:
         tall = jnp.concatenate(
             [scatter_sum(dot_left(x, y)) for x, y in head_pairs]
             + [scatter_sum(head_small.astype(jnp.float32))],
             1,
         )
-
-    returning = dot_left(place, back_tokens.astype(bf)).astype(bf)
-    returned = lax.all_to_all(
-        returning.reshape(devices, capacity, D), AXES, split_axis=0, concat_axis=0, tiled=True
-    ).reshape(slots, D)
-    back_top = jnp.concatenate([jnp.zeros((BUF, D), jnp.float32), dot_left(pick, returned)], 0)
-    trunk_pairs, trunk_small = trunk_backward(trunk[0], trunk[1:9], select, key_keep[None], back_top, kept)
     if direct:
         wide = reduce_products(
             trunk_pairs, trunk_small[None], D, TRUNK_WIDTH, (2 * r0, TRUNK_WIDTH // 2), nz, 5
@@ -1335,7 +1462,7 @@
         wide = wide.transpose(1, 0, 2).reshape(r0, -1)
     else:
         wide = jnp.concatenate(
-            [scatter_sum(dot_left(x, y)) for x, y in trunk_pairs]
+            [scatter_sum(dot_left(x[0][x[1]], y[0][y[1]])) for x, y in trunk_pairs]
             + [scatter_sum(trunk_small.astype(jnp.float32))],
             1,
         )

time: 841 us -> 803 us (0.955)
  local copies, waits for them, and re-layouts: 54.6 us -> 22.5 us
  Pallas kernels: 700 us -> 678 us
    unnamed x111 -> x71, local copies, waits for them, and re-layouts: 27.7 us -> 1.51 us
    squeeze x8 -> x0, local copies, waits for them, and re-layouts: 13.6 us -> none  [the longest x4 5.23 us: trunk_backward(): part = lambda name: kept[KEPT_INDEX[name]][layer]]
    pallas_call x2 -> x1, Pallas kernels: 21.9 us -> 9.39 us  [exchange(): pl.pallas_call(functools.partial(exchange_kernel, dp_count, nz), out_shap...]
    pallas_call x5 -> x4, Pallas kernels: 598 us -> 589 us  [the longest x1 180 us: gather_rows(): pl.pallas_call(functools.partial(gather_kernel, nz, chunks, len(sources))...]
  transfers between devices with their start and end apart: 4 -> 4, of which waited for: 2 -> 2; matrix products, arithmetic and copies ran while one was open for 3% -> 4% of each run, Pallas kernels for 33% -> 34%
where the time goes in v3:
time: 803 us; the launch traced here: 794 us
  Pallas kernels  678 us (84%)
  other arithmetic  38.9 us (5%)
  between operations  23.6 us (3%)
  local copies, waits for them, and re-layouts  22.5 us (3%)
  waiting for transfers between devices  13 us (2%)
  matrix products  9.01 us (1%)
  starting transfers between devices  8.65 us (1%)
    pallas_call x1, Pallas kernels, gather_rows(): pl.pallas_call(functools.partial(gather_kernel, nz, chunks, len(sources))...  180 us
    pallas_call x1, Pallas kernels, trunk_backward(): pl.pallas_call(functools.partial(backward_kernel, static, len(operands)),...  178 us
    pallas_call x1, Pallas kernels, reduce_products(): pl.pallas_call(functools.partial(reduce_kernel, *static), out_shape=shape...  139 us
    pallas_call x1, Pallas kernels, trunk_forward(): pl.pallas_call(functools.partial(forward_kernel, gather), out_shape=[jax....  92.3 us
    pallas_call x1, Pallas kernels, head_pass(): pl.pallas_call(functools.partial(head_kernel, tokens), out_shape=[jax.Sha...  79.5 us
  transfers between devices with their start and end apart: 4, of which 2 were waited for; matrix products, arithmetic and copies ran while one was open for 4% of the time, Pallas kernels for 34%

profile of v3, /device:TPU:0, one launch (start us, length us, event | category | flops | bytes accessed | tf_op | source)
XLA Modules:
  0.0 793.5 jit_solution(8719590320891001857)
XLA Ops:
  7.2 1.4 convert_element_type.154
  17.3 2.0 pad_maximum_fusion.3
  20.0 179.9 %shard_map.391 = (bf16[2,2,2,4,24,768]{5,4,3,2,1,0:T(8,128)(2,1)}, bf16[2,2,2,4,24,2304]{5,4,3,2,1,0:T(8,128)(2,1)}, bf16[2,2,2,4,24,768]{5,4,3,2,1,0:T(8,128)(2...) custom-call(bf16[2,24,9216]{2,1,0:T(8,128)(2,1)} %convert_element_ty, ...), custom_call_target="tpu_custom_call" | custom-call | tf_op jit(solution)/shard_map/pallas_call | solution.py:431
  205.8 92.3 %shard_map.392 = (bf16[2,320,768]{2,1,0:T(8,128)(2,1)}, bf16[2,320,2304]{2,1,0:T(8,128)(2,1)}, bf16[2,320,768]{2,1,0:T(8,128)(2,1)}, bf16[2,320,768]{2,1,0:T(8,1...) custom-call(bf16[768,768]{1,0:T(8,128)(2,1)} %bitcast.206, ...), custom_call_target="tpu_custom_call" | custom-call | tf_op jit(solution)/shard_map/pallas_call | solution.py:677
  299.0 2.1 fusion.6
  301.2 4.6 all-to-all-start
  309.1 1.7 fusion.16
  313.0 5.8 all-to-all-done
  323.5 79.5 %shard_map.393 = (bf16[4,192,3072]{2,1,0:T(8,128)(2,1)}, bf16[4,192,1024]{2,1,0:T(8,128)(2,1)}, bf16[4,192,1024]{2,1,0:T(8,128)(2,1)}, bf16[4,192,1024]{2,1,0:T(...) custom-call(bf16[4,192,256]{2,1,0:T(8,128)(2,1)} %pad_maximum_fusion, ...), custom_call_target="tpu_custom_call" | custom-call | tf_op jit(solution)/shard_map/pallas_call | solution.py:1207
  403.1 1.7 convolution_convert_fusion
  408.7 4.0 all-to-all-start.1
  413.3 2.0 convolution_bitcast_fusion.1
  415.9 2.0 pad_maximum_fusion.refs_36_
  418.0 6.5 all-to-all-done.1
  425.9 177.6 %shard_map.394 = (bf16[2,320,2304]{2,1,0:T(8,128)(2,1)}, bf16[2,320,768]{2,1,0:T(8,128)(2,1)}, bf16[2,320,3072]{2,1,0:T(8,128)(2,1)}, bf16[2,320,768]{2,1,0:T(8,...) custom-call(bf16[768,2304]{1,0:T(8,128)(2,1)} %bitcast.166, bf16[768,768]{1,0:T(8,128)(2,1)} %bitcast.184, ...), custom_call_target="tpu_custom_call" | custom-call | tf_op jit(solution)/shard_map/pallas_call | solution.py:892
  603.5 1.8 copy.97
  608.5 139.2 %shard_map.395 = f32[25,24,768]{2,1,0:T(8,128)} custom-call(bf16[2,320,768]{2,1,0:T(8,128)(2,1)} %get-tuple-element.86.refs_0_.refs_4_, bf16[2,320,768]{2,1,0:T(8,128)(2,1)} %get-tuple-element.87.refs_1_.refs_5_, bf16[2,320,768]{2,1,0:T(8,128)(2,1)} %get-tuple-element.88.refs_2_.refs_6_, bf16[2,320,768]{2,1,0:T(8,128)(2,1)} %get-tuple-element.125.refs_3_.refs_7_, ...), custom_call_target="tpu_custom_call" | custom-call | tf_op jit(solution)/shard_map/pallas_call | solution.py:323
  747.7 2.7 fusion.2
  752.4 9.4 %shard_map.396 = f32[32,8,128]{2,1,0:T(8,128)S(1)} custom-call(f32[8,128]{1,0:T(8,128)S(1)} %broadcast_in_dim.88.in_ref), custom_call_target="tpu_custom_call" | custom-call | tf_op jit(solution)/shard_map/pallas_call | solution.py:483
  769.8 1.7 multiply_subtract_fusion.3
  771.4 1.9 concatenate.42
  773.4 3.1 multiply_subtract_fusion.2
  777.8 4.1 multiply_subtract_fusion.1
  782.0 3.4 multiply_subtract_fusion
  (180 shorter events, 39.4 us)
Async XLA Ops:
  7.2 314.5 %all-gather.5.cloned.1.call-start = ((), (), s32[]{:S(2)}) async-start(), calls=%async_computation.2 | async-start | bytes 10813440 | tf_op jit(solution)/shard_map/all_gather | solution.py:1350
  8.7 7.4 copy-start.24
  8.7 7.5 copy-start.4
  9.6 312.1 %all-gather.7.cloned.1.call-start = ((), (), s32[]{:S(2)}) async-start(), calls=%async_computation.3 | async-start | bytes 10813440 | tf_op jit(solution)/shard_map/all_gather | solution.py:1350
  10.4 8.9 %copy-start.12 = (f32[656,24]{0,1:T(8,128)S(1)}, f32[656,24]{0,1:T(8,128)}, u32[]{:S(2)}) copy-start(f32[656,24]{0,1:T(8,128)} %param.32) | copy-start | bytes 188932
  16.2 186.4 %copy-start.28 = (s32[1,256]{1,0:T(1,128)S(1)}, s32[1,256]{1,0:T(1,128)}, u32[]{:S(2)}) copy-start(s32[1,256]{1,0:T(1,128)} %param.25) | copy-start | bytes 3076
  16.2 187.2 %copy-start.19 = (f32[3,160]{1,0:T(4,128)S(1)}, f32[3,160]{1,0:T(4,128)}, u32[]{:S(2)}) copy-start(f32[3,160]{1,0:T(4,128)} %param.34) | copy-start | bytes 5764
  16.2 187.4 %copy-start.23 = (bf16[1,256,16]{1,2,0:T(8,128)(2,1)S(1)}, bf16[1,256,16]{1,2,0:T(8,128)(2,1)}, u32[]{:S(2)}) copy-start(bf16[1,256,16]{1,2,0:T(8,128)(2,1)} %param.24) | copy-start | bytes 24580
  298.1 7.6 copy-start.7
  298.2 7.9 copy-start.16
  301.2 7.9 copy-start.18
  301.2 17.7 %all-to-all-start = ((bf16[32,8,896]{2,1,0:T(8,128)(2,1)}), bf16[32,8,896]{2,1,0:T(8,128)(2,1)S(1)}, u32[]{:S(2)}, u32[]{:S(2)}) async-start(bf16[32,8,896]{2,1,0:T(8,128)(2,1)} %fusion.6), calls=%async_computation | async-start | bytes 917504 | tf_op jit(solution)/shard_map/all_to_all | solution.py:1391
  306.1 6.2 copy-start.31
  406.9 5.7 copy-start.15
  406.9 6.4 copy-start.34
  408.7 15.8 %all-to-all-start.1 = ((bf16[32,8,768]{2,1,0:T(8,128)(2,1)}), bf16[32,8,768]{2,1,0:T(8,128)(2,1)S(1)}, u32[]{:S(2)}, u32[]{:S(2)}) async-start(bf16[32,8,768]{2,1,0:T(8,128)(2,1)} %fusion.7), calls=%async_computation.1 | async-start | bytes 786432 | tf_op jit(solution)/shard_map/all_to_all | solution.py:1437
  747.7 18.3 %copy-start = (f32[25,24,768]{2,1,0:T(8,128)S(1)}, f32[25,24,768]{2,1,0:T(8,128)}, u32[]{:S(2)}) copy-start(f32[25,24,768]{2,1,0:T(8,128)} %shard_map.395) | copy-start | bytes 5529604
  773.3 3.8 copy-start.25
  773.4 3.8 copy-start.29
  773.4 4.4 copy-start.6
  773.4 4.4 copy-start.11
  777.8 4.2 copy-start.5
  777.8 4.2 copy-start.9
  777.8 4.1 copy-start.10
  (15 other events, 39.1 us)
Sparse Core Ops, SparseCore 0:
  11.4 140.5 all-gather.4
  155.4 112.0 all-gather.6

commit v4 on v3

--- a/solution.py
+++ b/solution.py
@@ -39,33 +39,23 @@
 REDUCE_DEPTH = 3
 
 
-def reduce_program(nz, row_count, width, jobs, extra_count, refs, between=None):
-    job_count = len(jobs)
-    picked = lambda ref, index: ref if index is None else ref.at[index]
-    x_refs = [picked(ref, job[2]) for ref, job in zip(refs[:job_count], jobs)]
-    y_refs = [picked(ref, job[3]) for ref, job in zip(refs[job_count : 2 * job_count], jobs)]
-    position = 2 * job_count
-    extra_ref = None
-    if extra_count:
-        extra_ref = refs[position]
-        position += 1
-    out_ref = refs[position]
+def reduce_program(nz, row_count, width, columns_of, x_refs, y_refs, extra_ref, out_ref, scratch, between=None):
     (
         x_buf, y_buf, whole, land_core, first, land_first, second, land_second,
         last, last_low, land_last, extra_sem,
         load_sem, core_send, core_recv, first_send, first_recv, second_send, second_recv,
         last_send, last_recv, credit,
-    ) = refs[position + 1 :]
+    ) = scratch
     dp, z = lax.axis_index("dp"), lax.axis_index("fsdp")
     core, xb, yb = lax.rem(dp, 2), lax.rem(dp // 2, 2), dp // 4
     group = row_count // 8
     part = group // nz
     starts, total = [], 0
-    for _, columns, _, _ in jobs:
+    for columns in columns_of:
         starts.append(total)
         total += columns // width
     computed = total
-    total += extra_count
+    total += extra_ref.shape[0]
 
     core_peer = (dp + 1 - 2 * core, z)
     x_step, y_step = 2 - 4 * xb, 4 - 8 * yb
@@ -84,7 +74,7 @@
         )
 
     def prefetch(g):
-        for number, (_, columns, _, _) in enumerate(jobs):
+        for number, columns in enumerate(columns_of):
             start, stop = starts[number], starts[number] + columns // width
 
             @pl.when((g >= start) & (g < stop))
@@ -168,21 +158,20 @@
             for number in range(8):
                 put(number, product[number * group : (number + 1) * group].astype(jnp.bfloat16))
 
-        if extra_count:
-            @pl.when(g >= computed)
-            def _():
-                copies = [
-                    pltpu.make_async_copy(
-                        extra_ref.at[g - computed, pl.ds(number * group, group), :],
-                        whole.at[slot, number % 2, number // 2],
-                        extra_sem.at[number],
-                    )
-                    for number in range(8)
-                ]
-                for copy in copies:
-                    copy.start()
-                for copy in copies:
-                    copy.wait()
+        @pl.when(g >= computed)
+        def _():
+            copies = [
+                pltpu.make_async_copy(
+                    extra_ref.at[g - computed, pl.ds(number * group, group), :],
+                    whole.at[slot, number % 2, number // 2],
+                    extra_sem.at[number],
+                )
+                for number in range(8)
+            ]
+            for copy in copies:
+                copy.start()
+            for copy in copies:
+                copy.wait()
 
         @pl.when(g >= 4)
         def _():
@@ -279,57 +268,25 @@
             copy.wait_send()
 
 
-def reduce_kernel(nz, row_count, width, jobs, extra_count, *refs):
-    reduce_program(nz, row_count, width, jobs, extra_count, refs)
-
-
-def reduce_setup(pairs, extras, row_count, width, low_shape, nz):
-    bf = jnp.bfloat16
-    xs, ys = ([a if isinstance(a, tuple) else (a, None) for a in side] for side in zip(*pairs))
-    tokens = xs[0][0].shape[-2]
-    group, part = row_count // 8, row_count // 8 // nz
-    jobs = [(x.shape[-1], y.shape[-1], i, j) for (x, i), (y, j) in zip(xs, ys)]
-    total = sum(job[1] // width for job in jobs) + extras.shape[0]
-    low_rows, low_width = low_shape
-    dma, reg = pltpu.SemaphoreType.DMA, pltpu.SemaphoreType.REGULAR
-    operands = [x for x, _ in xs] + [y for y, _ in ys] + [extras]
-    scratch = [
+def reduce_scratch(tokens, row_count, width, total, low_shape, nz):
+    bf, group = jnp.bfloat16, row_count // 8
+    dma, depth = pltpu.SemaphoreType.DMA, REDUCE_DEPTH
+    return [
         pltpu.VMEM((2, tokens, row_count), bf),
         pltpu.VMEM((2, tokens, width), bf),
         pltpu.VMEM((2, 2, 4, group, width), bf),
         pltpu.VMEM((4, 4, group, width), bf),
-        pltpu.VMEM((REDUCE_DEPTH, 2, 2, group, width), bf),
+        pltpu.VMEM((depth, 2, 2, group, width), bf),
         pltpu.VMEM((total, 2, group, width), bf),
-        pltpu.VMEM((REDUCE_DEPTH, 2, group, width), bf),
+        pltpu.VMEM((depth, 2, group, width), bf),
         pltpu.VMEM((total, group, width), bf),
-        pltpu.VMEM((REDUCE_DEPTH, nz, low_rows, low_width), jnp.float32),
-        pltpu.VMEM((REDUCE_DEPTH, nz, low_rows, low_width), bf),
-        pltpu.VMEM((total, nz - 1, low_rows, low_width), bf),
+        pltpu.VMEM((depth, nz, *low_shape), jnp.float32),
+        pltpu.VMEM((depth, nz, *low_shape), bf),
+        pltpu.VMEM((total, nz - 1, *low_shape), bf),
         dma((8,)),
-        dma((2, 2)), dma((2,)), dma((4,)), dma((REDUCE_DEPTH,)), dma((total,)), dma((REDUCE_DEPTH,)), dma((total,)),
-        dma((REDUCE_DEPTH, nz - 1)), dma((total, nz - 1)), reg,
+        dma((2, 2)), dma((2,)), dma((4,)), dma((depth,)), dma((total,)), dma((depth,)), dma((total,)),
+        dma((depth, nz - 1)), dma((total, nz - 1)), pltpu.SemaphoreType.REGULAR,
     ]
-    return (
-        (nz, row_count, width, jobs, extras.shape[0]),
-        operands,
-        [pl.BlockSpec(memory_space=pl.ANY)] * len(operands),
-        jax.ShapeDtypeStruct((total, part, width), jnp.float32),
-        scratch,
-    )
-
-
-def reduce_products(pairs, extras, row_count, width, low_shape, nz, collective_id):
-    static, operands, specs, shape, scratch = reduce_setup(pairs, extras, row_count, width, low_shape, nz)
-    return pl.pallas_call(
-        functools.partial(reduce_kernel, *static),
-        out_shape=shape,
-        in_specs=specs,
-        out_specs=pl.BlockSpec(memory_space=pltpu.VMEM),
-        scratch_shapes=scratch,
-        compiler_params=pltpu.CompilerParams(
-            collective_id=collective_id, has_side_effects=True, vmem_limit_bytes=60 * 2**20
-        ),
-    )(*operands)
 
 
 def gather_program(nz, chunks, sources, results, sems):
@@ -629,16 +586,11 @@
     return pieces
 
 
-def forward_kernel(gather, *refs):
+def forward_kernel(*refs):
     entry_hbm, weight_hbm, (select_ref, mask_ref), refs = refs[0], refs[1:9], refs[9:11], refs[11:]
-    sources, refs = (refs[:1], refs[1:]) if gather else ((), refs)
     kept_hbm, (top_ref, gains_ref), refs = refs[: len(KEPT)], refs[len(KEPT) : len(KEPT) + 2], refs[len(KEPT) + 2 :]
-    results = ()
-    if gather:
-        count = 1 + max(chunk[3] for chunk in gather[1])
-        results, refs = refs[:count], refs[count:]
     entry, weights, kept_refs, refs = refs[0], refs[1:9], refs[9 : 9 + len(KEPT)], refs[9 + len(KEPT) :]
-    hidden, weight_sem, kept_sem = refs[:3]
+    hidden, weight_sem, kept_sem = refs
     kept = {name: ref for (name, _, _), ref in zip(KEPT, kept_refs)}
     local = [(entry_hbm, entry)] + list(zip(weight_hbm, weights))
     fetches = {id(ref): pltpu.make_async_copy(hbm, ref, weight_sem.at[k]) for k, (hbm, ref) in enumerate(local)}
@@ -652,80 +604,64 @@
         copy.start()
         leaving.append(copy)
 
-    steps = 0
-    if gather:
-        steps, step, finish = gather_program(*gather, sources, results, refs[3:])
     pieces = forward_pieces(
         weights, entry, select_ref, mask_ref, hidden, kept, top_ref, gains_ref, lambda ref: fetches[id(ref)].wait(), leave
     )
-    for i in range(max(steps, len(pieces))):
-        if i < steps:
-            step(i)
-        if i < len(pieces):
-            pieces[i]()
-    if gather:
-        finish()
+    for piece in pieces:
+        piece()
     for copy in leaving:
         copy.wait()
 
 
-def trunk_forward(entry, weights, select, mask, gather=None, sources=(), shapes=(), collective_id=None):
+def trunk_forward(entry, weights, select, mask):
     bf, f32 = jnp.bfloat16, jnp.float32
     vmem, hbm = pl.BlockSpec(memory_space=pltpu.VMEM), pl.BlockSpec(memory_space=pl.ANY)
     kept_shapes = [(2, SEQ, columns) for _, columns, _ in KEPT]
-    more = {} if gather is None else {"collective_id": collective_id, "has_side_effects": True}
     outs = pl.pallas_call(
-        functools.partial(forward_kernel, gather),
+        forward_kernel,
         out_shape=[jax.ShapeDtypeStruct(s, dtype) for s, (_, _, dtype) in zip(kept_shapes, KEPT)]
-        + [jax.ShapeDtypeStruct((LAT, D), bf), jax.ShapeDtypeStruct((16, D), f32)]
-        + [jax.ShapeDtypeStruct((2, 2, 2, gather[0], *shape), bf) for shape in shapes],
-        in_specs=[hbm] * 9 + [vmem] * 2 + [hbm] * len(sources),
-        out_specs=[hbm] * len(KEPT) + [vmem] * 2 + [hbm] * len(shapes),
+        + [jax.ShapeDtypeStruct((LAT, D), bf), jax.ShapeDtypeStruct((16, D), f32)],
+        in_specs=[hbm] * 9 + [vmem] * 2,
+        out_specs=[hbm] * len(KEPT) + [vmem] * 2,
         scratch_shapes=[pltpu.VMEM(w.shape, bf) for w in [entry] + weights]
         + [pltpu.VMEM(s, dtype) for s, (_, _, dtype) in zip(kept_shapes, KEPT)]
-        + [pltpu.VMEM((SEQ, D), f32), pltpu.SemaphoreType.DMA((9,)), pltpu.SemaphoreType.DMA((2, len(KEPT)))]
-        + ([] if gather is None else gather_sems(len(gather[1]), gather[0])),
-        compiler_params=pltpu.CompilerParams(vmem_limit_bytes=60 * 2**20, **more),
-    )(entry, *weights, select, mask, *sources)
+        + [pltpu.VMEM((SEQ, D), f32), pltpu.SemaphoreType.DMA((9,)), pltpu.SemaphoreType.DMA((2, len(KEPT)))],
+        compiler_params=pltpu.CompilerParams(vmem_limit_bytes=60 * 2**20),
+    )(entry, *weights, select, mask)
     count = len(KEPT)
-    return outs[count], outs[count + 1], outs[:count], outs[count + 2 :]
+    return outs[count], outs[count + 1], outs[:count]
 
 
 BACK_KEPT = ("packed", "inner", "norm_one", "norm_two", "inv_one", "inv_two")
-
-
-def backward_pieces(refs):
-    weight_hbm, (gains_ref, select_ref, mask_ref, top_ref), refs = refs[:8], refs[8:12], refs[12:]
-    kept_hbm, refs = refs[: len(BACK_KEPT)], refs[len(BACK_KEPT) :]
-    back_hbm, small_ref, refs = refs[: len(BACK)], refs[len(BACK)], refs[len(BACK) + 1 :]
-    buffers, kept_refs, refs = refs[:2], refs[2 : 2 + len(BACK_KEPT)], refs[2 + len(BACK_KEPT) :]
-    back_refs, (mixed, hidden, middle, decoder, gain_grad, weight_sem, kept_sem, back_sem) = refs[: len(BACK)], refs[len(BACK) :]
+BACK_NAMES = tuple(name for name, _ in BACK)
+
+
+def backward_pieces(layer, inputs, outputs, scratch):
+    weight_hbm, (gains_ref, select_ref, mask_ref, upstream_ref, gain_before_ref) = inputs[:4], inputs[4:9]
+    kept_hbm = inputs[9 : 9 + len(BACK_KEPT)]
+    back_hbm, (hidden, gain_grad, small_hbm) = outputs[: len(BACK)], outputs[len(BACK) :]
+    buffers, kept_refs, scratch = scratch[:2], scratch[2 : 2 + len(BACK_KEPT)], scratch[2 + len(BACK_KEPT) :]
+    back_refs, (mixed, middle, small_stage, weight_sem, kept_sem, back_sem, small_sem) = (
+        scratch[: len(BACK)], scratch[len(BACK) :]
+    )
     bf = jnp.bfloat16
-    back = {name: ref for (name, _), ref in zip(BACK, back_refs)}
-    kept = {name: ref for name, ref in zip(BACK_KEPT, kept_refs)}
-    places = []
-    for layer in (1, 0):
-        turn = 1 - layer
-        places += [
-            (turn, 0, FF, 4 * layer + 3), (1 - turn, 0, FF, 4 * layer + 2),
-            (turn, 0, D, 4 * layer + 1), (turn, D, 3 * D, 4 * layer),
-        ]
-    place_of = {place[3]: k for k, place in enumerate(places)}
-
-    def view(weight):
-        buffer, column, columns, _ = places[place_of[weight]]
-        return buffers[buffer].at[:, pl.ds(column, columns)]
-
-    def fetch(weight):
-        return pltpu.make_async_copy(weight_hbm[weight], view(weight), weight_sem.at[weight])
-
-    def fetch_kept(layer, name):
+    back = dict(zip(BACK_NAMES, back_refs))
+    kept = dict(zip(BACK_KEPT, kept_refs))
+    views = (
+        buffers[0].at[:, pl.ds(D, 3 * D)], buffers[0].at[:, pl.ds(0, D)], buffers[1], buffers[0]
+    )
+    QKV, OUT, UP, DOWN = range(4)
+
+    def fetch(k):
+        return pltpu.make_async_copy(weight_hbm[k], views[k], weight_sem.at[k])
+
+    def fetch_kept(name):
         k = BACK_KEPT.index(name)
         return pltpu.make_async_copy(kept_hbm[k].at[layer], kept_refs[k], kept_sem.at[k])
 
-    def leave(layer, name):
-        k = [n for n, _ in BACK].index(name)
-        return pltpu.make_async_copy(back_refs[k], back_hbm[k].at[layer], back_sem.at[k])
+    def leave(name):
+        k = BACK_NAMES.index(name)
+        return pltpu.make_async_copy(back_refs[k], back_hbm[k], back_sem.at[k])
 
     def gain(row):
         return gains_ref[row : row + 1, :]
@@ -736,65 +672,54 @@
         )
 
     def begin():
-        fetch(7).start()
-        fetch_kept(1, "inner").start()
-        fetch(6).start()
+        fetch(DOWN).start()
+        fetch_kept("inner").start()
+        fetch(UP).start()
         for name in ("norm_two", "inv_two", "packed", "norm_one", "inv_one"):
-            fetch_kept(1, name).start()
-        hidden[...] = top_ref[...]
-        gain_grad[...] = jnp.zeros_like(gain_grad)
-
-    def branch(layer):
+            fetch_kept(name).start()
+        upstream = upstream_ref[...]
         if layer == 0:
-            leave(1, "back_branch").wait()
+            upstream = upstream * jnp.transpose(jnp.broadcast_to(mask_ref[...], (128, SEQ)))[:, :1]
+        hidden[...] = upstream
+        gain_grad[...] = gain_before_ref[...]
+
+    def branch():
         back["back_branch"][...] = hidden[...].astype(bf)
-        leave(layer, "back_branch").start()
-        fetch(4 * layer + 3).wait()
-        fetch_kept(layer, "inner").wait()
-        if layer == 0:
-            leave(1, "back_inner").wait()
-
-    def widen(layer, part, parts):
+        leave("back_branch").start()
+        fetch(DOWN).wait()
+        fetch_kept("inner").wait()
+
+    def widen(part, parts):
         columns = slice(part * FF // parts, (part + 1) * FF // parts)
-        up = in_nn(back["back_branch"][...], view(4 * layer + 3)[:, columns])
+        up = in_nn(back["back_branch"][...], views[DOWN][:, columns])
         x = kept["inner"][:, columns]
         t = jnp.tanh(GELU_SCALE * (x + 0.044715 * x * x * x))
         slope = 0.5 * (1.0 + t) + 0.5 * x * (1.0 - t * t) * (GELU_SCALE * (1.0 + 3.0 * 0.044715 * x * x))
         back["back_inner"][:, columns] = (slope * up).astype(bf)
 
-    def narrow(layer):
-        fetch(4 * layer + 1).start()
-        fetch(4 * layer).start()
-        if layer == 1:
-            fetch_kept(0, "inner").start()
-        leave(layer, "back_inner").start()
-        fetch(4 * layer + 2).wait()
-        fetch_kept(layer, "norm_two").wait()
-        fetch_kept(layer, "inv_two").wait()
-        middle[...] = in_nt(back["back_inner"][...], view(4 * layer + 2)[...])
-
-    def renorm(layer):
+    def narrow():
+        fetch(OUT).start()
+        fetch(QKV).start()
+        leave("back_inner").start()
+        fetch(UP).wait()
+        fetch_kept("norm_two").wait()
+        fetch_kept("inv_two").wait()
+        middle[...] = in_nt(back["back_inner"][...], views[UP][...])
+
+    def renorm():
         value = middle[...]
         n = kept["norm_two"][...]
         gain_grad[2 * layer + 1 : 2 * layer + 2, :] = jnp.sum(value * n, 0, keepdims=True)
         middle[...] = hidden[...] + norm_step(value * gain(2 * layer + 1), n, kept["inv_two"][:, :1])
-        if layer == 0:
-            leave(1, "back_attn").wait()
         back["back_attn"][...] = middle[...].astype(bf)
-        leave(layer, "back_attn").start()
-        if layer == 1:
-            fetch(3).start()
-            fetch_kept(0, "norm_two").start()
-            fetch_kept(0, "inv_two").start()
-
-    def unmix(layer):
-        fetch(4 * layer + 1).wait()
-        fetch_kept(layer, "packed").wait()
-        if layer == 0:
-            leave(1, "back_packed").wait()
-        mixed[...] = in_nt(back["back_attn"][...], view(4 * layer + 1)[...]).astype(bf)
-
-    def attend(layer, pair):
+        leave("back_attn").start()
+
+    def unmix():
+        fetch(OUT).wait()
+        fetch_kept("packed").wait()
+        mixed[...] = in_nt(back["back_attn"][...], views[OUT][...]).astype(bf)
+
+    def attend(pair):
         low = low_half()
         at = lambda k: slice(k * D + pair * 2 * HD, k * D + (pair + 1) * 2 * HD)
         q, k, v = (kept["packed"][:, at(i)] for i in range(3))
@@ -816,108 +741,143 @@
         for i in range(3):
             back["back_packed"][:, at(i)] = jnp.where(low, parts[0][i], parts[1][i]).astype(bf)
 
-    def close(layer):
-        leave(layer, "back_packed").start()
-        fetch(4 * layer).wait()
-        fetch_kept(layer, "norm_one").wait()
-        fetch_kept(layer, "inv_one").wait()
-        value = in_nt(back["back_packed"][...], view(4 * layer)[...])
+    def close():
+        leave("back_packed").start()
+        fetch(QKV).wait()
+        fetch_kept("norm_one").wait()
+        fetch_kept("inv_one").wait()
+        value = in_nt(back["back_packed"][...], views[QKV][...])
         n = kept["norm_one"][...]
         gain_grad[2 * layer : 2 * layer + 1, :] = jnp.sum(value * n, 0, keepdims=True)
         hidden[...] = middle[...] + norm_step(value * gain(2 * layer), n, kept["inv_one"][:, :1])
-        if layer == 1:
-            fetch(2).start()
-            for name in ("packed", "norm_one", "inv_one"):
-                fetch_kept(0, name).start()
-            decoder[...] = hidden[...].astype(bf)
-            keep = jnp.transpose(jnp.broadcast_to(mask_ref[...], (128, SEQ)))[:, :1]
-            hidden[...] = hidden[...] * keep
+        for name in BACK_NAMES:
+            leave(name).wait()
 
     def small():
-        hidden_low = hidden[...].astype(bf)
-        small_ref[...] = (
-            in_tn(hidden_low, select_ref[:SEQ, :])
-            + in_tn(decoder[...], select_ref[SEQ : 2 * SEQ, :])
+        small_stage[...] = (
+            in_tn(hidden[...].astype(bf), select_ref[:SEQ, :])
+            + in_tn(upstream_ref[...].astype(bf), select_ref[SEQ : 2 * SEQ, :])
             + in_tn(gain_grad[...].astype(bf), select_ref[2 * SEQ :, :])
         ).astype(bf)
-        for name, _ in BACK:
-            leave(0, name).wait()
-
-    pieces = [begin]
-    for layer in (1, 0):
-        pieces.append(functools.partial(branch, layer))
-        for part in range(3):
-            pieces.append(functools.partial(widen, layer, part, 3))
-        pieces += [functools.partial(f, layer) for f in (narrow, renorm, unmix)]
-        for pair in range(HEADS // 2):
-            pieces.append(functools.partial(attend, layer, pair))
-        pieces.append(functools.partial(close, layer))
-    pieces.append(small)
-    return pieces
-
-
-def backward_kernel(reduction, operand_count, *refs):
-    fixed = 12 + len(BACK_KEPT)
-    results = len(BACK) + 1
+        copy = pltpu.make_async_copy(small_stage, small_hbm.at[0], small_sem)
+        copy.start()
+        copy.wait()
+
+    return (
+        [begin, branch]
+        + [functools.partial(widen, part, 3) for part in range(3)]
+        + [narrow, renorm, unmix]
+        + [functools.partial(attend, pair) for pair in range(HEADS // 2)]
+        + [close]
+        + ([small] if layer == 0 else [])
+    )
+
+
+def backward_kernel(layer, reduction, *refs):
+    input_count, output_count = 9 + len(BACK_KEPT), len(BACK) + 3
+    inputs, refs = refs[:input_count], refs[input_count:]
     if reduction is None:
-        for piece in backward_pieces(refs):
+        for piece in backward_pieces(layer, inputs, refs[:output_count], refs[output_count:]):
             piece()
         return
-    mine, refs = refs[:fixed], refs[fixed:]
-    operands, refs = refs[:operand_count], refs[operand_count:]
-    mine, refs = mine + refs[:results], refs[results:]
-    summed, refs = refs[0], refs[1:]
-    count = 2 + len(BACK_KEPT) + len(BACK) + 8
-    pieces = backward_pieces(mine + refs[:count])
-    chunks = summed.shape[0]
-    start = 0
-    per_turn = -(-len(pieces) // (chunks - start))
+    nz, row_count, width, jobs, has_extras = reduction
+    side_refs = []
+    for side in range(2):
+        chosen = []
+        for job in jobs:
+            if job[side] is None:
+                chosen.append((None, job[2 + side]))
+            else:
+                chosen.append((refs[0], job[side][0]))
+                refs = refs[1:]
+        side_refs.append(chosen)
+    extra_ref = None
+    if has_extras:
+        extra_ref, refs = refs[0], refs[1:]
+    outputs, summed, refs = refs[:output_count], refs[output_count], refs[output_count + 1 :]
+    scratch_count = 2 + len(BACK_KEPT) + len(BACK) + 7
+
+    def resolve(ref, index):
+        if ref is None:
+            return outputs[BACK_NAMES.index(index)]
+        return ref if index is None else ref.at[index]
+
+    x_refs, y_refs = ([resolve(*pair) for pair in chosen] for chosen in side_refs)
+    pieces = backward_pieces(layer, inputs, outputs, refs[:scratch_count])
+    each, stride = (1, 2) if layer == 1 else (2, 1)
 
     def between(i):
-        for turn in range(-(-len(pieces) // per_turn)):
-            @pl.when(i == start + turn)
+        for turn in range(-(-len(pieces) // each)):
+            @pl.when(i == turn * stride)
             def _():
-                for piece in pieces[turn * per_turn : (turn + 1) * per_turn]:
+                for piece in pieces[turn * each : (turn + 1) * each]:
                     piece()
 
-    reduce_program(*reduction, operands + (summed,) + refs[count:], between)
-
-
-def trunk_backward(gains, weights, select, mask, back_top, kept, reduction=None, collective_id=None):
+    reduce_program(
+        nz, row_count, width, [job[4] for job in jobs], x_refs, y_refs, outputs[-1] if extra_ref is None else extra_ref,
+        summed, refs[scratch_count:], between,
+    )
+
+
+def layer_backward(
+    layer, gains, weights, select, mask, upstream, gain_before, kept, pairs=None, extras=None, sizes=None, collective_id=None
+):
     bf, f32 = jnp.bfloat16, jnp.float32
     vmem, hbm = pl.BlockSpec(memory_space=pltpu.VMEM), pl.BlockSpec(memory_space=pl.ANY)
     kept_in = [kept[KEPT_INDEX[name]] for name in BACK_KEPT]
-    static, operands, specs, shape, scratch = reduction or (None, [], [], None, [])
-    more = {} if reduction is None else {"collective_id": collective_id, "has_side_effects": True}
+    static, operands, more, summed, scratch = None, [], {}, [], []
+    if pairs is not None:
+        row_count, width, low_shape, nz = sizes
+        widths, jobs, sides = dict(BACK), [], ([], [])
+        for pair in pairs:
+            marks, columns = [], 0
+            for side, entry in enumerate(pair):
+                if isinstance(entry, str):
+                    marks.append((None, entry))
+                    columns = widths[entry]
+                else:
+                    array, index = entry if isinstance(entry, tuple) else (entry, None)
+                    sides[side].append(array)
+                    marks.append(((index,), None))
+                    columns, tokens = array.shape[-1], array.shape[-2]
+            jobs.append((marks[0][0], marks[1][0], marks[0][1], marks[1][1], columns))
+        total = sum(job[4] // width for job in jobs) + (1 if extras is None else extras.shape[0])
+        operands = sides[0] + sides[1] + ([] if extras is None else [extras])
+        static = (nz, row_count, width, jobs, extras is not None)
+        summed = [jax.ShapeDtypeStruct((total, row_count // 8 // nz, width), f32)]
+        scratch = reduce_scratch(tokens, row_count, width, total, low_shape, nz)
+        more = {"collective_id": collective_id, "has_side_effects": True}
+    dma = pltpu.SemaphoreType.DMA
     outs = pl.pallas_call(
-        functools.partial(backward_kernel, static, len(operands)),
-        out_shape=[jax.ShapeDtypeStruct((2, SEQ, columns), bf) for _, columns in BACK]
-        + [jax.ShapeDtypeStruct((D, TRUNK_WIDTH), bf)]
-        + ([] if reduction is None else [shape]),
-        in_specs=[hbm] * 8 + [vmem] * 4 + [hbm] * len(BACK_KEPT) + specs,
-        out_specs=[hbm] * len(BACK) + [vmem] * (1 if reduction is None else 2),
+        functools.partial(backward_kernel, layer, static),
+        out_shape=[jax.ShapeDtypeStruct((SEQ, columns), bf) for _, columns in BACK]
+        + [
+            jax.ShapeDtypeStruct((SEQ, D), f32), jax.ShapeDtypeStruct((16, D), f32),
+            jax.ShapeDtypeStruct((1, D, TRUNK_WIDTH), bf),
+        ]
+        + summed,
+        in_specs=[hbm] * 4 + [vmem] * 5 + [hbm] * (len(BACK_KEPT) + len(operands)),
+        out_specs=[hbm] * len(BACK) + [vmem] * 2 + [hbm] + [vmem] * len(summed),
         scratch_shapes=[pltpu.VMEM((D, FF), bf)] * 2
         + [pltpu.VMEM(a.shape[1:], a.dtype) for a in kept_in]
         + [pltpu.VMEM((SEQ, columns), bf) for _, columns in BACK]
         + [
-            pltpu.VMEM((SEQ, D), bf), pltpu.VMEM((SEQ, D), f32), pltpu.VMEM((SEQ, D), f32), pltpu.VMEM((SEQ, D), bf),
-            pltpu.VMEM((16, D), f32),
-            pltpu.SemaphoreType.DMA((8,)), pltpu.SemaphoreType.DMA((len(BACK_KEPT),)),
-            pltpu.SemaphoreType.DMA((len(BACK),)),
+            pltpu.VMEM((SEQ, D), bf), pltpu.VMEM((SEQ, D), f32),
+            pltpu.VMEM((D, TRUNK_WIDTH) if layer == 0 else (16, 128), bf),
+            dma((4,)), dma((len(BACK_KEPT),)), dma((len(BACK),)), dma,
         ]
         + scratch,
         compiler_params=pltpu.CompilerParams(vmem_limit_bytes=60 * 2**20, **more),
-    )(*weights, gains, select, mask, back_top, *kept_in, *operands)
-    back = dict(zip([name for name, _ in BACK], outs))
-    pairs = []
-    for layer in range(2):
-        left = lambda name: (kept[KEPT_INDEX[name]], layer)
-        right = lambda name: (back[name], layer)
-        pairs += [
-            (left("normed"), right("back_packed")), (left("mixed"), right("back_attn")),
-            (left("second"), right("back_inner")), (right("back_branch"), left("upper")),
-        ]
-    return pairs, outs[len(BACK)], outs[len(BACK) + 1 :]
+    )(*weights, gains, select, mask, upstream, gain_before, *kept_in, *operands)
+    return dict(zip(BACK_NAMES, outs)), *outs[len(BACK) :]
+
+
+def layer_pairs(layer, kept, back):
+    left = lambda name: (kept[KEPT_INDEX[name]], layer)
+    return [
+        (left("normed"), back["back_packed"]), (left("mixed"), back["back_attn"]),
+        (left("second"), back["back_inner"]), (back["back_branch"], left("upper")),
+    ]
 
 
 ROWS_AT_ONCE = 192
@@ -1337,16 +1297,15 @@
         1,
     )
     chunks, shapes = gather_plan(
-        [(1, None, r0, (TRUNK_WIDTH,)), (0, 0, r0, TRUNK_PARTS), (0, 1, r0, TRUNK_PARTS)], TRUNK_WIDTH
-    )
-    later = [(0, None, r1, EDGE_PARTS)]
-    edge_chunks, edge_shapes = gather_plan(later, HEAD_WIDTH)
-    whole = lambda arrays: [a.reshape(devices * a.shape[4], -1) for a in arrays]
+        [(1, None, r0, (TRUNK_WIDTH,)), (0, 0, r0, TRUNK_PARTS), (0, 1, r0, TRUNK_PARTS), (2, None, r1, EDGE_PARTS)],
+        TRUNK_WIDTH,
+    )
+    sources = [low_blocks, low_entry, low_edges]
     if direct:
-        trunk = whole(gather_rows([low_blocks, low_entry], chunks, shapes, nz, 1))
+        gathered = [a.reshape(devices * a.shape[4], -1) for a in gather_rows(sources, chunks, shapes, nz, 1)]
     else:
-        trunk = plain_gather([low_blocks, low_entry], chunks, shapes)
-        edge_mats = plain_gather([low_edges], edge_chunks, edge_shapes)
+        gathered = plain_gather(sources, chunks, shapes)
+    trunk, edge_mats = gathered[:9], gathered[9:]
     head_blocks = [lax.all_gather(low_head[b], AXES, axis=0, tiled=True) for b in range(HB)]
 
     early = trunk[0][::r0, 2 * SEQ + CH + 4 : 2 * SEQ + CH + 8].astype(jnp.float32)
@@ -1367,13 +1326,7 @@
     select = (pick_rows[:, None] == columns[None, :]).astype(bf) + jnp.pad(
         clean, ((BUF, SEQ + 16), (2 * SEQ, TRUNK_WIDTH - 2 * SEQ - CH))
     )
-    if direct:
-        top_rows, gains, kept, edge_mats = trunk_forward(
-            trunk[0], trunk[1:9], select, key_keep[None], (nz, edge_chunks), [low_edges], edge_shapes, 2
-        )
-        edge_mats = whole(edge_mats)
-    else:
-        top_rows, gains, kept, _ = trunk_forward(trunk[0], trunk[1:9], select, key_keep[None])
+    top_rows, gains, kept = trunk_forward(trunk[0], trunk[1:9], select, key_keep[None])
 
     capacity = (LAT + devices - 1) // devices
     slots = devices * capacity
@@ -1438,36 +1391,47 @@
         returning.reshape(devices, capacity, D), AXES, split_axis=0, concat_axis=0, tiled=True
     ).reshape(slots, D)
     back_top = jnp.concatenate([jnp.zeros((BUF, D), jnp.float32), dot_left(pick, returned)], 0)
-    reduction = None
+    mask = key_keep[None]
+    no_gain = jnp.zeros((16, D), jnp.float32)
     if direct:
         extras = jnp.stack(
             [head_small[:, k : k + HEAD_WIDTH] for k in range(0, head_small.shape[1], HEAD_WIDTH)]
         )
-        reduction = reduce_setup(head_pairs, extras, HW, HEAD_WIDTH, (r1, HEAD_WIDTH), nz)
-    trunk_pairs, trunk_small, tall = trunk_backward(
-        gains, trunk[1:9], select, key_keep[None], back_top, kept, reduction, 4
-    )
-    if direct:
-        tall = tall[0].transpose(1, 0, 2).reshape(r1, -1)
+        decoder_back, back_decoder, gain_grad, _, tall = layer_backward(
+            1, gains, trunk[5:9], select, mask, back_top, no_gain, kept,
+            head_pairs, extras, (HW, HEAD_WIDTH, (r1, HEAD_WIDTH), nz), 4,
+        )
+        tall = tall.transpose(1, 0, 2).reshape(r1, -1)
+        own = {name: name for name in BACK_NAMES}
+        trunk_pairs = layer_pairs(1, kept, decoder_back) + layer_pairs(0, kept, own)
+        *_, wide = layer_backward(
+            0, gains, trunk[1:5], select, mask, back_decoder, gain_grad, kept,
+            trunk_pairs, None, (D, TRUNK_WIDTH, (2 * r0, TRUNK_WIDTH // 2), nz), 5,
+        )
+        wide = wide.transpose(1, 0, 2).reshape(r0, -1)
     else:
         tall = jnp.concatenate(
             [scatter_sum(dot_left(x, y)) for x, y in head_pairs]
             + [scatter_sum(head_small.astype(jnp.float32))],
             1,
         )
-    if direct:
-        wide = reduce_products(
-            trunk_pairs, trunk_small[None], D, TRUNK_WIDTH, (2 * r0, TRUNK_WIDTH // 2), nz, 5
+        decoder_back, back_decoder, gain_grad, _ = layer_backward(
+            1, gains, trunk[5:9], select, mask, back_top, no_gain, kept
         )
-        wide = wide.transpose(1, 0, 2).reshape(r0, -1)
-    else:
+        encoder_back, _, _, trunk_small = layer_backward(
+            0, gains, trunk[1:5], select, mask, back_decoder, gain_grad, kept
+        )
+        whole = lambda entry: entry[0][entry[1]] if isinstance(entry, tuple) else entry
         wide = jnp.concatenate(
-            [scatter_sum(dot_left(x[0][x[1]], y[0][y[1]])) for x, y in trunk_pairs]
-            + [scatter_sum(trunk_small.astype(jnp.float32))],
+            [
+                scatter_sum(dot_left(whole(x), whole(y)))
+                for x, y in layer_pairs(1, kept, decoder_back) + layer_pairs(0, kept, encoder_back)
+            ]
+            + [scatter_sum(trunk_small[0].astype(jnp.float32))],
             1,
         )
     block_columns, head_columns = sum(TRUNK_PARTS), sum(HEAD_PARTS)
-    block_grad = jnp.stack([wide[:, l * block_columns : (l + 1) * block_columns] for l in range(2)])
+    block_grad = jnp.stack([wide[:, l * block_columns : (l + 1) * block_columns] for l in (1, 0)])
     rest = wide[:, 2 * block_columns :]
     entry_grad = rest[:, : 2 * SEQ + CH].T
     gain_grad = rest[:, 2 * SEQ + CH : 2 * SEQ + CH + 4].T.reshape(2, 2, r0)

time: 803 us -> 775 us (0.965)
  Pallas kernels: 678 us -> 654 us
    pallas_call x3, Pallas kernels: 409 us -> 322 us  [the longest x2 291 us: layer_backward(): pl.pallas_call(functools.partial(backward_kernel, layer, static), out_sha...]
    pallas_call x1, Pallas kernels: 180 us -> 243 us  [gather_rows(): pl.pallas_call(functools.partial(gather_kernel, nz, chunks, len(sources))...]
  transfers between devices with their start and end apart: 4 -> 4, of which waited for: 2 -> 2; matrix products, arithmetic and copies ran while one was open for 4% -> 4% of each run, Pallas kernels for 34% -> 36%
where the time goes in v4:
time: 775 us; the launch traced here: 766 us
  Pallas kernels  654 us (84%)
  other arithmetic  36.6 us (5%)
  between operations  23.6 us (3%)
  local copies, waits for them, and re-layouts  22.4 us (3%)
  waiting for transfers between devices  12.1 us (2%)
  matrix products  10.6 us (1%)
    pallas_call x2, Pallas kernels, layer_backward(): pl.pallas_call(functools.partial(backward_kernel, layer, static), out_sha...  291 us
    pallas_call x1, Pallas kernels, gather_rows(): pl.pallas_call(functools.partial(gather_kernel, nz, chunks, len(sources))...  243 us
    pallas_call x1, Pallas kernels, head_pass(): pl.pallas_call(functools.partial(head_kernel, tokens), out_shape=[jax.Sha...  79.7 us
    pallas_call x1, Pallas kernels, trunk_forward(): pl.pallas_call(forward_kernel, out_shape=[jax.ShapeDtypeStruct(s, dtype)...  30.2 us
  transfers between devices with their start and end apart: 4, of which 2 were waited for; matrix products, arithmetic and copies ran while one was open for 4% of the time, Pallas kernels for 36%

profile of v4, /device:TPU:0, one launch (start us, length us, event | category | flops | bytes accessed | tf_op | source)
XLA Modules:
  0.0 765.7 jit_solution(17841662201929117200)
XLA Ops:
  7.2 1.4 convert_element_type.154
  18.3 2.0 pad_maximum_fusion.3
  21.0 243.3 %shard_map.391 = (bf16[2,2,2,4,24,768]{5,4,3,2,1,0:T(8,128)(2,1)}, bf16[2,2,2,4,24,2304]{5,4,3,2,1,0:T(8,128)(2,1)}, bf16[2,2,2,4,24,768]{5,4,3,2,1,0:T(8,128)(2...) custom-call(bf16[2,24,9216]{2,1,0:T(8,128)(2,1)} %convert_element_ty, ...), custom_call_target="tpu_custom_call" | custom-call | tf_op jit(solution)/shard_map/pallas_call | solution.py:388
  269.2 30.2 %shard_map.392 = (bf16[2,320,768]{2,1,0:T(8,128)(2,1)}, bf16[2,320,2304]{2,1,0:T(8,128)(2,1)}, bf16[2,320,768]{2,1,0:T(8,128)(2,1)}, bf16[2,320,768]{2,1,0:T(8,1...) custom-call(bf16[768,768]{1,0:T(8,128)(2,1)} %bitcast.205, ...), custom_call_target="tpu_custom_call" | custom-call | tf_op jit(solution)/shard_map/pallas_call | solution.py:620
  300.3 2.1 fusion.6
  302.4 2.9 all-to-all-start
  308.7 1.7 fusion.16
  312.6 5.8 all-to-all-done
  323.1 79.7 %shard_map.393 = (bf16[4,192,3072]{2,1,0:T(8,128)(2,1)}, bf16[4,192,1024]{2,1,0:T(8,128)(2,1)}, bf16[4,192,1024]{2,1,0:T(8,128)(2,1)}, bf16[4,192,1024]{2,1,0:T(...) custom-call(bf16[4,192,256]{2,1,0:T(8,128)(2,1)} %pad_maximum_fusion, ...), custom_call_target="tpu_custom_call" | custom-call | tf_op jit(solution)/shard_map/pallas_call | solution.py:1167
  402.8 1.7 convolution_convert_fusion
  409.0 4.0 all-to-all-start.1
  413.7 2.1 convolution_bitcast_fusion.1
  417.3 2.0 pad_maximum_fusion.refs_33_
  419.3 5.5 all-to-all-done.1
  426.9 146.5 %shard_map.394 = (bf16[320,2304]{1,0:T(8,128)(2,1)}, bf16[320,768]{1,0:T(8,128)(2,1)}, bf16[320,3072]{1,0:T(8,128)(2,1)}, bf16[320,768]{1,0:T(8,128)(2,1)}, f32[...) custom-call(bf16[768,2304]{1,0:T(8,128)(2,1)} %bitcast.166, ...), custom_call_target="tpu_custom_call" | custom-call | tf_op jit(solution)/shard_map/pallas_call | solution.py:851
  573.4 1.8 copy.97
  578.1 144.9 %shard_map.395 = (bf16[320,2304]{1,0:T(8,128)(2,1)}, bf16[320,768]{1,0:T(8,128)(2,1)}, bf16[320,3072]{1,0:T(8,128)(2,1)}, bf16[320,768]{1,0:T(8,128)(2,1)}, f32[...) custom-call(bf16[768,2304]{1,0:T(8,128)(2,1)} %bitcast.164, ...), custom_call_target="tpu_custom_call" | custom-call | tf_op jit(solution)/shard_map/pallas_call | solution.py:851
  723.0 2.6 fusion.2
  727.6 9.1 %shard_map.396 = f32[32,8,128]{2,1,0:T(8,128)S(1)} custom-call(f32[8,128]{1,0:T(8,128)S(1)} %broadcast_in_dim.88.in_ref), custom_call_target="tpu_custom_call" | custom-call | tf_op jit(solution)/shard_map/pallas_call | solution.py:440
  738.2 1.6 copy.96
  742.5 1.7 multiply_subtract_fusion.3
  745.6 3.0 multiply_subtract_fusion.2
  749.9 2.7 multiply_subtract_fusion.1
  754.1 3.4 multiply_subtract_fusion
  (179 shorter events, 40.6 us)
Async XLA Ops:
  7.2 314.1 %all-gather.5.cloned.1.call-start = ((), (), s32[]{:S(2)}) async-start(), calls=%async_computation.2 | async-start | bytes 10813440 | tf_op jit(solution)/shard_map/all_gather | solution.py:1309
  8.7 7.4 copy-start.23
  8.7 7.5 copy-start.18
  8.7 7.7 copy-start.1
  9.6 311.6 %all-gather.7.cloned.1.call-start = ((), (), s32[]{:S(2)}) async-start(), calls=%async_computation.3 | async-start | bytes 10813440 | tf_op jit(solution)/shard_map/all_gather | solution.py:1309
  10.6 9.7 %copy-start.13 = (f32[656,24]{0,1:T(8,128)S(1)}, f32[656,24]{0,1:T(8,128)}, u32[]{:S(2)}) copy-start(f32[656,24]{0,1:T(8,128)} %param.32) | copy-start | bytes 188932
  16.4 250.6 %copy-start.27 = (s32[1,256]{1,0:T(1,128)S(1)}, s32[1,256]{1,0:T(1,128)}, u32[]{:S(2)}) copy-start(s32[1,256]{1,0:T(1,128)} %param.25) | copy-start | bytes 3076
  16.4 251.4 %copy-start.22 = (bf16[1,256,16]{1,2,0:T(8,128)(2,1)S(1)}, bf16[1,256,16]{1,2,0:T(8,128)(2,1)}, u32[]{:S(2)}) copy-start(bf16[1,256,16]{1,2,0:T(8,128)(2,1)} %param.24) | copy-start | bytes 24580
  299.4 5.9 copy-start.6
  299.4 6.2 copy-start.16
  302.4 6.2 copy-start.17
  302.4 16.0 %all-to-all-start = ((bf16[32,8,896]{2,1,0:T(8,128)(2,1)}), bf16[32,8,896]{2,1,0:T(8,128)(2,1)S(1)}, u32[]{:S(2)}, u32[]{:S(2)}) async-start(bf16[32,8,896]{2,1,0:T(8,128)(2,1)} %fusion.6), calls=%async_computation | async-start | bytes 917504 | tf_op jit(solution)/shard_map/all_to_all | solution.py:1344
  305.6 6.2 copy-start.30
  407.3 5.7 copy-start.15
  407.3 6.3 copy-start.33
  409.0 15.8 %all-to-all-start.1 = ((bf16[32,8,768]{2,1,0:T(8,128)(2,1)}), bf16[32,8,768]{2,1,0:T(8,128)(2,1)S(1)}, u32[]{:S(2)}, u32[]{:S(2)}) async-start(bf16[32,8,768]{2,1,0:T(8,128)(2,1)} %fusion.7), calls=%async_computation.1 | async-start | bytes 786432 | tf_op jit(solution)/shard_map/all_to_all | solution.py:1390
  744.2 5.7 copy-start.11
  745.6 3.7 copy-start.24
  745.6 3.7 copy-start.28
  745.6 4.3 copy-start.3
  745.6 4.3 copy-start.5
  745.6 4.2 copy-start.10
  749.9 3.7 copy-start.8
  749.9 4.2 copy-start.9
  (14 other events, 36.1 us)
Sparse Core Ops, SparseCore 0:
  11.4 138.8 all-gather.4
  153.7 116.9 all-gather.6

commit v5 on v4

--- a/solution.py
+++ b/solution.py
@@ -60,11 +60,6 @@
     core_peer = (dp + 1 - 2 * core, z)
     x_step, y_step = 2 - 4 * xb, 4 - 8 * yb
     z_peers = [(dp, lax.rem(z + s, nz)) for s in range(1, nz)]
-    barrier = pltpu.get_barrier_semaphore()
-    for peer in [core_peer, (dp + x_step, z), (dp + y_step, z)] + z_peers:
-        pl.semaphore_signal(barrier, inc=1, device_id=peer, device_id_type=MESH_IDS)
-    pl.semaphore_wait(barrier, 2 + nz)
-
     def loads(x_ref, y_ref, column, slot):
         return (
             pltpu.make_async_copy(x_ref, x_buf.at[slot], load_sem.at[0, slot]),
@@ -81,6 +76,12 @@
             def _():
                 for copy in loads(x_refs[number], y_refs[number], (g - start) * width, lax.rem(g, 2)):
                     copy.start()
+
+    prefetch(0)
+    barrier = pltpu.get_barrier_semaphore()
+    for peer in [core_peer, (dp + x_step, z), (dp + y_step, z)] + z_peers:
+        pl.semaphore_signal(barrier, inc=1, device_id=peer, device_id_type=MESH_IDS)
+    pl.semaphore_wait(barrier, 2 + nz)
 
     def core_copy(g):
         return pltpu.make_async_remote_copy(
@@ -239,8 +240,6 @@
             out_ref[g, :, pl.ds(k * low_width, low_width)] = value[k * part : (k + 1) * part]
 
     lags = REDUCE_LAGS
-    prefetch(0)
-
     @pl.loop(0, total + lags[-1])
     def _(i):
         for stage, lag in zip((stage_out, stage_last, stage_second, stage_first), lags[:0:-1]):
@@ -892,7 +891,7 @@
 
 
 def head_kernel(tokens, *refs):
-    (embed_ref, noisy_ref, target_ref, grad_col_ref, loss_col_ref, bias_ref, cond_ref), refs = refs[:7], refs[7:]
+    (embed_ref, noisy_ref, target_ref, loss_col_ref, bias_ref, cond_ref), refs = refs[:6], refs[6:]
     count = len(HEAD_WEIGHTS)
     block_hbm, edge_hbm, refs = refs[:HB], refs[HB : HB + 7], refs[HB + 7 :]
     weight_hbm = [
@@ -905,7 +904,7 @@
     weights, refs = refs[:count], refs[count:]
     left, refs = refs[: len(HEAD_LEFT)], refs[len(HEAD_LEFT) :]
     (
-        time_inner, conditioning, projected, cond_sum, stream, back_silu, t0, t1, t2,
+        time_inner, conditioning, projected, cond_sum, stream, back_silu, t0, t1,
         scale1, normed, inner, gate, branch, inverse, weight_sem, left_sem,
     ) = refs
     cond_t, time_two_t, shift_t, scale_t, time_one_t, in_t, out_t = weights[3 * HB :]
@@ -945,50 +944,63 @@
     def add_bias_grad(row, value):
         bias_grad_ref[row : row + 1, :] += jnp.sum(value.astype(jnp.float32), 0, keepdims=True)
 
-    @pl.loop(0, COPIES)
-    def _(c):
+    base = per_block * HB
+    doubled = [per_block * b for b in range(HB)] + [base + 2, base + 3]
+
+    def leave(k, c, half):
+        source = left[k].at[pl.ds(half * tokens, tokens), :] if k in doubled else left[k]
+        return pltpu.make_async_copy(source, left_hbm[k].at[c], left_sem.at[k, half if k in doubled else 0])
+
+    def one_copy(pair, half):
+        c = 2 * pair + half
+        own = slice(half * tokens, (half + 1) * tokens)
+
         def need(*numbers):
-            @pl.when(c == 0)
-            def _():
-                for k in numbers:
-                    fetch(k).wait()
-
-        def leave(k):
-            return pltpu.make_async_copy(left[k], left_hbm[k].at[c], left_sem.at[k])
+            if half == 0:
+                @pl.when(pair == 0)
+                def _():
+                    for k in numbers:
+                        fetch(k).wait()
+
+        def send(k):
+            leave(k, c, half).start()
 
         def room(*numbers):
-            @pl.when(c > 0)
-            def _():
-                for k in numbers:
-                    leave(k).wait()
-
-        base = per_block * HB
+            for k in numbers:
+                if half == 1 and k not in doubled:
+                    leave(k, c, half).wait()
+                else:
+                    @pl.when(pair > 0)
+                    def _():
+                        leave(k, c, half).wait()
+
         room(base, base + 1)
         need(3 * HB)
 
-        @pl.when(c == 0)
-        def _():
-            projected[...] = nt(cond_ref[...], cond_t[...])
+        if half == 0:
+            @pl.when(pair == 0)
+            def _():
+                projected[...] = nt(cond_ref[...], cond_t[...])
 
         need(3 * HB + 4, 3 * HB + 1, 3 * HB + 5)
-        time_inner[...] = nt(embed_ref[c], time_one_t[...])
+        t1[...] = nt(embed_ref[c], time_one_t[...])
 
         def _(r):
-            value = time_inner[r, :] + bias(10)
-            time_inner[r, :] = value
+            value = t1[r, :] + bias(10)
+            time_inner[own, :] = value
             time_hidden[r, :] = (value * sigmoid(value)).astype(bf)
         by_rows(_)
-        leave(base + 1).start()
+        send(base + 1)
         t0[...] = nt(time_hidden[...], time_two_t[...])
         stream[...] = nt(noisy_ref[c], in_t[...])
 
         def _(r):
             value = projected[r, :] + (t0[r, :] + bias(11))
-            conditioning[r, :] = value
+            conditioning[own, :] = value
             silu_cond[r, :] = (value * sigmoid(value)).astype(bf)
             stream[r, :] = stream[r, :] + bias(14)
         by_rows(_)
-        leave(base).start()
+        send(base)
 
         for b in range(HB):
             w_mod, w_up, w_down = weights[3 * b : 3 * b + 3]
@@ -997,7 +1009,6 @@
             need(3 * b)
             t0[...] = nn(silu_cond[...], w_mod[:, :HW])
             t1[...] = nn(silu_cond[...], w_mod[:, HW : 2 * HW])
-            gate[b] = nn(silu_cond[...], w_mod[:, 2 * HW :])
 
             def _(r):
                 value = stream[r, :]
@@ -1010,7 +1021,7 @@
                 scale1[b, r, :] = s
                 shaped[r, :] = (n * s + (t0[r, :] + bias(5 * b))).astype(bf)
             by_rows(_)
-            leave(per_block * b + 1).start()
+            send(per_block * b + 1)
             need(3 * b + 1)
             inner[b] = nn(shaped[...], w_up[...])
 
@@ -1019,20 +1030,21 @@
                 inner[b, r, :] = value
                 hidden[r, :] = (value * sigmoid(value)).astype(bf)
             by_rows(_)
-            leave(per_block * b + 4).start()
+            send(per_block * b + 4)
             need(3 * b + 2)
-            branch[b] = nt(hidden[...], w_down[...])
+            t0[...] = nn(silu_cond[...], w_mod[:, 2 * HW :])
+            t1[...] = nt(hidden[...], w_down[...])
 
             def _(r):
-                value = branch[b, r, :] + bias(5 * b + 4)
-                g = gate[b, r, :] + bias(5 * b + 2)
-                branch[b, r, :] = value
-                gate[b, r, :] = g
+                value = t1[r, :] + bias(5 * b + 4)
+                g = t0[r, :] + bias(5 * b + 2)
+                branch[b, r, :] = value.astype(bf)
+                gate[b, r, :] = g.astype(bf)
                 stream[r, :] = stream[r, :] + g * value
             by_rows(_)
 
         need(3 * HB + 2, 3 * HB + 3, 3 * HB + 6)
-        room(*range(base + 2, base + 8))
+        room(*range(base + 4, base + 8))
         t0[...] = nt(silu_cond[...], shift_t[...])
         t1[...] = nt(silu_cond[...], scale_t[...])
         def _(r):
@@ -1042,19 +1054,19 @@
             n = centred * inv
             s = 1.0 + (t1[r, :] + bias(13))
             inverse[HB, r, :] = jnp.broadcast_to(inv, (ROWS_AT_ONCE, 128))
-            t2[r, :] = n
+            back_silu[own, :] = n
             t1[r, :] = s
             final_low[r, :] = (n * s + (t0[r, :] + bias(12))).astype(bf)
         by_rows(_)
-        leave(base + 6).start()
+        send(base + 6)
         difference = nn(final_low[...], out_t[...]) - target_ref[c]
         loss_ref[...] += loss_col_ref[c] * difference * difference
-        pred_ref[c] = (grad_col_ref[c] * difference).astype(bf)
+        pred_ref[c] = (loss_col_ref[c] * bias_ref[15:16, :128] * difference).astype(bf)
         t0[...] = nt(pred_ref[c], out_t[...])
 
         def _(r):
             back = t0[r, :]
-            n = t2[r, :]
+            n = back_silu[own, :]
             low_shift, low_scale = back.astype(bf), (back * n).astype(bf)
             back_shift[r, :] = low_shift
             back_scale[r, :] = low_scale
@@ -1065,9 +1077,9 @@
                 up - jnp.mean(up, -1, keepdims=True) - n * jnp.mean(up * n, -1, keepdims=True)
             )
         by_rows(_)
-        leave(base + 4).start()
-        leave(base + 5).start()
-        back_silu[...] = nn(back_shift[...], shift_t[...]) + nn(back_scale[...], scale_t[...])
+        send(base + 4)
+        send(base + 5)
+        back_silu[own, :] = nn(back_shift[...], shift_t[...]) + nn(back_scale[...], scale_t[...])
 
         for b in reversed(range(HB)):
             w_mod, w_up, w_down = weights[3 * b : 3 * b + 3]
@@ -1075,14 +1087,14 @@
 
             def _(r):
                 back = stream[r, :]
-                low = (back * gate[b, r, :]).astype(bf)
-                low_gate = (back * branch[b, r, :]).astype(bf)
+                low = (back * gate[b, r, :].astype(jnp.float32)).astype(bf)
+                low_gate = (back * branch[b, r, :].astype(jnp.float32)).astype(bf)
                 back_branch[r, :] = low
-                bm[r, 2 * HW :] = low_gate
+                bm[own, 2 * HW :] = low_gate
                 add_bias_grad(5 * b + 4, low)
                 add_bias_grad(5 * b + 2, low_gate)
             by_rows(_)
-            leave(per_block * b + 3).start()
+            send(per_block * b + 3)
             t0[...] = nn(back_branch[...], w_down[...])
 
             def _(r):
@@ -1092,15 +1104,15 @@
                 back_inner[r, :] = low
                 add_bias_grad(5 * b + 3, low)
             by_rows(_)
-            leave(per_block * b + 2).start()
+            send(per_block * b + 2)
             t0[...] = nt(back_inner[...], w_up[...])
 
             def _(r):
                 back = t0[r, :]
                 n = normed[b, r, :]
                 low_shift, low_scale = back.astype(bf), (back * n).astype(bf)
-                bm[r, :HW] = low_shift
-                bm[r, HW : 2 * HW] = low_scale
+                bm[own, :HW] = low_shift
+                bm[own, HW : 2 * HW] = low_scale
                 add_bias_grad(5 * b, low_shift)
                 add_bias_grad(5 * b + 1, low_scale)
                 up = back * scale1[b, r, :]
@@ -1108,37 +1120,55 @@
                     up - jnp.mean(up, -1, keepdims=True) - n * jnp.mean(up * n, -1, keepdims=True)
                 )
             by_rows(_)
-            leave(per_block * b).start()
-            back_silu[...] += nt(bm[...], w_mod[...])
+            send(per_block * b)
 
         def _(r):
-            value = conditioning[r, :]
-            s = sigmoid(value)
-            back = back_silu[r, :] * (s * (1.0 + value * (1.0 - s)))
-            low, low_stream = back.astype(bf), stream[r, :].astype(bf)
-            cond_sum[r, :] = cond_sum[r, :] + back
-            back_time[r, :] = low
+            low_stream = stream[r, :].astype(bf)
             back_low[r, :] = low_stream
-            add_bias_grad(11, low)
             add_bias_grad(14, low_stream)
         by_rows(_)
-        leave(base + 2).start()
-        leave(base + 7).start()
-        t0[...] = nn(back_time[...], time_two_t[...])
-
-        def _(r):
-            value = time_inner[r, :]
+        send(base + 7)
+
+    @pl.loop(0, COPIES // 2)
+    def _(pair):
+        for half in range(2):
+            one_copy(pair, half)
+        for b in range(HB):
+            for n in range(0, HW, 256):
+                back_silu[:, n : n + 256] += nt(left[per_block * b][...], weights[3 * b][n : n + 256, :])
+        for half in range(2):
+            @pl.when(pair > 0)
+            def _():
+                leave(base + 2, 2 * pair + half, half).wait()
+                leave(base + 3, 2 * pair + half, half).wait()
+
+        for first in range(0, 2 * tokens, 32):
+            own, sum_rows = slice(first, first + 32), slice(first % tokens, first % tokens + 32)
+            value = conditioning[own, :]
             s = sigmoid(value)
-            low = (t0[r, :] * (s * (1.0 + value * (1.0 - s)))).astype(bf)
-            back_time_inner[r, :] = low
+            back = back_silu[own, :] * (s * (1.0 + value * (1.0 - s)))
+            low = back.astype(bf)
+            cond_sum[sum_rows, :] = cond_sum[sum_rows, :] + back
+            back_time[own, :] = low
+            add_bias_grad(11, low)
+        for n in range(0, HW, 256):
+            back_silu[:, n : n + 256] = nn(back_time[...], time_two_t[:, n : n + 256])
+        for first in range(0, 2 * tokens, 32):
+            own = slice(first, first + 32)
+            value = time_inner[own, :]
+            s = sigmoid(value)
+            low = (back_silu[own, :] * (s * (1.0 + value * (1.0 - s)))).astype(bf)
+            back_time_inner[own, :] = low
             add_bias_grad(10, low)
-        by_rows(_)
-        leave(base + 3).start()
+        for half in range(2):
+            leave(base + 2, 2 * pair + half, half).start()
+            leave(base + 3, 2 * pair + half, half).start()
 
     back_cond_ref[...] = cond_sum[...].astype(bf)
     back_token_ref[...] = nn(back_cond_ref[...], cond_t[...]).astype(bf)
     for k in range(len(HEAD_LEFT)):
-        pltpu.make_async_copy(left[k], left_hbm[k].at[COPIES - 1], left_sem.at[k]).wait()
+        for half in (0, 1) if k in doubled else (1,):
+            leave(k, COPIES - 2 + half, half).wait()
 
 
 def head_pass(
@@ -1174,20 +1204,27 @@
             jax.ShapeDtypeStruct((5 * (HB + 1) + 1, HW), f32),
             jax.ShapeDtypeStruct((tokens, 128), f32),
         ],
-        in_specs=[vmem] * 7 + [hbm] * (HB + 7),
+        in_specs=[vmem] * 6 + [hbm] * (HB + 7),
         out_specs=[hbm] * len(HEAD_LEFT) + [vmem] * 5,
         scratch_shapes=[pltpu.VMEM(shape, bf) for shape in HEAD_WEIGHTS]
-        + [pltpu.VMEM((tokens, k * HW), bf) for k in HEAD_LEFT]
-        + [units()] * 9
-        + [units(HB)] * 5
+        + [
+            pltpu.VMEM((2 * tokens if k in (0, 5, 5 * HB + 2, 5 * HB + 3) else tokens, units_of * HW), bf)
+            for k, units_of in enumerate(HEAD_LEFT)
+        ]
+        + [pltpu.VMEM((2 * tokens, HW), f32)] * 2
+        + [units()] * 3
+        + [pltpu.VMEM((2 * tokens, HW), f32)]
+        + [units()] * 2
+        + [units(HB)] * 3
+        + [pltpu.VMEM((HB, tokens, HW), bf)] * 2
         + [
             pltpu.VMEM((HB + 1, tokens, 128), f32),
-            pltpu.SemaphoreType.DMA((len(HEAD_WEIGHTS),)), pltpu.SemaphoreType.DMA((len(HEAD_LEFT),)),
+            pltpu.SemaphoreType.DMA((len(HEAD_WEIGHTS),)), pltpu.SemaphoreType.DMA((len(HEAD_LEFT), 2)),
         ],
-        compiler_params=pltpu.CompilerParams(vmem_limit_bytes=60 * 2**20),
+        compiler_params=pltpu.CompilerParams(vmem_limit_bytes=63_400_000),
     )(
-        time_embed, noisy, target, by_copy * (2.0 / (CH * weight_total)), by_copy * (1.0 / CH),
-        jnp.pad(biases.reshape(5 * (HB + 1), HW), ((0, 1), (0, 0))), cond_rows,
+        time_embed, noisy, target, by_copy * (1.0 / CH),
+        jnp.concatenate([biases.reshape(5 * (HB + 1), HW), jnp.full((1, HW), 2.0 / weight_total)], 0), cond_rows,
         *blocks, *edges,
     )
     left = [a.reshape(COPIES * tokens, -1) for a in outs[: len(HEAD_LEFT)]]

time: 775 us -> 768 us (level)
  no operation moved by 1% of the time
where the time goes in v5:
time: 768 us; the launch traced here: 759 us
  Pallas kernels  647 us (84%)
  other arithmetic  36.1 us (5%)
  between operations  23.5 us (3%)
  local copies, waits for them, and re-layouts  22.1 us (3%)
  waiting for transfers between devices  12 us (2%)
  matrix products  10.6 us (1%)
    pallas_call x2, Pallas kernels, layer_backward(): pl.pallas_call(functools.partial(backward_kernel, layer, static), out_sha...  290 us
    pallas_call x1, Pallas kernels, gather_rows(): pl.pallas_call(functools.partial(gather_kernel, nz, chunks, len(sources))...  243 us
    pallas_call x1, Pallas kernels, head_pass(): pl.pallas_call(functools.partial(head_kernel, tokens), out_shape=[jax.Sha...  74.7 us
    pallas_call x1, Pallas kernels, trunk_forward(): pl.pallas_call(forward_kernel, out_shape=[jax.ShapeDtypeStruct(s, dtype)...  30.4 us
  transfers between devices with their start and end apart: 4, of which 2 were waited for; matrix products, arithmetic and copies ran while one was open for 4% of the time, Pallas kernels for 36%

profile of v5, /device:TPU:0, one launch (start us, length us, event | category | flops | bytes accessed | tf_op | source)
XLA Modules:
  0.0 758.7 jit_solution(14913454125571118029)
XLA Ops:
  7.2 1.4 convert_element_type.155
  18.3 2.0 pad_maximum_fusion.3
  21.0 243.3 %shard_map.391 = (bf16[2,2,2,4,24,768]{5,4,3,2,1,0:T(8,128)(2,1)}, bf16[2,2,2,4,24,2304]{5,4,3,2,1,0:T(8,128)(2,1)}, bf16[2,2,2,4,24,768]{5,4,3,2,1,0:T(8,128)(2...) custom-call(bf16[2,24,9216]{2,1,0:T(8,128)(2,1)} %convert_element_ty, ...), custom_call_target="tpu_custom_call" | custom-call | tf_op jit(solution)/shard_map/pallas_call | solution.py:387
  269.2 30.4 %shard_map.392 = (bf16[2,320,768]{2,1,0:T(8,128)(2,1)}, bf16[2,320,2304]{2,1,0:T(8,128)(2,1)}, bf16[2,320,768]{2,1,0:T(8,128)(2,1)}, bf16[2,320,768]{2,1,0:T(8,1...) custom-call(bf16[768,768]{1,0:T(8,128)(2,1)} %bitcast.203, ...), custom_call_target="tpu_custom_call" | custom-call | tf_op jit(solution)/shard_map/pallas_call | solution.py:619
  300.5 2.1 fusion.6
  302.6 2.9 all-to-all-start
  309.6 1.7 fusion.16
  312.9 5.7 all-to-all-done
  322.4 74.7 %shard_map.393 = (bf16[4,192,3072]{2,1,0:T(8,128)(2,1)}, bf16[4,192,1024]{2,1,0:T(8,128)(2,1)}, bf16[4,192,1024]{2,1,0:T(8,128)(2,1)}, bf16[4,192,1024]{2,1,0:T(...) custom-call(bf16[4,192,256]{2,1,0:T(8,128)(2,1)} %pad_maximum_fusion, ...), custom_call_target="tpu_custom_call" | custom-call | tf_op jit(solution)/shard_map/pallas_call | solution.py:1197
  397.1 1.7 convolution_convert_fusion
  403.4 4.0 all-to-all-start.1
  408.0 2.1 convolution_bitcast_fusion.1
  411.6 2.0 pad_maximum_fusion.refs_33_
  413.6 5.5 all-to-all-done.1
  421.2 145.0 %shard_map.394 = (bf16[320,2304]{1,0:T(8,128)(2,1)}, bf16[320,768]{1,0:T(8,128)(2,1)}, bf16[320,3072]{1,0:T(8,128)(2,1)}, bf16[320,768]{1,0:T(8,128)(2,1)}, f32[...) custom-call(bf16[768,2304]{1,0:T(8,128)(2,1)} %bitcast.164, ...), custom_call_target="tpu_custom_call" | custom-call | tf_op jit(solution)/shard_map/pallas_call | solution.py:850
  566.2 1.8 copy.114
  570.9 144.8 %shard_map.395 = (bf16[320,2304]{1,0:T(8,128)(2,1)}, bf16[320,768]{1,0:T(8,128)(2,1)}, bf16[320,3072]{1,0:T(8,128)(2,1)}, bf16[320,768]{1,0:T(8,128)(2,1)}, f32[...) custom-call(bf16[768,2304]{1,0:T(8,128)(2,1)} %bitcast.162, ...), custom_call_target="tpu_custom_call" | custom-call | tf_op jit(solution)/shard_map/pallas_call | solution.py:850
  715.7 2.6 fusion.2
  720.3 9.3 %shard_map.396 = f32[32,8,128]{2,1,0:T(8,128)S(1)} custom-call(f32[8,128]{1,0:T(8,128)S(1)} %broadcast_in_dim.47.in_ref), custom_call_target="tpu_custom_call" | custom-call | tf_op jit(solution)/shard_map/pallas_call | solution.py:439
  731.2 1.6 copy.113
  735.5 1.7 multiply_subtract_fusion.3
  738.6 3.0 multiply_subtract_fusion.2
  742.9 2.7 multiply_subtract_fusion.1
  747.1 3.4 multiply_subtract_fusion
  (177 shorter events, 39.7 us)
Async XLA Ops:
  7.2 314.3 %all-gather.5.cloned.1.call-start = ((), (), s32[]{:S(2)}) async-start(), calls=%async_computation.2 | async-start | bytes 10813440 | tf_op jit(solution)/shard_map/all_gather | solution.py:1346
  8.7 7.4 copy-start.22
  8.7 7.5 copy-start.18
  8.7 7.7 %copy-start.1 = (f32[2,24,9216]{2,1,0:T(8,128)S(1)}, f32[2,24,9216]{2,1,0:T(8,128)}, u32[]{:S(2)}) copy-start(f32[2,24,9216]{2,1,0:T(8,128)} %param.30) | copy-start | bytes 5308420
  9.6 311.9 %all-gather.7.cloned.1.call-start = ((), (), s32[]{:S(2)}) async-start(), calls=%async_computation.3 | async-start | bytes 10813440 | tf_op jit(solution)/shard_map/all_gather | solution.py:1346
  10.6 9.7 %copy-start.13 = (f32[656,24]{0,1:T(8,128)S(1)}, f32[656,24]{0,1:T(8,128)}, u32[]{:S(2)}) copy-start(f32[656,24]{0,1:T(8,128)} %param.32) | copy-start | bytes 188932
  16.4 250.6 %copy-start.26 = (s32[1,256]{1,0:T(1,128)S(1)}, s32[1,256]{1,0:T(1,128)}, u32[]{:S(2)}) copy-start(s32[1,256]{1,0:T(1,128)} %param.25) | copy-start | bytes 3076
  16.4 251.4 %copy-start.21 = (bf16[1,256,16]{1,2,0:T(8,128)(2,1)S(1)}, bf16[1,256,16]{1,2,0:T(8,128)(2,1)}, u32[]{:S(2)}) copy-start(bf16[1,256,16]{1,2,0:T(8,128)(2,1)} %param.24) | copy-start | bytes 24580
  299.6 5.9 copy-start.16
  299.6 6.1 copy-start.6
  302.6 16.0 %all-to-all-start = ((bf16[32,8,896]{2,1,0:T(8,128)(2,1)}), bf16[32,8,896]{2,1,0:T(8,128)(2,1)S(1)}, u32[]{:S(2)}, u32[]{:S(2)}) async-start(bf16[32,8,896]{2,1,0:T(8,128)(2,1)} %fusion.6), calls=%async_computation | async-start | bytes 917504 | tf_op jit(solution)/shard_map/all_to_all | solution.py:1381
  305.8 3.7 copy-start.17
  306.2 6.0 copy-start.30
  401.6 5.7 copy-start.15
  401.6 6.3 copy-start.33
  403.4 15.8 %all-to-all-start.1 = ((bf16[32,8,768]{2,1,0:T(8,128)(2,1)}), bf16[32,8,768]{2,1,0:T(8,128)(2,1)S(1)}, u32[]{:S(2)}, u32[]{:S(2)}) async-start(bf16[32,8,768]{2,1,0:T(8,128)(2,1)} %fusion.7), calls=%async_computation.1 | async-start | bytes 786432 | tf_op jit(solution)/shard_map/all_to_all | solution.py:1427
  737.1 5.7 copy-start.11
  738.5 3.7 copy-start.23
  738.5 3.7 copy-start.28
  738.6 4.3 copy-start.3
  738.6 4.3 copy-start.5
  738.6 4.2 copy-start.10
  742.9 3.7 copy-start.8
  742.9 4.2 copy-start.9
  (14 other events, 36.1 us)
Sparse Core Ops, SparseCore 0:
  11.4 138.8 all-gather.4
  153.7 116.9 all-gather.6
